TPU v7x, 512 devices: a whole 4x8x8 slice. The times are simulated.
512 devices in a mesh: space: 64 (over x, z, core), chan: 8 (over y).
Axes of the slice: x: 4, y: 8, z: 8, core: 2. Of those that a mesh axis runs over, the one named last changes fastest.
Arguments:
- features: bfloat16 [256, 128, 512], P(None, 'space'), may hold values from -12 to 17
- first_weight: bfloat16 [27, 256, 256], P(None, 'chan'), may hold values from -0.078125 to 0.078125
- first_gain: float32 [256], P('chan'), may hold values from 0.5 to 1.5
- first_bias: float32 [256], P('chan'), may hold values from -3 to 3
- down_weight: bfloat16 [27, 320, 256], P(None, None, 'chan'), may hold values from -0.078125 to 0.078125
- down_gain: float32 [320], P('chan'), may hold values from 0.5 to 1.5
- down_bias: float32 [320], P('chan'), may hold values from -3 to 3
- third_weight: bfloat16 [27, 320, 320], P(None, 'chan'), may hold values from -0.0625 to 0.0625
- third_gain: float32 [320], P('chan'), may hold values from 0.5 to 1.5
- third_bias: float32 [320], P('chan'), may hold values from -3 to 3
Outputs:
- bottleneck: bfloat16 [320, 64, 128], P('chan', 'space')
All inputs are finite; a program needn't handle non-finite values.
Results may differ from a plain program's by a relative error of at most 0.027.
Values may be sent and summed in bfloat16 or wider, within the bound.
No kernel may reach another device: no remote copies, remote signals or barrier semaphores. Data moves between devices by JAX's collectives and lax.ppermute only.
A program may use at most 64 MiB of HBM per device.

v0:
```python
import jax
import jax.numpy as jnp
from jax import lax
from jax.sharding import PartitionSpec as P

COLS = 32


EPSILON = 1e-05
SLOPE = 0.01


def extended(block, sides, width):
    for axis, dim in sides:
        count = lax.axis_size(axis)
        forward = [(i, i + 1) for i in range(count - 1)]
        backward = [(target, source) for source, target in forward]
        low = lax.ppermute(
            lax.slice_in_dim(block, block.shape[dim] - width, None, axis=dim), axis, forward
        )
        high = lax.ppermute(lax.slice_in_dim(block, 0, width, axis=dim), axis, backward)
        block = jnp.concatenate([low, block, high], axis=dim)
    return block


def from_behind(value, axis, by):
    count = lax.axis_size(axis)
    pairs = [(i, i + by) for i in range(count) if 0 <= i + by < count]
    return lax.ppermute(value, axis, pairs)


def shifted(volume, row_step, col_step, col_count):
    cell_count = volume.shape[2]
    margin = col_count + 1
    padded = jnp.pad(volume, ((0, 0), (0, 0), (margin, margin)))
    offset = margin + row_step * col_count + col_step
    moved_cells = lax.slice_in_dim(padded, offset, offset + cell_count, axis=2)
    column = jnp.arange(cell_count, dtype=jnp.int32) % col_count + col_step
    inside = (column >= 0) & (column < col_count)
    return jnp.where(inside, moved_cells, jnp.zeros((), moved_cells.dtype))


def convolve_same(padded, weight, col_count):
    depth_count = padded.shape[1] - 2
    summed = jnp.zeros((weight.shape[1], depth_count, padded.shape[2]), jnp.float32)
    for row_tap in range(3):
        for col_tap in range(3):
            moved_cells = shifted(padded, row_tap - 1, col_tap - 1, col_count)
            for depth_tap in range(3):
                kernel = weight[depth_tap * 9 + row_tap * 3 + col_tap]
                summed = summed + jnp.einsum(
                    "oi,izp->ozp",
                    kernel,
                    moved_cells[:, depth_tap : depth_tap + depth_count],
                    preferred_element_type=jnp.float32,
                )
    return summed


def phase_split(volume, col_count):
    chan_count, depth_count, cell_count = volume.shape
    lattice = volume.reshape(
        chan_count, depth_count, cell_count // (2 * col_count), 2, col_count // 2, 2
    )
    return [
        [
            lattice[:, :, :, row_phase, :, col_phase].reshape(
                chan_count, depth_count, cell_count // 4
            )
            for col_phase in range(2)
        ]
        for row_phase in range(2)
    ]


def down_taps(layers, col_count):
    taps = []
    for depth_tap in range(3):
        phases = phase_split(layers[depth_tap], col_count)
        for row_tap in range(3):
            for col_tap in range(3):
                source = phases[(row_tap + 1) % 2][(col_tap + 1) % 2]
                taps.append(
                    shifted(
                        source, -1 if row_tap == 0 else 0, -1 if col_tap == 0 else 0, col_count // 2
                    )
                )
    return taps


def normalize(summed, gain, bias, spaces):
    cell_total = summed.shape[1] * summed.shape[2] * spaces
    average = lax.psum(jnp.sum(summed, axis=(1, 2)), "space") / cell_total
    centred = summed - average[:, None, None]
    spread = lax.psum(jnp.sum(centred * centred, axis=(1, 2)), "space") / cell_total
    scaled = (
        gain[:, None, None] * centred * lax.rsqrt(spread[:, None, None] + EPSILON)
        + bias[:, None, None]
    )
    return jnp.where(scaled >= 0, scaled, SLOPE * scaled).astype(jnp.bfloat16)


def local(
    features,
    first_weight,
    first_gain,
    first_bias,
    down_weight,
    down_gain,
    down_bias,
    third_weight,
    third_gain,
    third_bias,
):
    spaces = lax.axis_size("space")
    framed = extended(features, (("space", 1),), 1)
    first = convolve_same(framed, first_weight, COLS)
    level = normalize(first, first_gain, first_bias, spaces)
    even_slices = level[:, 0::2]
    odd_slices = level[:, 1::2]
    blank = jnp.zeros_like(level[:, :1])
    layers = (
        jnp.concatenate([blank, odd_slices], axis=1),
        jnp.concatenate([even_slices, blank], axis=1),
        jnp.concatenate([odd_slices, blank], axis=1),
    )
    taps = down_taps(layers, COLS)
    summed = jnp.zeros(
        (down_weight.shape[1] // lax.axis_size("chan") * lax.axis_size("chan"),)
        + taps[0].shape[1:],
        jnp.float32,
    )
    for tap_number in range(27):
        summed = summed + jnp.einsum(
            "oi,izp->ozp",
            down_weight[tap_number],
            taps[tap_number],
            preferred_element_type=jnp.float32,
        )
    reduced = lax.psum_scatter(
        summed.astype(jnp.bfloat16), "chan", scatter_dimension=0, tiled=True
    ).astype(jnp.float32)
    carried = from_behind(reduced[:, -1:], "space", 1)
    reduced = jnp.concatenate([reduced[:, :1] + carried, reduced[:, 1:-1]], axis=1)
    bottom = normalize(reduced, down_gain, down_bias, spaces)
    gathered = lax.all_gather(bottom, "chan", axis=0, tiled=True)
    padded = extended(gathered, (("space", 1),), 1)
    third = convolve_same(padded, third_weight, COLS // 2)
    return normalize(third, third_gain, third_bias, spaces)


def solution(mesh):
    return jax.shard_map(
        local,
        mesh=mesh,
        in_specs=(
            P(None, "space", None),
            P(None, "chan", None),
            P("chan"),
            P("chan"),
            P(None, None, "chan"),
            P("chan"),
            P("chan"),
            P(None, "chan", None),
            P("chan"),
            P("chan"),
        ),
        out_specs=P("chan", "space", None),
        check_vma=False,
    )
```

profile of v0, /device:TPU:1, one launch (start us, length us, event | category | flops | bytes accessed | tf_op | source)
XLA Modules:
  0.0 876.3 jit_solution(9091579398320351419)
XLA Ops:
  6.5 2.1 fusion.344
  8.7 5.5 collective-permute-start
  14.3 4.7 collective-permute-start.1
  19.2 2.8 collective-permute-done.1
  22.0 3.0 fusion.45
  26.1 0.2 convolution_add_fusion.26
  26.3 0.2 convolution_add_fusion.25
  26.9 0.2 convolution_add_fusion.22
  27.1 0.2 convolution_add_fusion.21
  27.3 0.2 convolution_add_fusion.20
  28.1 0.2 fusion.26
  28.7 0.2 fusion.21
  28.9 0.2 fusion.20
  29.1 0.2 fusion.19
  29.7 0.2 fusion.16
  30.3 0.3 fusion.346
  30.6 127.6 %psum.42 = f32[32]{0:T(128)S(1)} all-reduce(f32[32]{0:T(128)S(1)} %get-tuple-element.69), channel_id=1, replica_groups=mesh['space'=64,'chan'=8] {'space'}, use_global_device_ids=true, to_apply=%region_1.2 | all-reduce | flops 32 | bytes 256 | tf_op jit(solution)/shard_map/psum | solution.py:93
  158.4 125.3 %psum.43 = f32[32]{0:T(128)S(1)} all-reduce(f32[32]{0:T(128)S(1)} %multiply_reduce_fusion), channel_id=1, replica_groups=mesh['space'=64,'chan'=8] {'space'}, use_global_device_ids=true, to_apply=%region_3.4 | all-reduce | flops 32 | bytes 256 | tf_op jit(solution)/shard_map/psum | solution.py:95
  284.1 1.7 broadcast_select_fusion.1
  285.8 0.3 fusion.100
  286.1 0.3 convolution_add_fusion.15
  286.4 0.3 convolution_add_fusion.14
  286.7 0.3 convolution_add_fusion.13
  287.0 0.3 convolution_add_fusion.12
  287.2 0.3 convolution_add_fusion.11
  287.5 0.3 convolution_add_fusion.10
  288.0 0.8 broadcast_select_fusion.5
  288.8 0.3 convolution_add_fusion.9
  289.1 0.3 convolution_add_fusion.8
  289.3 0.3 convolution_add_fusion.7
  289.6 0.3 convolution_add_fusion.6
  289.9 0.3 convolution_add_fusion.5
  290.3 0.3 convolution_add_fusion.4
  290.5 0.3 convolution_add_fusion.3
  290.8 0.3 convolution_add_fusion.2
  291.1 0.3 convolution_add_fusion.1
  291.4 0.3 fusion.10
  291.7 0.3 fusion.9
  291.9 0.3 fusion.8
  292.2 0.3 fusion.7
  292.5 0.3 fusion.6
  292.8 0.3 fusion.5
  293.1 0.3 fusion.4
  293.4 0.3 fusion.3
  293.6 0.3 fusion.2
  294.0 0.3 fusion.1
  294.2 0.3 fusion.12
  294.5 0.7 copy.139
  295.2 27.4 %reduce-scatter.4.cloned.1.call-done = bf16[40,256]{1,0:T(8,128)(2,1)} async-done(((bf16[320,256]{1,0:T(8,128)(2,1)}), bf16[40,256]{1,0:T(8,128)(2,1)}) %reduce-scatter.4.cloned.1.call-update) | async-done | bytes 20496
  322.6 0.7 bitcast_convert_fusion
  323.3 9.2 %collective-permute-start.2 = (f32[40,1,128]{2,0,1:T(8,128)S(1)}, f32[40,1,128]{2,0,1:T(8,128)S(1)}, u32[]{:S(2)}, u32[]{:S(2)}) collective-permute-start(f32[40,1,128]{2,0,1:T(8,128)S(1)} %slice.793), channel_id=1, source_target_pairs={{0,8},{8,16},{16,24},{24,32},{32,40},{40,48},{48,56},{56,64},{64,7... | collective-permute-start | bytes 61448 | tf_op jit(solution)/shard_map/ppermute | solution.py:29
  332.6 0.9 collective-permute-done.2
  333.6 125.6 %psum.44 = f32[40]{0:T(128)S(1)} all-reduce(f32[40]{0:T(128)S(1)} %fusion.342), channel_id=1, replica_groups=mesh['space'=64,'chan'=8] {'space'}, use_global_device_ids=true, to_apply=%region_6.7 | all-reduce | flops 40 | bytes 320 | tf_op jit(solution)/shard_map/psum | solution.py:93
  459.3 126.6 %psum.45 = f32[40]{0:T(128)S(1)} all-reduce(f32[40]{0:T(128)S(1)} %multiply_reduce_fusion.2), channel_id=1, replica_groups=mesh['space'=64,'chan'=8] {'space'}, use_global_device_ids=true, to_apply=%region_8.9 | all-reduce | flops 40 | bytes 320 | tf_op jit(solution)/shard_map/psum | solution.py:95
  586.0 18.5 %all_gather.3 = bf16[320,1,128]{2,0,1:T(8,128)(2,1)S(1)} all-gather(bf16[40,1,128]{2,0,1:T(8,128)(2,1)S(1)} %fusion.256), channel_id=1, replica_groups=mesh['space'=64,'chan'=8] {'chan'}, dimensions={0}, use_global_device_ids=true | all-gather | bytes 92160 | tf_op jit(solution)/shard_map/all_gather | solution.py:146
  604.5 4.7 collective-permute-start.3
  609.2 5.2 collective-permute-start.4
  614.5 0.9 collective-permute-done.4
  615.4 0.7 fusion.84
  616.1 0.4 copy-done.1
  620.4 0.2 fusion.347
  620.6 123.8 %psum.46 = f32[40]{0:T(128)S(1)} all-reduce(f32[40]{0:T(128)S(1)} %get-tuple-element.71), channel_id=1, replica_groups=mesh['space'=64,'chan'=8] {'space'}, use_global_device_ids=true, to_apply=%region_10.11 | all-reduce | flops 40 | bytes 320 | tf_op jit(solution)/shard_map/psum | solution.py:93
  744.6 124.2 %psum.47 = f32[40]{0:T(128)S(1)} all-reduce(f32[40]{0:T(128)S(1)} %multiply_reduce_fusion.1), channel_id=1, replica_groups=mesh['space'=64,'chan'=8] {'space'}, use_global_device_ids=true, to_apply=%region_12.13 | all-reduce | flops 40 | bytes 320 | tf_op jit(solution)/shard_map/psum | solution.py:95
  868.8 0.7 fusion.312
  (118 shorter events, 8.6 us)
Async XLA Ops:
  6.5 316.0 %reduce-scatter.4.cloned.1.call-start = ((), (), s32[]{:S(2)}) async-start(), calls=%async_computation.1 | async-start | bytes 184320
  8.7 10.4 %copy-start = (bf16[256,2,512]{2,1,0:T(2,128)(2,1)S(1)}, bf16[256,2,512]{2,1,0:T(2,128)(2,1)}, u32[]{:S(2)}) copy-start(bf16[256,2,512]{2,1,0:T(2,128)(2,1)} %param.10) | copy-start | bytes 1572868
  8.7 10.3 %collective-permute-start = (bf16[256,1,512]{2,0,1:T(8,128)(2,1)S(1)}, bf16[256,1,512]{2,0,1:T(8,128)(2,1)S(1)}, u32[]{:S(2)}, u32[]{:S(2)}) collective-permute-start(bf16[256,1,512]{2,0,1:T(8,128)(2,1)S(1)} %copy.137), channel_id=1, source_target_pairs={{0,8},{8,16},{16,24},{24,32},{32,40},{40,48},{48,56},{56,64},{64,7... | collective-permute-start | bytes 786440 | tf_op jit(solution)/shard_map/ppermute | solution.py:18
  14.3 7.7 collective-permute-start.1
  22.0 3.1 copy-start.3
  30.1 253.6 %copy-start.4 = (f32[32]{0:T(128)S(1)}, f32[32]{0:T(128)}, u32[]{:S(2)}) copy-start(f32[32]{0:T(128)} %param.13) | copy-start | bytes 388
  30.1 253.6 %copy-start.5 = (f32[32]{0:T(128)S(1)}, f32[32]{0:T(128)}, u32[]{:S(2)}) copy-start(f32[32]{0:T(128)} %param.12) | copy-start | bytes 388
  30.1 253.6 %copy-start.8 = (pred[2]{0:T(512)(128)(4,1)S(1)}, pred[2]{0:T(512)(128)(4,1)}, u32[]{:S(2)}) copy-start(pred[2]{0:T(512)(128)(4,1)} %constant.196.clone.1) | copy-start | bytes 10
  284.0 1.7 copy-start.2
  294.0 292.0 %copy-start.9 = (f32[40]{0:T(128)S(1)}, f32[40]{0:T(128)}, u32[]{:S(2)}) copy-start(f32[40]{0:T(128)} %param.16) | copy-start | bytes 484
  294.0 292.0 %copy-start.10 = (f32[40]{0:T(128)S(1)}, f32[40]{0:T(128)}, u32[]{:S(2)}) copy-start(f32[40]{0:T(128)} %param.15) | copy-start | bytes 484
  323.3 10.1 %collective-permute-start.2 = (f32[40,1,128]{2,0,1:T(8,128)S(1)}, f32[40,1,128]{2,0,1:T(8,128)S(1)}, u32[]{:S(2)}, u32[]{:S(2)}) collective-permute-start(f32[40,1,128]{2,0,1:T(8,128)S(1)} %slice.793), channel_id=1, source_target_pairs={{0,8},{8,16},{16,24},{24,32},{32,40},{40,48},{48,56},{56,64},{64,7... | collective-permute-start | bytes 61448 | tf_op jit(solution)/shard_map/ppermute | solution.py:29
  604.5 10.0 %collective-permute-start.3 = (bf16[320,1,128]{2,0,1:T(8,128)(2,1)S(1)}, bf16[320,1,128]{2,0,1:T(8,128)(2,1)S(1)}, u32[]{:S(2)}, u32[]{:S(2)}) collective-permute-start(bf16[320,1,128]{2,0,1:T(8,128)(2,1)S(1)} %all_gather.3), channel_id=1, source_target_pairs={{0,8},{8,16},{16,24},{24,32},{32,40},{40,48},{48,56},{56,64},{64,7... | collective-permute-start | bytes 245768 | tf_op jit(solution)/shard_map/ppermute | solution.py:18
  609.2 6.2 collective-permute-start.4
  615.4 1.2 copy-start.1
  618.6 250.2 %copy-start.6 = (f32[40]{0:T(128)S(1)}, f32[40]{0:T(128)}, u32[]{:S(2)}) copy-start(f32[40]{0:T(128)} %param.19) | copy-start | bytes 484
  618.6 250.2 %copy-start.7 = (f32[40]{0:T(128)S(1)}, f32[40]{0:T(128)}, u32[]{:S(2)}) copy-start(f32[40]{0:T(128)} %param.18) | copy-start | bytes 484
Sparse Core Ops, SparseCore 0:
  295.3 27.2 reduce-scatter.3
where the time goes:
time: 877 us; the launch traced here: 876 us
  blocking collectives  772 us (88%)
  waiting for transfers between devices  31.9 us (4%)
  starting transfers between devices  29.4 us (3%)
  matrix products  16.6 us (2%)
  between operations  14.2 us (2%)
    psum x3, blocking collectives, normalize(): average = lax.psum(jnp.sum(summed, axis=(1, 2)), 'space') / cell_total  377 us
    psum x3, blocking collectives, normalize(): lax.psum(jnp.sum(centred * centred, axis=(1, 2)), 'space') / cell_total  376 us
    unnamed x2, waiting for transfers between devices  27.4 us
    all_gather x1, blocking collectives, local(): gathered = lax.all_gather(bottom, 'chan', axis=0, tiled=True)  18.5 us
  transfers between devices with their start and end apart: 6, of which 4 were waited for; matrix products, arithmetic and copies ran while one was open for 0% of the time, Pallas kernels for 0%

commit v1 on v0

--- a/solution.py
+++ b/solution.py
@@ -88,13 +88,28 @@
     return taps
 
 
-def normalize(summed, gain, bias, spaces):
-    cell_total = summed.shape[1] * summed.shape[2] * spaces
-    average = lax.psum(jnp.sum(summed, axis=(1, 2)), "space") / cell_total
+def everyone(row, axis):
+    count = lax.axis_size(axis)
+    copies = jnp.broadcast_to(row[None], (count,) + row.shape)
+    return lax.all_to_all(copies, axis, 0, 0, tiled=True)
+
+
+def normalize(summed, gain, bias):
+    chan_count = summed.shape[0]
+    average = jnp.mean(summed, axis=(1, 2))
     centred = summed - average[:, None, None]
-    spread = lax.psum(jnp.sum(centred * centred, axis=(1, 2)), "space") / cell_total
+    spread = jnp.mean(centred * centred, axis=(1, 2))
+    row = jnp.pad(jnp.concatenate([average, spread])[None], ((0, 0), (0, 128 - 2 * chan_count)))
+    rows = everyone(row, "space")[:, 0]
+    averages = rows[:, :chan_count]
+    average = jnp.mean(averages, axis=0)
+    spread = jnp.mean(rows[:, chan_count : 2 * chan_count], axis=0) + jnp.mean(
+        (averages - average[None]) ** 2, axis=0
+    )
     scaled = (
-        gain[:, None, None] * centred * lax.rsqrt(spread[:, None, None] + EPSILON)
+        gain[:, None, None]
+        * (summed - average[:, None, None])
+        * lax.rsqrt(spread[:, None, None] + EPSILON)
         + bias[:, None, None]
     )
     return jnp.where(scaled >= 0, scaled, SLOPE * scaled).astype(jnp.bfloat16)
@@ -112,10 +127,9 @@
     third_gain,
     third_bias,
 ):
-    spaces = lax.axis_size("space")
     framed = extended(features, (("space", 1),), 1)
     first = convolve_same(framed, first_weight, COLS)
-    level = normalize(first, first_gain, first_bias, spaces)
+    level = normalize(first, first_gain, first_bias)
     even_slices = level[:, 0::2]
     odd_slices = level[:, 1::2]
     blank = jnp.zeros_like(level[:, :1])
@@ -137,16 +151,20 @@
             taps[tap_number],
             preferred_element_type=jnp.float32,
         )
-    reduced = lax.psum_scatter(
-        summed.astype(jnp.bfloat16), "chan", scatter_dimension=0, tiled=True
-    ).astype(jnp.float32)
+    chans = lax.axis_size("chan")
+    parts = summed.astype(jnp.bfloat16).reshape(
+        (chans, summed.shape[0] // chans) + summed.shape[1:]
+    )
+    reduced = jnp.sum(
+        lax.all_to_all(parts, "chan", 0, 0, tiled=True).astype(jnp.float32), axis=0
+    )
     carried = from_behind(reduced[:, -1:], "space", 1)
     reduced = jnp.concatenate([reduced[:, :1] + carried, reduced[:, 1:-1]], axis=1)
-    bottom = normalize(reduced, down_gain, down_bias, spaces)
-    gathered = lax.all_gather(bottom, "chan", axis=0, tiled=True)
+    bottom = normalize(reduced, down_gain, down_bias)
+    gathered = everyone(bottom, "chan").reshape((-1,) + bottom.shape[1:])
     padded = extended(gathered, (("space", 1),), 1)
     third = convolve_same(padded, third_weight, COLS // 2)
-    return normalize(third, third_gain, third_bias, spaces)
+    return normalize(third, third_gain, third_bias)
 
 
 def solution(mesh):

time: 877 us -> 140 us (0.16)
  blocking collectives: 772 us -> 58.2 us
  waiting for transfers between devices: 31.9 us -> 16.8 us
  between operations: 14.2 us -> 1.01 us
    psum x6 -> x0, blocking collectives: 753 us -> none  [the longest x3 377 us: normalize(): average = lax.psum(jnp.sum(summed, axis=(1, 2)), 'space') / cell_total]
    all_to_all x0 -> x4, blocking collectives: none -> 58.2 us  [the longest x3 43.4 us: everyone(): return lax.all_to_all(copies, axis, 0, 0, tiled=True)]
    unnamed x2 -> x0, waiting for transfers between devices: 27.4 us -> none
    all_gather x1 -> x0, blocking collectives: 18.5 us -> none  [local(): gathered = lax.all_gather(bottom, 'chan', axis=0, tiled=True)]
    all_to_all x0 -> x1, starting transfers between devices: none -> 12.9 us  [everyone(): return lax.all_to_all(copies, axis, 0, 0, tiled=True)]
    all_to_all x0 -> x1, waiting for transfers between devices: none -> 9.27 us  [everyone(): return lax.all_to_all(copies, axis, 0, 0, tiled=True)]
where the time goes in v1:
time: 140 us
  blocking collectives  58.2 us (42%)
  starting transfers between devices  33.7 us (24%)
  waiting for transfers between devices  16.8 us (12%)
  matrix products  16.6 us (12%)
  other arithmetic  9.02 us (6%)
  local copies, waits for them, and re-layouts  4.55 us (3%)
    all_to_all x3, blocking collectives, everyone(): return lax.all_to_all(copies, axis, 0, 0, tiled=True)  43.4 us
    all_to_all x1, blocking collectives, local(): lax.all_to_all(parts, 'chan', 0, 0, tiled=True).astype(jnp.float32)  14.8 us
    all_to_all x1, starting transfers between devices, everyone(): return lax.all_to_all(copies, axis, 0, 0, tiled=True)  12.9 us
    ppermute x2, starting transfers between devices, extended(): lax.ppermute(lax.slice_in_dim(block, block.shape[dim] - width, None, axis...  9.45 us
    dot_general x54, matrix products, convolve_same(): jnp.einsum('oi,izp->ozp', kernel, moved_cells[:, depth_tap:depth_tap + de...  9.28 us
    all_to_all x1, waiting for transfers between devices, everyone(): return lax.all_to_all(copies, axis, 0, 0, tiled=True)  9.27 us
    dot_general x27, matrix products, local(): jnp.einsum('oi,izp->ozp', down_weight[tap_number], taps[tap_number], pref...  7.28 us
    ppermute x2, waiting for transfers between devices, extended(): lax.ppermute(lax.slice_in_dim(block, 0, width, axis=dim), axis, backward)  6.63 us
  transfers between devices with their start and end apart: 6, of which 4 were waited for; matrix products, arithmetic and copies ran while one was open for 0% of the time, Pallas kernels for 0%

profile of v1, /device:TPU:1, one launch (start us, length us, event | category | flops | bytes accessed | tf_op | source)
XLA Modules:
  0.0 139.8 jit_solution(5146193608653081480)
XLA Ops:
  0.0 2.2 %fusion.344 = (bf16[256,1,512]{2,1,0:T(2,128)(2,1)S(1)}, bf16[256,1,512]{2,1,0:T(2,128)(2,1)S(1)}) fusion(bf16[256,2,512]{2,1,0:T(2,128)(2,1)} %param.10), kind=kLoop, calls=%fused_computation.525 | loop fusion | bytes 1048576 | tf_op jit(solution)/shard_map/slice | solution.py:21
  2.3 5.5 %collective-permute-start = (bf16[256,1,512]{2,0,1:T(8,128)(2,1)S(1)}, bf16[256,1,512]{2,0,1:T(8,128)(2,1)S(1)}, u32[]{:S(2)}, u32[]{:S(2)}) collective-permute-start(bf16[256,1,512]{2,0,1:T(8,128)(2,1)S(1)} %copy.246), channel_id=1, source_target_pairs={{0,8},{8,16},{16,24},{24,32},{32,40},{40,48},{48,56},{56,64},{64,7... | collective-permute-start | bytes 786440 | tf_op jit(solution)/shard_map/ppermute | solution.py:18
  7.9 4.7 %collective-permute-start.1 = (bf16[256,1,512]{2,0,1:T(8,128)(2,1)S(1)}, bf16[256,1,512]{2,0,1:T(8,128)(2,1)S(1)}, u32[]{:S(2)}, u32[]{:S(2)}) collective-permute-start(bf16[256,1,512]{2,0,1:T(8,128)(2,1)S(1)} %copy.247), channel_id=1, source_target_pairs={{8,0},{16,8},{24,16},{32,24},{40,32},{48,40},{56,48},{64,56},{72,6... | collective-permute-start | bytes 786440 | tf_op jit(solution)/shard_map/ppermute | solution.py:21
  12.7 2.8 %collective-permute-done.1 = bf16[256,1,512]{2,0,1:T(8,128)(2,1)S(1)} collective-permute-done((bf16[256,1,512]{2,0,1:T(8,128)(2,1)S(1)}, bf16[256,1,512]{2,0,1:T(8,128)(2,1)S(1)}, u32[]{:S(2)}, u32[]{:S(2)}) %collective-permute-start.1) | collective-permute-done | bytes 262176 | tf_op jit(solution)/shard_map/ppermute | solution.py:21
  15.6 3.1 %fusion.44 = (bf16[256,4,512]{2,0,1:T(8,128)(2,1)S(1)}, bf16[256,4,512]{2,0,1:T(8,128)(2,1)S(1)}, bf16[256,4,512]{2,0,1:T(8,128)(2,1)S(1)}, bf16[256,4,512]{2,0,...) fusion(bf16[256,4,512]{2,0,1:T(8,128)(2,1)S(1)} %constant_dynam, ...), kind=kLoop, calls=%fused_computation.127 | loop fusion | flops 4718592 | bytes 10487296 | tf_op jit(solution)/shard_map/jit(_where)/select_n | solution.py:40
  19.3 0.2 convolution_add_fusion.28
  19.5 0.2 convolution_add_fusion.27
  19.9 0.2 convolution_add_fusion.25
  20.1 0.2 convolution_add_fusion.24
  20.3 0.2 convolution_add_fusion.23
  20.9 0.2 convolution_add_fusion.20
  21.1 0.2 convolution_add_fusion.19
  21.3 0.2 convolution_add_fusion.18
  21.7 0.2 fusion.25
  22.1 0.2 fusion.21
  22.7 0.2 fusion.18
  22.9 0.2 fusion.17
  23.1 0.2 fusion.16
  23.9 0.3 fusion.346
  24.5 0.6 broadcast_in_dim.262
  25.1 12.9 %all-to-all-start = ((f32[64,1,128]{2,1,0:T(1,128)}), f32[64,1,128]{2,1,0:T(1,128)S(1)}, u32[]{:S(2)}, u32[]{:S(2)}) async-start(f32[64,1,128]{2,1,0:T(1,128)} %broadcast_in_dim.262), calls=%async_computation | async-start | bytes 65536 | tf_op jit(solution)/shard_map/all_to_all | solution.py:94
  38.1 9.3 %all-to-all-done = f32[64,1,128]{2,1,0:T(1,128)S(1)} async-done(((f32[64,1,128]{2,1,0:T(1,128)}), f32[64,1,128]{2,1,0:T(1,128)S(1)}, u32[]{:S(2)}, u32[]{:S(2)}) %all-to-all-start) | async-done | bytes 32800 | tf_op jit(solution)/shard_map/all_to_all | solution.py:94
  48.1 1.7 %broadcast_select_fusion.1 = (bf16[32,2,8,1,16,1]{0,5,4,3,2,1:T(2,128)(2,1)S(1)}, bf16[32,2,8,1,16,1]{0,5,4,3,2,1:T(2,128)(2,1)S(1)}, bf16[32,2,8,1,16,1]{0,5,4,...) fusion(pred[8,16]{1,0:T(8,128)(4,1)S(1)} %fusion.317, ...), kind=kLoop, calls=%fused_computation.170 | loop fusion | flops 65536 | bytes 360576 | tf_op jit(solution)/shard_map/jit(_where)/select_n | solution.py:40
  49.9 0.3 fusion.99
  50.2 0.3 convolution_add_fusion.15
  50.4 0.3 convolution_add_fusion.14
  50.8 0.3 convolution_add_fusion.13
  51.1 0.3 convolution_add_fusion.12
  51.3 0.3 convolution_add_fusion.11
  51.6 0.3 convolution_add_fusion.10
  52.1 0.8 broadcast_select_fusion.5
  52.9 0.3 convolution_add_fusion.9
  53.2 0.3 convolution_add_fusion.8
  53.4 0.3 convolution_add_fusion.7
  53.7 0.3 convolution_add_fusion.6
  54.0 0.3 convolution_add_fusion.5
  54.4 0.3 convolution_add_fusion.4
  54.6 0.3 convolution_add_fusion.3
  54.9 0.3 convolution_add_fusion.2
  55.1 0.3 convolution_add_fusion.1
  55.5 0.3 fusion.10
  55.8 0.3 fusion.9
  56.0 0.3 fusion.8
  56.3 0.3 fusion.7
  56.6 0.3 fusion.6
  56.9 0.3 fusion.5
  57.2 0.3 fusion.4
  57.5 0.3 fusion.3
  57.7 0.3 fusion.2
  58.1 0.3 fusion.1
  58.3 0.3 fusion.11
  58.6 14.8 %all_to_all.25 = bf16[8,40,2,128]{3,1,2,0:T(8,128)(2,1)S(1)} all-to-all(bf16[8,40,2,128]{3,1,2,0:T(8,128)(2,1)S(1)} %copy.192), channel_id=1, replica_groups=mesh['space'=64,'chan'=8] {'chan'}, dimensions={0} | all-to-all | bytes 327680 | tf_op jit(solution)/shard_map/all_to_all | solution.py:159
  73.5 4.7 %collective-permute-start.2 = (f32[40,1,128]{2,0,1:T(8,128)S(1)}, f32[40,1,128]{2,0,1:T(8,128)S(1)}, u32[]{:S(2)}, u32[]{:S(2)}) collective-permute-start(f32[40,1,128]{2,0,1:T(8,128)S(1)} %slice.819), channel_id=1, source_target_pairs={{0,8},{8,16},{16,24},{24,32},{32,40},{40,48},{48,56},{56,64},{64,7... | collective-permute-start | bytes 61448 | tf_op jit(solution)/shard_map/ppermute | solution.py:29
  78.1 0.9 collective-permute-done.2
  79.5 16.5 %all_to_all.26 = f32[64,1,128]{2,1,0:T(1,128)S(1)} all-to-all(f32[64,1,128]{2,1,0:T(1,128)S(1)} %broadcast_in_dim.269), channel_id=1, replica_groups=mesh['space'=64,'chan'=8] {'space'}, dimensions={0} | all-to-all | bytes 65536 | tf_op jit(solution)/shard_map/all_to_all | solution.py:94
  96.5 9.8 %all_to_all.27 = bf16[8,40,1,128]{3,1,2,0:T(8,128)(2,1)S(1)} all-to-all(bf16[8,40,1,128]{3,1,2,0:T(8,128)(2,1)S(1)} %broadcast_in_dim.271), channel_id=1, replica_groups=mesh['space'=64,'chan'=8] {'chan'}, dimensions={0} | all-to-all | bytes 163840 | tf_op jit(solution)/shard_map/all_to_all | solution.py:94
  106.3 3.9 %collective-permute-start.3 = (bf16[320,1,128]{2,0,1:T(8,128)(2,1)S(1)}, bf16[320,1,128]{2,0,1:T(8,128)(2,1)S(1)}, u32[]{:S(2)}, u32[]{:S(2)}) collective-permute-start(bf16[320,1,128]{2,0,1:T(8,128)(2,1)S(1)} %bitcast.582), channel_id=1, source_target_pairs={{0,8},{8,16},{16,24},{24,32},{32,40},{40,48},{48,56},{56,64},{64,7... | collective-permute-start | bytes 245768 | tf_op jit(solution)/shard_map/ppermute | solution.py:18
  110.2 1.9 %collective-permute-start.4 = (bf16[320,1,128]{2,0,1:T(8,128)(2,1)S(1)}, bf16[320,1,128]{2,0,1:T(8,128)(2,1)S(1)}, u32[]{:S(2)}, u32[]{:S(2)}) collective-permute-start(bf16[320,1,128]{2,0,1:T(8,128)(2,1)S(1)} %bitcast.583), channel_id=1, source_target_pairs={{8,0},{16,8},{24,16},{32,24},{40,32},{48,40},{56,48},{64,56},{72,6... | collective-permute-start | bytes 245768 | tf_op jit(solution)/shard_map/ppermute | solution.py:21
  112.2 3.8 %collective-permute-done.4 = bf16[320,1,128]{2,0,1:T(8,128)(2,1)S(1)} collective-permute-done((bf16[320,1,128]{2,0,1:T(8,128)(2,1)S(1)}, bf16[320,1,128]{2,0,1:T(8,128)(2,1)S(1)}, u32[]{:S(2)}, u32[]{:S(2)}) %collective-permute-start.4) | collective-permute-done | bytes 81952 | tf_op jit(solution)/shard_map/ppermute | solution.py:21
  116.0 0.7 fusion.83
  116.7 0.5 copy-done.1
  121.0 0.2 fusion.347
  121.5 17.2 %all_to_all.28 = f32[64,1,128]{2,1,0:T(1,128)S(1)} all-to-all(f32[64,1,128]{2,1,0:T(1,128)S(1)} %broadcast_in_dim.277), channel_id=1, replica_groups=mesh['space'=64,'chan'=8] {'space'}, dimensions={0} | all-to-all | bytes 65536 | tf_op jit(solution)/shard_map/all_to_all | solution.py:94
  139.1 0.7 fusion.311
  (137 shorter events, 9.5 us)
Async XLA Ops:
  2.2 10.4 %copy-start = (bf16[256,2,512]{2,1,0:T(2,128)(2,1)S(1)}, bf16[256,2,512]{2,1,0:T(2,128)(2,1)}, u32[]{:S(2)}) copy-start(bf16[256,2,512]{2,1,0:T(2,128)(2,1)} %param.10) | copy-start | bytes 1572868
  2.3 10.3 %collective-permute-start = (bf16[256,1,512]{2,0,1:T(8,128)(2,1)S(1)}, bf16[256,1,512]{2,0,1:T(8,128)(2,1)S(1)}, u32[]{:S(2)}, u32[]{:S(2)}) collective-permute-start(bf16[256,1,512]{2,0,1:T(8,128)(2,1)S(1)} %copy.246), channel_id=1, source_target_pairs={{0,8},{8,16},{16,24},{24,32},{32,40},{40,48},{48,56},{56,64},{64,7... | collective-permute-start | bytes 786440 | tf_op jit(solution)/shard_map/ppermute | solution.py:18
  7.9 7.7 %collective-permute-start.1 = (bf16[256,1,512]{2,0,1:T(8,128)(2,1)S(1)}, bf16[256,1,512]{2,0,1:T(8,128)(2,1)S(1)}, u32[]{:S(2)}, u32[]{:S(2)}) collective-permute-start(bf16[256,1,512]{2,0,1:T(8,128)(2,1)S(1)} %copy.247), channel_id=1, source_target_pairs={{8,0},{16,8},{24,16},{32,24},{40,32},{48,40},{56,48},{64,56},{72,6... | collective-permute-start | bytes 786440 | tf_op jit(solution)/shard_map/ppermute | solution.py:21
  15.6 3.1 %copy-start.3 = (bf16[27,32,256]{2,1,0:T(8,128)(2,1)S(1)}, bf16[27,32,256]{2,1,0:T(8,128)(2,1)}, u32[]{:S(2)}) copy-start(bf16[27,32,256]{2,1,0:T(8,128)(2,1)} %param.11) | copy-start | bytes 1327108
  23.7 24.1 %copy-start.4 = (f32[32]{0:T(128)S(1)}, f32[32]{0:T(128)}, u32[]{:S(2)}) copy-start(f32[32]{0:T(128)} %param.13) | copy-start | bytes 388
  23.7 24.1 %copy-start.5 = (f32[32]{0:T(128)S(1)}, f32[32]{0:T(128)}, u32[]{:S(2)}) copy-start(f32[32]{0:T(128)} %param.12) | copy-start | bytes 388
  23.7 24.1 %copy-start.8 = (pred[2]{0:T(512)(128)(4,1)S(1)}, pred[2]{0:T(512)(128)(4,1)}, u32[]{:S(2)}) copy-start(pred[2]{0:T(512)(128)(4,1)} %constant.209.clone.1) | copy-start | bytes 10
  25.1 22.2 %all-to-all-start = ((f32[64,1,128]{2,1,0:T(1,128)}), f32[64,1,128]{2,1,0:T(1,128)S(1)}, u32[]{:S(2)}, u32[]{:S(2)}) async-start(f32[64,1,128]{2,1,0:T(1,128)} %broadcast_in_dim.262), calls=%async_computation | async-start | bytes 65536 | tf_op jit(solution)/shard_map/all_to_all | solution.py:94
  48.1 1.7 %copy-start.2 = (bf16[27,320,32]{1,2,0:T(8,128)(2,1)S(1)}, bf16[27,320,32]{1,2,0:T(8,128)(2,1)}, u32[]{:S(2)}) copy-start(bf16[27,320,32]{1,2,0:T(8,128)(2,1)} %param.14) | copy-start | bytes 1658884
  58.3 38.0 %copy-start.9 = (f32[40]{0:T(128)S(1)}, f32[40]{0:T(128)}, u32[]{:S(2)}) copy-start(f32[40]{0:T(128)} %param.16) | copy-start | bytes 484
  58.3 38.0 %copy-start.10 = (f32[40]{0:T(128)S(1)}, f32[40]{0:T(128)}, u32[]{:S(2)}) copy-start(f32[40]{0:T(128)} %param.15) | copy-start | bytes 484
  73.5 5.6 %collective-permute-start.2 = (f32[40,1,128]{2,0,1:T(8,128)S(1)}, f32[40,1,128]{2,0,1:T(8,128)S(1)}, u32[]{:S(2)}, u32[]{:S(2)}) collective-permute-start(f32[40,1,128]{2,0,1:T(8,128)S(1)} %slice.819), channel_id=1, source_target_pairs={{0,8},{8,16},{16,24},{24,32},{32,40},{40,48},{48,56},{56,64},{64,7... | collective-permute-start | bytes 61448 | tf_op jit(solution)/shard_map/ppermute | solution.py:29
  106.3 5.9 %collective-permute-start.3 = (bf16[320,1,128]{2,0,1:T(8,128)(2,1)S(1)}, bf16[320,1,128]{2,0,1:T(8,128)(2,1)S(1)}, u32[]{:S(2)}, u32[]{:S(2)}) collective-permute-start(bf16[320,1,128]{2,0,1:T(8,128)(2,1)S(1)} %bitcast.582), channel_id=1, source_target_pairs={{0,8},{8,16},{16,24},{24,32},{32,40},{40,48},{48,56},{56,64},{64,7... | collective-permute-start | bytes 245768 | tf_op jit(solution)/shard_map/ppermute | solution.py:18
  110.2 5.8 %collective-permute-start.4 = (bf16[320,1,128]{2,0,1:T(8,128)(2,1)S(1)}, bf16[320,1,128]{2,0,1:T(8,128)(2,1)S(1)}, u32[]{:S(2)}, u32[]{:S(2)}) collective-permute-start(bf16[320,1,128]{2,0,1:T(8,128)(2,1)S(1)} %bitcast.583), channel_id=1, source_target_pairs={{8,0},{16,8},{24,16},{32,24},{40,32},{48,40},{56,48},{64,56},{72,6... | collective-permute-start | bytes 245768 | tf_op jit(solution)/shard_map/ppermute | solution.py:21
  116.0 1.2 copy-start.1
  119.4 19.8 %copy-start.6 = (f32[40]{0:T(128)S(1)}, f32[40]{0:T(128)}, u32[]{:S(2)}) copy-start(f32[40]{0:T(128)} %param.19) | copy-start | bytes 484
  119.4 19.8 %copy-start.7 = (f32[40]{0:T(128)S(1)}, f32[40]{0:T(128)}, u32[]{:S(2)}) copy-start(f32[40]{0:T(128)} %param.18) | copy-start | bytes 484

commit v2 on v0

v2 whole, which is shorter than its diff:
```python
import jax
import jax.numpy as jnp
from jax import lax
from jax.experimental import pallas as pl
from jax.experimental.pallas import tpu as pltpu
from jax.sharding import PartitionSpec as P

ROWS = 16
COLS = 32
CELLS = ROWS * COLS
HALF_ROWS = ROWS // 2
HALF_COLS = COLS // 2
HALF_CELLS = HALF_ROWS * HALF_COLS
LANES = 128
PAIR = 48
AFFINE_ROWS = 16
EPSILON = 1e-05
SLOPE = 0.01

VMEM = pl.BlockSpec(memory_space=pltpu.VMEM)


def kernel_call(body, outputs, operands, flops, name):
    return pl.pallas_call(
        body,
        out_shape=outputs,
        in_specs=[VMEM] * len(operands),
        out_specs=jax.tree.map(lambda _: VMEM, outputs),
        compiler_params=pltpu.CompilerParams(vmem_limit_bytes=32 * 1024 * 1024),
        cost_estimate=pl.CostEstimate(flops=flops, bytes_accessed=2 << 20, transcendentals=0),
        name=name,
    )(*operands)


def iota(shape, dim):
    return lax.broadcasted_iota(jnp.int32, shape, dim)


def dot(a, b):
    return jnp.dot(a, b, preferred_element_type=jnp.float32)


def dot_nt(a, b):
    return lax.dot_general(a, b, (((1,), (1,)), ((), ())), preferred_element_type=jnp.float32)


def to_row(column, offset):
    n = column.shape[0]
    hit = iota((n, LANES), 1) == iota((n, LANES), 0) + offset
    return jnp.sum(jnp.where(hit, column, 0.0), axis=0, keepdims=True)


def to_column(row, offset, n):
    width = row.shape[1]
    hit = iota((n, width), 1) == iota((n, width), 0) + offset
    return jnp.sum(jnp.where(hit, row, 0.0), axis=1, keepdims=True)


def shift_add(taps, out_chans, row_count, col_count):
    cells = row_count * col_count
    block = 3 * out_chans
    cell = iota((block, cells), 1)
    above = pltpu.roll(taps[:block], col_count, axis=1)
    below = pltpu.roll(taps[2 * block :], cells - col_count, axis=1)
    rows = (
        taps[block : 2 * block]
        + jnp.where(cell >= col_count, above, 0.0)
        + jnp.where(cell < cells - col_count, below, 0.0)
    )
    column = iota((out_chans, cells), 1) % col_count
    left = pltpu.roll(rows[:out_chans], 1, axis=1)
    right = pltpu.roll(rows[2 * out_chans :], cells - 1, axis=1)
    return (
        rows[out_chans : 2 * out_chans]
        + jnp.where(column != 0, left, 0.0)
        + jnp.where(column != col_count - 1, right, 0.0)
    )


def leaky(value):
    return jnp.where(value >= 0, value, SLOPE * value)


def send_kernel(features_ref, weight_ref, slices_ref, send_ref):
    chans = features_ref.shape[0]
    pairs = features_ref[...].reshape(2 * chans, CELLS)
    for j in range(2):
        pick = (iota((chans, 2 * chans), 1) == 2 * iota((chans, 2 * chans), 0) + j).astype(
            jnp.bfloat16
        )
        slices_ref[j] = dot(pick, pairs).astype(jnp.bfloat16)
    block = weight_ref.shape[0] // 3
    out_chans = block // 9
    lower, upper = slices_ref[0], slices_ref[1]
    tap0, tap1 = weight_ref[:block], weight_ref[block : 2 * block]
    send_ref[0] = shift_add(dot(tap0, lower) + dot(tap1, upper), out_chans, ROWS, COLS)
    send_ref[1] = shift_add(dot(tap0, upper), out_chans, ROWS, COLS)


def own_kernel(
    slices_ref, weight_ref, third_ref, gain_ref, bias_ref,
    own_ref, select_ref, stacked_ref, affine_ref,
):
    block = weight_ref.shape[0] // 3
    out_chans = block // 9
    lower, upper = slices_ref[0], slices_ref[1]
    tap1, tap2 = weight_ref[block : 2 * block], weight_ref[2 * block :]
    own_ref[0] = shift_add(dot(tap2, lower), out_chans, ROWS, COLS)
    own_ref[1] = shift_add(dot(tap1, lower) + dot(tap2, upper), out_chans, ROWS, COLS)

    place = iota((HALF_CELLS, CELLS), 0)
    cell = iota((HALF_CELLS, CELLS), 1)
    row, column = cell // COLS, cell % COLS
    row_gap = row - 2 * (place // HALF_COLS)
    column_gap = column - 2 * (place % HALF_COLS)
    for tap in range(9):
        hit = (row_gap == tap // 3 - 1) & (column_gap == tap % 3 - 1)
        select_ref[tap * HALF_CELLS : (tap + 1) * HALF_CELLS] = hit.astype(jnp.bfloat16)

    third_out, third_in = third_ref.shape[1:]
    stacked_ref[...] = jnp.zeros_like(stacked_ref)
    wide = stacked_ref.shape[2] // 3
    for depth in range(3):
        for tap in range(9):
            stacked_ref[tap, :third_out, depth * wide : depth * wide + third_in] = third_ref[
                depth * 9 + tap
            ]

    n = gain_ref.shape[1]
    start = lax.axis_index("chan") * n
    rows = []
    lane = iota((n, LANES), 1)
    channel = iota((n, LANES), 0) + start
    columns = [to_column(ref[...], 0, n) for ref in (gain_ref, bias_ref)]
    for column in columns:
        for k in range(2):
            hit = channel == lane + k * LANES
            rows.append(jnp.sum(jnp.where(hit, column, 0.0), axis=0, keepdims=True))
    gain_hit = channel == lane + 2 * LANES
    bias_hit = (channel == lane + 2 * LANES - LANES // 2) & (lane >= LANES // 2)
    tail = jnp.where(gain_hit, columns[0], 0.0) + jnp.where(bias_hit, columns[1], 0.0)
    rows.append(jnp.sum(tail, axis=0, keepdims=True))
    row = iota((AFFINE_ROWS, LANES), 0)
    values = jnp.zeros((AFFINE_ROWS, LANES), jnp.float32)
    for k, value in enumerate(rows):
        values = jnp.where(row == k, value, values)
    high = values.astype(jnp.bfloat16).astype(jnp.float32)
    middle = (values - high).astype(jnp.bfloat16).astype(jnp.float32)
    low = values - high - middle
    affine_ref[...] = (
        high + pltpu.roll(middle, 5, axis=0) + pltpu.roll(low, 10, axis=0)
    ).astype(jnp.bfloat16)


def total_kernel(own_ref, got_ref, first0_ref, first1_ref, copies_ref):
    at_start = lax.axis_index("space") == 0
    first0 = got_ref[0] + jnp.where(at_start, 0.0, own_ref[0])
    first1 = own_ref[1] + jnp.where(at_start, 0.0, got_ref[1])
    first0_ref[...] = first0
    first1_ref[...] = first1
    cells = 2 * CELLS
    mean = (
        jnp.sum(first0, axis=1, keepdims=True) + jnp.sum(first1, axis=1, keepdims=True)
    ) / cells
    spread = (
        jnp.sum((first0 - mean) ** 2, axis=1, keepdims=True)
        + jnp.sum((first1 - mean) ** 2, axis=1, keepdims=True)
    ) / cells
    row = to_row(mean, 0) + to_row(spread, mean.shape[0])
    copies_ref[...] = jnp.broadcast_to(row, copies_ref.shape)


def column_statistics(rows, n):
    average = jnp.mean(rows, axis=0, keepdims=True)
    apart = jnp.mean((rows - average) ** 2, axis=0, keepdims=True)
    mean = to_column(average, 0, n)
    spread = to_column(average, n, n) + to_column(apart, 0, n)
    return mean, spread


def down_kernel(
    rows_ref, first0_ref, first1_ref, first2_ref, gain_ref, bias_ref,
    select_ref, weight_ref, affine_ref, copies_ref,
):
    n = first0_ref.shape[0]
    mean, spread = column_statistics(rows_ref[...], n)
    gain = to_column(gain_ref[...], 0, n)
    bias = to_column(bias_ref[...], 0, n)
    scale = gain * lax.rsqrt(spread + EPSILON)
    at_start = lax.axis_index("space") == 0

    def level(ref):
        return leaky(scale * (ref[...] - mean) + bias)

    layers = jnp.concatenate(
        [
            jnp.where(at_start, 0.0, level(first0_ref)),
            level(first1_ref),
            level(first2_ref),
            jnp.zeros((LANES - 3 * n, CELLS), jnp.float32),
        ],
        axis=0,
    ).astype(jnp.bfloat16)
    out_chans = weight_ref.shape[1]
    picked = dot_nt(select_ref[...], layers).astype(jnp.bfloat16)
    windows, weights = [], []
    for tap in range(9):
        windows.append(picked[tap * HALF_CELLS : (tap + 1) * HALF_CELLS])
        for depth in range(3):
            at = (depth * 9 + tap) * n
            weights.append(weight_ref[at : at + n])
        weights.append(jnp.zeros((LANES - 3 * n, out_chans), jnp.bfloat16))
    parts = dot(jnp.concatenate(windows, axis=1), jnp.concatenate(weights, axis=0))
    half = HALF_CELLS // 2
    tail = parts[:, 2 * LANES :]
    packed = jnp.concatenate(
        [
            parts[:, :LANES],
            parts[:, LANES : 2 * LANES],
            jnp.concatenate([tail[:half], tail[half:]], axis=1),
        ],
        axis=0,
    ).astype(jnp.bfloat16)
    message = jnp.concatenate([packed, affine_ref[...]], axis=0)
    for c in range(copies_ref.shape[0]):
        copies_ref[c] = message


def fold(row):
    return row + pltpu.roll(row, LANES // 2, axis=1)


def reduced_kernel(parts_ref, packed_ref, affine_ref, copies_ref):
    total = parts_ref[0].astype(jnp.float32)
    for c in range(1, parts_ref.shape[0]):
        total = total + parts_ref[c].astype(jnp.float32)
    size = packed_ref.shape[0]
    packed = total[:size]
    packed_ref[...] = packed
    tail = total[size:]
    affine_ref[...] = (
        tail
        + pltpu.roll(tail, AFFINE_ROWS - 5, axis=0)
        + pltpu.roll(tail, AFFINE_ROWS - 10, axis=0)
    )
    blocks = (packed[:LANES], packed[LANES : 2 * LANES], packed[2 * LANES :])
    means, spreads = [], []
    for k, block in enumerate(blocks):
        mean = jnp.sum(block, axis=0, keepdims=True) / HALF_CELLS
        if k == 2:
            mean = fold(mean)
        spread = jnp.sum((block - mean) ** 2, axis=0, keepdims=True) / HALF_CELLS
        if k == 2:
            spread = fold(spread)
        means.append(mean)
        spreads.append(spread)
    lane = iota((1, LANES), 1)
    last = jnp.where(lane < LANES // 2, means[2], spreads[2])
    row = jnp.concatenate(means[:2] + spreads[:2] + [last], axis=1)
    copies_ref[...] = jnp.broadcast_to(row, copies_ref.shape)


def third_kernel(
    rows_ref, own_ref, before_ref, after_ref, affine_ref, stacked_ref, third_ref, copies_ref
):
    rows = rows_ref[...]
    average = jnp.mean(rows, axis=0, keepdims=True)
    apart = jnp.mean((rows - average) ** 2, axis=0, keepdims=True)
    lane = iota((1, LANES), 1)
    in_low = lane < LANES // 2

    def piece(row, k):
        return row[:, k * LANES : (k + 1) * LANES]

    def swap(row):
        return pltpu.roll(row, LANES // 2, axis=1)

    last, last_apart = piece(average, 4), piece(apart, 4)
    affine = affine_ref[...]
    gains = [affine[0:1], affine[1:2]]
    biases = [affine[2:3], affine[3:4]]
    both = affine[4:5]
    gains.append(jnp.where(in_low, both, swap(both)))
    biases.append(jnp.where(in_low, swap(both), both))
    means = [piece(average, 0), piece(average, 1), jnp.where(in_low, last, swap(last))]
    spreads = [
        piece(average, 2) + piece(apart, 0),
        piece(average, 3) + piece(apart, 1),
        jnp.where(in_low, swap(last) + last_apart, last + swap(last_apart)),
    ]
    space = lax.axis_index("space")
    here = [space != 0, None, space != lax.axis_size("space") - 1]
    size = own_ref.shape[0]
    edges = (0, LANES, 2 * LANES, size)
    columns = []
    for ref, keep in zip((before_ref, own_ref, after_ref), here):
        blocks = []
        for k in range(3):
            block = ref[edges[k] : edges[k + 1]]
            scale = gains[k] * lax.rsqrt(spreads[k] + EPSILON)
            block = leaky(scale * (block - means[k]) + biases[k])
            if keep is not None:
                block = jnp.where(keep, block, 0.0)
            blocks.append(block)
        tail = blocks[2]
        tail = jnp.concatenate([tail, pltpu.roll(tail, LANES // 2, axis=1)], axis=0)
        blocks[2] = jnp.where(iota(tail.shape, 1) < LANES // 2, tail, 0.0)
        columns += [block.astype(jnp.bfloat16) for block in blocks]
    bottom = jnp.concatenate(columns, axis=1)
    taps = dot_nt(stacked_ref[...].reshape(9 * PAIR, bottom.shape[1]), bottom)
    n = third_ref.shape[0]
    third = shift_add(taps, PAIR, HALF_ROWS, HALF_COLS)[:n]
    third_ref[...] = third
    mean = jnp.sum(third, axis=1, keepdims=True) / HALF_CELLS
    spread = jnp.sum((third - mean) ** 2, axis=1, keepdims=True) / HALF_CELLS
    row = to_row(mean, 0) + to_row(spread, n)
    copies_ref[...] = jnp.broadcast_to(row, copies_ref.shape)


def last_kernel(rows_ref, third_ref, gain_ref, bias_ref, out_ref):
    n = third_ref.shape[0]
    mean, spread = column_statistics(rows_ref[...], n)
    gain = to_column(gain_ref[...], 0, n)
    bias = to_column(bias_ref[...], 0, n)
    scale = gain * lax.rsqrt(spread + EPSILON)
    out_ref[...] = leaky(scale * (third_ref[...] - mean) + bias).astype(jnp.bfloat16)


def neighbour(value, by):
    count = lax.axis_size("space")
    return lax.ppermute(value, "space", [(i, (i + by) % count) for i in range(count)])


def exchange(copies, axis):
    return lax.all_to_all(copies, axis, 0, 0, tiled=True)


def struct(shape, dtype=jnp.float32):
    return jax.ShapeDtypeStruct(shape, dtype)


def local(
    features,
    first_weight,
    first_gain,
    first_bias,
    down_weight,
    down_gain,
    down_bias,
    third_weight,
    third_gain,
    third_bias,
):
    spaces, chans = lax.axis_size("space"), lax.axis_size("chan")
    in_chans = features.shape[0]
    n = first_weight.shape[1]
    m = third_weight.shape[1]
    wide = down_weight.shape[1]
    packed_rows = wide * HALF_CELLS // LANES
    first_weight = first_weight.reshape(27 * n, in_chans)
    down_weight = jnp.transpose(down_weight, (0, 2, 1)).reshape(27 * n, wide)
    gains = [v.reshape(1, -1) for v in (first_gain, down_gain, third_gain)]
    biases = [v.reshape(1, -1) for v in (first_bias, down_bias, third_bias)]
    unit = 2 * 9 * n * in_chans * CELLS

    slices, send = kernel_call(
        send_kernel,
        (struct((2, in_chans, CELLS), jnp.bfloat16), struct((2, n, CELLS))),
        (features, first_weight),
        4 * unit,
        "send",
    )
    got = neighbour(send, 1)
    own, select, stacked, affine = kernel_call(
        own_kernel,
        (
            struct((2, n, CELLS)),
            struct((9 * HALF_CELLS, CELLS), jnp.bfloat16),
            struct((9, PAIR, 3 * 3 * LANES), jnp.bfloat16),
            struct((AFFINE_ROWS, LANES), jnp.bfloat16),
        ),
        (slices, first_weight, third_weight, gains[1], biases[1]),
        4 * unit,
        "own",
    )
    first0, first1, copies = kernel_call(
        total_kernel,
        (struct((n, CELLS)), struct((n, CELLS)), struct((spaces, LANES))),
        (own, got),
        1 << 20,
        "total",
    )
    first2 = neighbour(first0, -1)
    rows = exchange(copies, "space")
    copies = kernel_call(
        down_kernel,
        struct((chans, packed_rows + AFFINE_ROWS, LANES), jnp.bfloat16),
        (rows, first0, first1, first2, gains[0], biases[0], select, down_weight, affine),
        unit,
        "down",
    )
    parts = exchange(copies, "chan")
    packed, affine, copies = kernel_call(
        reduced_kernel,
        (struct((packed_rows, LANES)), struct((AFFINE_ROWS, LANES)), struct((spaces, 5 * LANES))),
        (parts,),
        1 << 20,
        "reduced",
    )
    before, after = neighbour(packed, 1), neighbour(packed, -1)
    rows = exchange(copies, "space")
    third, copies = kernel_call(
        third_kernel,
        (struct((m, HALF_CELLS)), struct((spaces, LANES))),
        (rows, packed, before, after, affine, stacked),
        unit,
        "third",
    )
    rows = exchange(copies, "space")
    out = kernel_call(
        last_kernel,
        struct((m, HALF_CELLS), jnp.bfloat16),
        (rows, third, gains[2], biases[2]),
        1 << 20,
        "last",
    )
    return out.reshape(m, 1, HALF_CELLS)


def solution(mesh):
    return jax.shard_map(
        local,
        mesh=mesh,
        in_specs=(
            P(None, "space", None),
            P(None, "chan", None),
            P("chan"),
            P("chan"),
            P(None, None, "chan"),
            P("chan"),
            P("chan"),
            P(None, "chan", None),
            P("chan"),
            P("chan"),
        ),
        out_specs=P("chan", "space", None),
        check_vma=False,
    )
```

time: 877 us -> 104 us (0.12)
  blocking collectives: 772 us -> 60.1 us
  waiting for transfers between devices: 31.9 us -> 7.16 us
  matrix products: 16.6 us -> 0 us
  between operations: 14.2 us -> 0.15 us
    psum x6 -> x0, blocking collectives: 753 us -> none  [the longest x3 377 us: normalize(): average = lax.psum(jnp.sum(summed, axis=(1, 2)), 'space') / cell_total]
    all_to_all x0 -> x3, blocking collectives: none -> 60.1 us  [exchange(): return lax.all_to_all(copies, axis, 0, 0, tiled=True)]
    unnamed x2 -> x0, waiting for transfers between devices: 27.4 us -> none
    all_gather x1 -> x0, blocking collectives: 18.5 us -> none  [local(): gathered = lax.all_gather(bottom, 'chan', axis=0, tiled=True)]
    dot_general x81 -> x0, matrix products: 16.6 us -> none  [the longest x54 9.32 us: convolve_same(): jnp.einsum('oi,izp->ozp', kernel, moved_cells[:, depth_tap:depth_tap + de...]
    ppermute x5 -> x4, starting transfers between devices: 29.4 us -> 20.1 us  [neighbour(): lax.ppermute(value, 'space', [(i, (i + by) % count) for i in range(count)])]
  transfers between devices with their start and end apart: 6 -> 5, of which waited for: 4 -> 2; matrix products, arithmetic and copies ran while one was open for 0% -> 0% of each run, Pallas kernels for 0% -> 1%
where the time goes in v2:
time: 104 us
  blocking collectives  60.1 us (58%)
  starting transfers between devices  26.8 us (26%)
  waiting for transfers between devices  7.16 us (7%)
  Pallas kernels  5.02 us (5%)
  local copies, waits for them, and re-layouts  4.31 us (4%)
    all_to_all x3, blocking collectives, exchange(): return lax.all_to_all(copies, axis, 0, 0, tiled=True)  60.1 us
    ppermute x4, starting transfers between devices, neighbour(): lax.ppermute(value, 'space', [(i, (i + by) % count) for i in range(count)])  20.1 us
    all_to_all x1, starting transfers between devices, exchange(): return lax.all_to_all(copies, axis, 0, 0, tiled=True)  6.7 us
    all_to_all x1, waiting for transfers between devices, exchange(): return lax.all_to_all(copies, axis, 0, 0, tiled=True)  5.12 us
    pallas_call x7, Pallas kernels, kernel_call(): pl.pallas_call(body, out_shape=outputs, in_specs=[VMEM] * len(operands),...  5.02 us
    unnamed x21, local copies, waits for them, and re-layouts  3.48 us
  transfers between devices with their start and end apart: 5, of which 2 were waited for; matrix products, arithmetic and copies ran while one was open for 0% of the time, Pallas kernels for 1%

profile of v2, /device:TPU:1, one launch (start us, length us, event | category | flops | bytes accessed | tf_op | source)
XLA Modules:
  0.0 103.5 jit_solution(8574174096350050771)
XLA Ops:
  0.0 0.0 copy-start
  0.0 0.0 copy-start.2
  0.0 1.1 %copy-done.2 = bf16[27,32,256]{2,1,0:T(8,128)(2,1)S(1)} copy-done((bf16[27,32,256]{2,1,0:T(8,128)(2,1)S(1)}, bf16[27,32,256]{2,1,0:T(8,128)(2,1)}, u32[]{:S(2)}) %copy-start.2) | copy-done | bytes 442392
  1.1 0.0 copy-start.9
  1.1 1.0 %copy-done.9 = bf16[256,2,512]{2,1,0:T(2,128)(2,1)S(1)} copy-done((bf16[256,2,512]{2,1,0:T(2,128)(2,1)S(1)}, bf16[256,2,512]{2,1,0:T(2,128)(2,1)}, u32[]{:S(2)}) %copy-start.9) | copy-done | bytes 524312
  2.1 1.0 send.1
  3.2 0.0 copy-start.1
  3.2 0.0 copy-start.3
  3.2 0.0 copy-start.4
  3.2 5.5 %collective-permute-start = (f32[2,32,512]{2,1,0:T(8,128)S(1)}, f32[2,32,512]{2,1,0:T(8,128)S(1)}, u32[]{:S(2)}, u32[]{:S(2)}) collective-permute-start(f32[2,32,512]{2,1,0:T(8,128)S(1)} %get-tuple-element.21), channel_id=1, source_target_pairs={{0,8},{8,16},{16,24},{24,32},{32,40},{40,48},{48,56},{56,64},{64,7... | collective-permute-start | bytes 393224 | tf_op jit(solution)/shard_map/ppermute | solution.py:331
  8.7 0.0 copy-done
  8.8 0.0 copy-start.7
  8.8 0.6 copy-done.7
  9.4 0.0 copy-start.8
  9.4 0.7 copy-done.8
  10.1 0.9 own.1
  10.9 2.0 %collective-permute-done.got_ref = f32[2,32,512]{2,1,0:T(8,128)S(1)} collective-permute-done((f32[2,32,512]{2,1,0:T(8,128)S(1)}, f32[2,32,512]{2,1,0:T(8,128)S(1)}, u32[]{:S(2)}, u32[]{:S(2)}) %collective-permute-start) | collective-permute-done | bytes 131104 | tf_op jit(solution)/shard_map/ppermute | solution.py:331
  13.0 0.2 total.1
  13.2 9.0 %collective-permute-start.1 = (f32[32,512]{1,0:T(8,128)S(1)}, f32[32,512]{1,0:T(8,128)S(1)}, u32[]{:S(2)}, u32[]{:S(2)}) collective-permute-start(f32[32,512]{1,0:T(8,128)S(1)} %get-tuple-element.23.first0_ref), channel_id=1, source_target_pairs={{0,504},{8,0},{16,8},{24,16},{32,24},{40,32},{48,40},{56,48},{64,5... | collective-permute-start | bytes 196616 | tf_op jit(solution)/shard_map/ppermute | solution.py:331
  22.2 14.8 %all_to_all.38 = f32[64,1,128]{2,1,0:T(1,128)S(1)} all-to-all(f32[64,1,128]{2,1,0:T(1,128)S(1)} %bitcast.30), channel_id=1, replica_groups=mesh['space'=64,'chan'=8] {'space'}, dimensions={0} | all-to-all | bytes 65536 | tf_op jit(solution)/shard_map/all_to_all | solution.py:335
  37.0 0.0 collective-permute-done.1.first2_ref
  37.0 0.0 copy-done.1
  37.0 0.0 copy-done.3
  37.0 0.0 copy-done.4
  37.0 1.1 %down.1 = bf16[8,336,128]{2,1,0:T(8,128)(2,1)S(1)} custom-call(f32[64,128]{1,0:T(8,128)S(1)} %bitcast.28, f32[32,512]{1,0:T(8,128)S(1)} %get-tuple-element.23.first0_ref, f32[32,512]{1,0:T(8,128)S(1)} %get-tuple-element.24.first1_ref, f32[32,512]{1,0:T(8,128)S(1)} %collective-permute-done.1.first2_ref, f32[1,32]{1,0:T(1,128)S(1)} %bitcast.32, ...), custom_call_target="tpu_custom_call" | custom-call | flops 75497472 | bytes 2097152 | tf_op jit(solution)/shard_map/down/pallas_call | solution.py:24
  38.1 26.0 %all_to_all.39.parts_ref = bf16[8,336,128]{2,1,0:T(8,128)(2,1)S(1)} all-to-all(bf16[8,336,128]{2,1,0:T(8,128)(2,1)S(1)} %down.1), channel_id=1, replica_groups=mesh['space'=64,'chan'=8] {'chan'}, dimensions={0} | all-to-all | bytes 1376256 | tf_op jit(solution)/shard_map/all_to_all | solution.py:335
  64.1 0.2 reduced.1
  64.3 0.8 copy.12
  65.2 0.0 copy-start.5
  65.2 0.0 copy-start.6
  65.2 6.7 %all-to-all-start.2 = ((f32[64,1,640]{2,1,0:T(1,128)}), f32[64,1,640]{2,1,0:T(1,128)S(1)}, u32[]{:S(2)}, u32[]{:S(2)}) async-start(f32[64,1,640]{2,1,0:T(1,128)} %copy.12), calls=%async_computation.2 | async-start | bytes 327680 | tf_op jit(solution)/shard_map/all_to_all | solution.py:335
  71.9 2.5 %collective-permute-start.3 = (f32[320,128]{1,0:T(8,128)S(1)}, f32[320,128]{1,0:T(8,128)S(1)}, u32[]{:S(2)}, u32[]{:S(2)}) collective-permute-start(f32[320,128]{1,0:T(8,128)S(1)} %get-tuple-element.28.own_ref), channel_id=1, source_target_pairs={{0,504},{8,0},{16,8},{24,16},{32,24},{40,32},{48,40},{56,48},{64,5... | collective-permute-start | bytes 491528 | tf_op jit(solution)/shard_map/ppermute | solution.py:331
  74.4 3.1 %collective-permute-start.2 = (f32[320,128]{1,0:T(8,128)S(1)}, f32[320,128]{1,0:T(8,128)S(1)}, u32[]{:S(2)}, u32[]{:S(2)}) collective-permute-start(f32[320,128]{1,0:T(8,128)S(1)} %get-tuple-element.28.own_ref), channel_id=1, source_target_pairs={{0,8},{8,16},{16,24},{24,32},{32,40},{40,48},{48,56},{56,64},{64,7... | collective-permute-start | bytes 491528 | tf_op jit(solution)/shard_map/ppermute | solution.py:331
  77.5 5.1 %all-to-all-done.2 = f32[64,1,640]{2,1,0:T(1,128)S(1)} async-done(((f32[64,1,640]{2,1,0:T(1,128)}), f32[64,1,640]{2,1,0:T(1,128)S(1)}, u32[]{:S(2)}, u32[]{:S(2)}) %all-to-all-start.2) | async-done | bytes 163872 | tf_op jit(solution)/shard_map/all_to_all | solution.py:335
  82.6 0.0 collective-permute-done.3.after_ref
  82.6 0.0 collective-permute-done.2.before_ref
  82.6 0.9 third.1
  83.5 19.3 %all_to_all.40 = f32[64,1,128]{2,1,0:T(1,128)S(1)} all-to-all(f32[64,1,128]{2,1,0:T(1,128)S(1)} %bitcast.31), channel_id=1, replica_groups=mesh['space'=64,'chan'=8] {'space'}, dimensions={0} | all-to-all | bytes 65536 | tf_op jit(solution)/shard_map/all_to_all | solution.py:335
  102.8 0.0 copy-done.5
  102.8 0.0 copy-done.6
  102.8 0.7 last.1
  (1 shorter events, 0.0 us)
Async XLA Ops:
  0.0 8.7 %copy-start = (bf16[27,40,320]{2,1,0:T(8,128)(2,1)S(1)}, bf16[27,40,320]{2,1,0:T(8,128)(2,1)}, u32[]{:S(2)}) copy-start(bf16[27,40,320]{2,1,0:T(8,128)(2,1)} %third_ref.1) | copy-start | bytes 2073604
  0.0 1.1 %copy-start.2 = (bf16[27,32,256]{2,1,0:T(8,128)(2,1)S(1)}, bf16[27,32,256]{2,1,0:T(8,128)(2,1)}, u32[]{:S(2)}) copy-start(bf16[27,32,256]{2,1,0:T(8,128)(2,1)} %param.11) | copy-start | bytes 1327108
  1.1 1.0 %copy-start.9 = (bf16[256,2,512]{2,1,0:T(2,128)(2,1)S(1)}, bf16[256,2,512]{2,1,0:T(2,128)(2,1)}, u32[]{:S(2)}) copy-start(bf16[256,2,512]{2,1,0:T(2,128)(2,1)} %features_ref.1) | copy-start | bytes 1572868
  3.2 33.8 %copy-start.1 = (bf16[27,320,32]{1,2,0:T(8,128)(2,1)S(1)}, bf16[27,320,32]{1,2,0:T(8,128)(2,1)}, u32[]{:S(2)}) copy-start(bf16[27,320,32]{1,2,0:T(8,128)(2,1)} %param.14) | copy-start | bytes 1658884
  3.2 33.8 %copy-start.3 = (f32[32]{0:T(128)S(1)}, f32[32]{0:T(128)}, u32[]{:S(2)}) copy-start(f32[32]{0:T(128)} %param.12) | copy-start | bytes 388
  3.2 33.8 %copy-start.4 = (f32[32]{0:T(128)S(1)}, f32[32]{0:T(128)}, u32[]{:S(2)}) copy-start(f32[32]{0:T(128)} %param.13) | copy-start | bytes 388
  3.2 9.8 %collective-permute-start = (f32[2,32,512]{2,1,0:T(8,128)S(1)}, f32[2,32,512]{2,1,0:T(8,128)S(1)}, u32[]{:S(2)}, u32[]{:S(2)}) collective-permute-start(f32[2,32,512]{2,1,0:T(8,128)S(1)} %get-tuple-element.21), channel_id=1, source_target_pairs={{0,8},{8,16},{16,24},{24,32},{32,40},{40,48},{48,56},{56,64},{64,7... | collective-permute-start | bytes 393224 | tf_op jit(solution)/shard_map/ppermute | solution.py:331
  8.8 0.7 copy-start.7
  9.4 0.7 copy-start.8
  13.2 23.8 %collective-permute-start.1 = (f32[32,512]{1,0:T(8,128)S(1)}, f32[32,512]{1,0:T(8,128)S(1)}, u32[]{:S(2)}, u32[]{:S(2)}) collective-permute-start(f32[32,512]{1,0:T(8,128)S(1)} %get-tuple-element.23.first0_ref), channel_id=1, source_target_pairs={{0,504},{8,0},{16,8},{24,16},{32,24},{40,32},{48,40},{56,48},{64,5... | collective-permute-start | bytes 196616 | tf_op jit(solution)/shard_map/ppermute | solution.py:331
  65.2 37.6 %copy-start.5 = (f32[40]{0:T(128)S(1)}, f32[40]{0:T(128)}, u32[]{:S(2)}) copy-start(f32[40]{0:T(128)} %param.18) | copy-start | bytes 484
  65.2 37.7 %copy-start.6 = (f32[40]{0:T(128)S(1)}, f32[40]{0:T(128)}, u32[]{:S(2)}) copy-start(f32[40]{0:T(128)} %param.19) | copy-start | bytes 484
  65.2 17.4 %all-to-all-start.2 = ((f32[64,1,640]{2,1,0:T(1,128)}), f32[64,1,640]{2,1,0:T(1,128)S(1)}, u32[]{:S(2)}, u32[]{:S(2)}) async-start(f32[64,1,640]{2,1,0:T(1,128)} %copy.12), calls=%async_computation.2 | async-start | bytes 327680 | tf_op jit(solution)/shard_map/all_to_all | solution.py:335
  71.9 10.7 %collective-permute-start.3 = (f32[320,128]{1,0:T(8,128)S(1)}, f32[320,128]{1,0:T(8,128)S(1)}, u32[]{:S(2)}, u32[]{:S(2)}) collective-permute-start(f32[320,128]{1,0:T(8,128)S(1)} %get-tuple-element.28.own_ref), channel_id=1, source_target_pairs={{0,504},{8,0},{16,8},{24,16},{32,24},{40,32},{48,40},{56,48},{64,5... | collective-permute-start | bytes 491528 | tf_op jit(solution)/shard_map/ppermute | solution.py:331
  74.4 8.2 %collective-permute-start.2 = (f32[320,128]{1,0:T(8,128)S(1)}, f32[320,128]{1,0:T(8,128)S(1)}, u32[]{:S(2)}, u32[]{:S(2)}) collective-permute-start(f32[320,128]{1,0:T(8,128)S(1)} %get-tuple-element.28.own_ref), channel_id=1, source_target_pairs={{0,8},{8,16},{16,24},{24,32},{32,40},{40,48},{48,56},{56,64},{64,7... | collective-permute-start | bytes 491528 | tf_op jit(solution)/shard_map/ppermute | solution.py:331

commit v3 on v2

v3 whole, which is shorter than its diff:
```python
import jax
import jax.numpy as jnp
from jax import lax
from jax.experimental import pallas as pl
from jax.experimental.pallas import tpu as pltpu
from jax.sharding import PartitionSpec as P

ROWS = 16
COLS = 32
CELLS = ROWS * COLS
HALF_ROWS = ROWS // 2
HALF_COLS = COLS // 2
HALF_CELLS = HALF_ROWS * HALF_COLS
LANES = 128
PAIR = 48
EPSILON = 1e-05
SLOPE = 0.01

VMEM = pl.BlockSpec(memory_space=pltpu.VMEM)
HBM = pl.BlockSpec(memory_space=pltpu.HBM)


def kernel_call(body, outputs, operands, flops, name, in_specs=None, scratch=()):
    return pl.pallas_call(
        body,
        out_shape=outputs,
        in_specs=in_specs or [VMEM] * len(operands),
        out_specs=jax.tree.map(lambda _: VMEM, outputs),
        scratch_shapes=scratch,
        compiler_params=pltpu.CompilerParams(vmem_limit_bytes=32 * 1024 * 1024),
        cost_estimate=pl.CostEstimate(flops=flops, bytes_accessed=2 << 20, transcendentals=0),
        name=name,
    )(*operands)


def iota(shape, dim):
    return lax.broadcasted_iota(jnp.int32, shape, dim)


def dot(a, b):
    return jnp.dot(a, b, preferred_element_type=jnp.float32)


def dot_nt(a, b):
    return lax.dot_general(a, b, (((1,), (1,)), ((), ())), preferred_element_type=jnp.float32)


def to_row(column, offset):
    n = column.shape[0]
    hit = iota((n, LANES), 1) == iota((n, LANES), 0) + offset
    return jnp.sum(jnp.where(hit, column, 0.0), axis=0, keepdims=True)


def to_column(row, offset, n):
    width = row.shape[1]
    hit = iota((n, width), 1) == iota((n, width), 0) + offset
    return jnp.sum(jnp.where(hit, row, 0.0), axis=1, keepdims=True)


def shift_add(taps, out_chans, row_count, col_count):
    cells = row_count * col_count
    block = 3 * out_chans
    cell = iota((block, cells), 1)
    above = pltpu.roll(taps[:block], col_count, axis=1)
    below = pltpu.roll(taps[2 * block :], cells - col_count, axis=1)
    rows = (
        taps[block : 2 * block]
        + jnp.where(cell >= col_count, above, 0.0)
        + jnp.where(cell < cells - col_count, below, 0.0)
    )
    column = iota((out_chans, cells), 1) % col_count
    left = pltpu.roll(rows[:out_chans], 1, axis=1)
    right = pltpu.roll(rows[2 * out_chans :], cells - 1, axis=1)
    return (
        rows[out_chans : 2 * out_chans]
        + jnp.where(column != 0, left, 0.0)
        + jnp.where(column != col_count - 1, right, 0.0)
    )


def leaky(value):
    return jnp.where(value >= 0, value, SLOPE * value)


def send_kernel(
    features_hbm, weight_hbm, slices_ref, up_ref, down_ref, features_ref, weight_ref, sems
):
    loads = [
        pltpu.make_async_copy(features_hbm, features_ref, sems.at[0]),
        pltpu.make_async_copy(weight_hbm, weight_ref, sems.at[1]),
    ]
    for load in loads:
        load.start()
    chans = features_ref.shape[0]
    loads[0].wait()
    pairs = features_ref[...].reshape(2 * chans, CELLS)
    for j in range(2):
        pick = (iota((chans, 2 * chans), 1) == 2 * iota((chans, 2 * chans), 0) + j).astype(
            jnp.bfloat16
        )
        slices_ref[j] = dot(pick, pairs).astype(jnp.bfloat16)
    block = weight_ref.shape[0] // 3
    out_chans = block // 9
    lower, upper = slices_ref[0], slices_ref[1]
    loads[1].wait()
    tap0, tap1, tap2 = (weight_ref[k * block : (k + 1) * block] for k in range(3))
    up_ref[0] = shift_add(dot(tap0, lower) + dot(tap1, upper), out_chans, ROWS, COLS)
    up_ref[1] = shift_add(dot(tap0, upper), out_chans, ROWS, COLS)
    at_start = lax.axis_index("space") == 0
    down_ref[...] = jnp.where(at_start, 0.0, shift_add(dot(tap2, lower), out_chans, ROWS, COLS))


def own_kernel(slices_ref, weight_ref, third_ref, own_ref, select_ref, stacked_ref):
    block = weight_ref.shape[0] // 3
    out_chans = block // 9
    lower, upper = slices_ref[0], slices_ref[1]
    tap1, tap2 = weight_ref[block : 2 * block], weight_ref[2 * block :]
    own_ref[...] = shift_add(dot(tap1, lower) + dot(tap2, upper), out_chans, ROWS, COLS)

    place = iota((HALF_CELLS, CELLS), 0)
    cell = iota((HALF_CELLS, CELLS), 1)
    row, column = cell // COLS, cell % COLS
    row_gap = row - 2 * (place // HALF_COLS)
    column_gap = column - 2 * (place % HALF_COLS)
    for tap in range(9):
        hit = (row_gap == tap // 3 - 1) & (column_gap == tap % 3 - 1)
        select_ref[tap * HALF_CELLS : (tap + 1) * HALF_CELLS] = hit.astype(jnp.bfloat16)

    third_out, third_in = third_ref.shape[1:]
    stacked_ref[...] = jnp.zeros_like(stacked_ref)
    wide = stacked_ref.shape[2] // 3
    for depth in range(3):
        for tap in range(9):
            stacked_ref[tap, :third_out, depth * wide : depth * wide + third_in] = third_ref[
                depth * 9 + tap
            ]


def total_kernel(up_ref, down_ref, own_ref, got_ref, back_ref, first_ref, copies_ref):
    at_start = lax.axis_index("space") == 0
    first0 = got_ref[0] + down_ref[...]
    first1 = own_ref[...] + jnp.where(at_start, 0.0, got_ref[1])
    first_ref[0] = first0
    first_ref[1] = first1
    first_ref[2] = up_ref[0] + back_ref[...]
    cells = 2 * CELLS
    mean = (
        jnp.sum(first0, axis=1, keepdims=True) + jnp.sum(first1, axis=1, keepdims=True)
    ) / cells
    spread = (
        jnp.sum((first0 - mean) ** 2, axis=1, keepdims=True)
        + jnp.sum((first1 - mean) ** 2, axis=1, keepdims=True)
    ) / cells
    row = to_row(mean, 0) + to_row(spread, mean.shape[0])
    copies_ref[...] = jnp.broadcast_to(row, copies_ref.shape)


def column_statistics(rows, n):
    average = jnp.mean(rows, axis=0, keepdims=True)
    apart = jnp.mean((rows - average) ** 2, axis=0, keepdims=True)
    mean = to_column(average, 0, n)
    spread = to_column(average, n, n) + to_column(apart, 0, n)
    return mean, spread


def down_kernel(
    rows_ref, first_ref, gain_ref, bias_ref, select_ref, weight_ref, parts_ref
):
    n = first_ref.shape[1]
    mean, spread = column_statistics(rows_ref[...], n)
    gain = to_column(gain_ref[...], 0, n)
    bias = to_column(bias_ref[...], 0, n)
    scale = gain * lax.rsqrt(spread + EPSILON)
    at_start = lax.axis_index("space") == 0
    levels = [leaky(scale * (first_ref[k] - mean) + bias) for k in range(3)]
    levels[0] = jnp.where(at_start, 0.0, levels[0])
    levels.append(jnp.zeros((LANES - 3 * n, CELLS), jnp.float32))
    layers = jnp.concatenate(levels, axis=0).astype(jnp.bfloat16)
    out_chans = weight_ref.shape[1]
    picked = dot_nt(select_ref[...], layers).astype(jnp.bfloat16)
    windows, weights = [], []
    for tap in range(9):
        windows.append(picked[tap * HALF_CELLS : (tap + 1) * HALF_CELLS])
        for depth in range(3):
            at = (depth * 9 + tap) * n
            weights.append(weight_ref[at : at + n])
        weights.append(jnp.zeros((LANES - 3 * n, out_chans), jnp.bfloat16))
    parts = dot(jnp.concatenate(windows, axis=1), jnp.concatenate(weights, axis=0))
    spare = -out_chans % LANES
    parts = jnp.concatenate([parts, jnp.zeros((HALF_CELLS, spare), jnp.float32)], axis=1).T
    share = parts_ref.shape[1]
    for c in range(parts_ref.shape[0]):
        parts_ref[c] = parts[c * share : (c + 1) * share].astype(jnp.bfloat16)


def own_statistics(value):
    cells = value.shape[1]
    mean = jnp.sum(value, axis=1, keepdims=True) / cells
    spread = jnp.sum((value - mean) ** 2, axis=1, keepdims=True) / cells
    return to_row(mean, 0) + to_row(spread, value.shape[0])


def reduced_kernel(parts_ref, reduced_ref, copies_ref):
    total = parts_ref[0].astype(jnp.float32)
    for c in range(1, parts_ref.shape[0]):
        total = total + parts_ref[c].astype(jnp.float32)
    reduced_ref[...] = total
    copies_ref[...] = jnp.broadcast_to(own_statistics(total), copies_ref.shape)


def bottom_kernel(rows_ref, before_ref, own_ref, after_ref, gain_ref, bias_ref, copies_ref):
    n = own_ref.shape[0]
    mean, spread = column_statistics(rows_ref[...], n)
    gain = to_column(gain_ref[...], 0, n)
    bias = to_column(bias_ref[...], 0, n)
    scale = gain * lax.rsqrt(spread + EPSILON)
    space = lax.axis_index("space")
    keeps = (space != 0, None, space != lax.axis_size("space") - 1)
    for k, (ref, keep) in enumerate(zip((before_ref, own_ref, after_ref), keeps)):
        bottom = leaky(scale * (ref[...] - mean) + bias)
        if keep is not None:
            bottom = jnp.where(keep, bottom, 0.0)
        bottom = bottom.astype(jnp.bfloat16)
        for c in range(copies_ref.shape[0]):
            copies_ref[c, k] = bottom


def third_kernel(bottom_ref, stacked_ref, third_ref, copies_ref):
    chans, depths, share, cells = bottom_ref.shape
    wide = stacked_ref.shape[2] // depths
    blocks = []
    for k in range(depths):
        blocks += [bottom_ref[c, k].astype(jnp.float32) for c in range(chans)]
        blocks.append(jnp.zeros((wide - chans * share, cells), jnp.float32))
    bottom = jnp.concatenate(blocks, axis=0).astype(jnp.bfloat16)
    taps = dot(stacked_ref[...].reshape(9 * PAIR, bottom.shape[0]), bottom)
    third = shift_add(taps, PAIR, HALF_ROWS, HALF_COLS)[: third_ref.shape[0]]
    third_ref[...] = third
    copies_ref[...] = jnp.broadcast_to(own_statistics(third), copies_ref.shape)


def last_kernel(rows_ref, third_ref, gain_ref, bias_ref, out_ref):
    n = third_ref.shape[0]
    mean, spread = column_statistics(rows_ref[...], n)
    gain = to_column(gain_ref[...], 0, n)
    bias = to_column(bias_ref[...], 0, n)
    scale = gain * lax.rsqrt(spread + EPSILON)
    out_ref[...] = leaky(scale * (third_ref[...] - mean) + bias).astype(jnp.bfloat16)


def neighbour(value, by):
    count = lax.axis_size("space")
    return lax.ppermute(value, "space", [(i, (i + by) % count) for i in range(count)])


def exchange(copies, axis):
    return lax.all_to_all(copies, axis, 0, 0, tiled=True)


def struct(shape, dtype=jnp.float32):
    return jax.ShapeDtypeStruct(shape, dtype)


def local(
    features,
    first_weight,
    first_gain,
    first_bias,
    down_weight,
    down_gain,
    down_bias,
    third_weight,
    third_gain,
    third_bias,
):
    spaces, chans = lax.axis_size("space"), lax.axis_size("chan")
    in_chans = features.shape[0]
    n = first_weight.shape[1]
    m = third_weight.shape[1]
    wide = down_weight.shape[1]
    first_weight = first_weight.reshape(27 * n, in_chans)
    down_weight = jnp.transpose(down_weight, (0, 2, 1)).reshape(27 * n, wide)
    gains = [v.reshape(1, -1) for v in (first_gain, down_gain, third_gain)]
    biases = [v.reshape(1, -1) for v in (first_bias, down_bias, third_bias)]
    unit = 2 * 9 * n * in_chans * CELLS

    slices, up, down = kernel_call(
        send_kernel,
        (
            struct((2, in_chans, CELLS), jnp.bfloat16),
            struct((2, n, CELLS)),
            struct((n, CELLS)),
        ),
        (features, first_weight),
        4 * unit,
        "send",
        in_specs=[HBM, HBM],
        scratch=[
            pltpu.VMEM(features.shape, jnp.bfloat16),
            pltpu.VMEM(first_weight.shape, jnp.bfloat16),
            pltpu.SemaphoreType.DMA((2,)),
        ],
    )
    got = neighbour(up, 1)
    back = neighbour(down, -1)
    own, select, stacked = kernel_call(
        own_kernel,
        (
            struct((n, CELLS)),
            struct((9 * HALF_CELLS, CELLS), jnp.bfloat16),
            struct((9, PAIR, 3 * 3 * LANES), jnp.bfloat16),
        ),
        (slices, first_weight, third_weight),
        2 * unit,
        "own",
    )
    first, copies = kernel_call(
        total_kernel,
        (struct((3, n, CELLS)), struct((spaces, LANES))),
        (up, down, own, got, back),
        1 << 20,
        "total",
    )
    rows = exchange(copies, "space")
    parts = kernel_call(
        down_kernel,
        struct((chans, m, HALF_CELLS), jnp.bfloat16),
        (rows, first, gains[0], biases[0], select, down_weight),
        unit,
        "down",
    )
    parts = exchange(parts, "chan")
    reduced, copies = kernel_call(
        reduced_kernel,
        (struct((m, HALF_CELLS)), struct((spaces, LANES))),
        (parts,),
        1 << 20,
        "reduced",
    )
    before, after = neighbour(reduced, 1), neighbour(reduced, -1)
    rows = exchange(copies, "space")
    copies = kernel_call(
        bottom_kernel,
        struct((chans, 3, m, HALF_CELLS), jnp.bfloat16),
        (rows, before, reduced, after, gains[1], biases[1]),
        1 << 20,
        "bottom",
    )
    bottom = exchange(copies, "chan")
    third, copies = kernel_call(
        third_kernel,
        (struct((m, HALF_CELLS)), struct((spaces, LANES))),
        (bottom, stacked),
        unit,
        "third",
    )
    rows = exchange(copies, "space")
    out = kernel_call(
        last_kernel,
        struct((m, HALF_CELLS), jnp.bfloat16),
        (rows, third, gains[2], biases[2]),
        1 << 20,
        "last",
    )
    return out.reshape(m, 1, HALF_CELLS)


def solution(mesh):
    return jax.shard_map(
        local,
        mesh=mesh,
        in_specs=(
            P(None, "space", None),
            P(None, "chan", None),
            P("chan"),
            P("chan"),
            P(None, None, "chan"),
            P("chan"),
            P("chan"),
            P(None, "chan", None),
            P("chan"),
            P("chan"),
        ),
        out_specs=P("chan", "space", None),
        check_vma=False,
    )
```

time: 104 us -> 104 us (level)
  blocking collectives: 60.1 us -> 68.6 us
  starting transfers between devices: 26.8 us -> 22.3 us
  waiting for transfers between devices: 7.16 us -> 3.91 us
  local copies, waits for them, and re-layouts: 4.31 us -> 2.17 us
  Pallas kernels: 5.02 us -> 6.13 us
    all_to_all x3 -> x4, blocking collectives: 60.1 us -> 68.6 us  [exchange(): return lax.all_to_all(copies, axis, 0, 0, tiled=True)]
    all_to_all x1, waiting for transfers between devices: 5.12 us -> 0.45 us  [exchange(): return lax.all_to_all(copies, axis, 0, 0, tiled=True)]
    ppermute x4, starting transfers between devices: 20.1 us -> 16.3 us  [neighbour(): lax.ppermute(value, 'space', [(i, (i + by) % count) for i in range(count)])]
    ppermute x4, waiting for transfers between devices: 2.03 us -> 3.47 us  [neighbour(): lax.ppermute(value, 'space', [(i, (i + by) % count) for i in range(count)])]
    unnamed x21 -> x20, local copies, waits for them, and re-layouts: 3.48 us -> 2.17 us
    pallas_call x7 -> x8, Pallas kernels: 5.02 us -> 6.13 us  [kernel_call(): pl.pallas_call(body, out_shape=outputs, in_specs=in_specs or [VMEM] * len...]
where the time goes in v3:
time: 104 us; the launch traced here: 103 us
  blocking collectives  68.6 us (66%)
  starting transfers between devices  22.3 us (21%)
  Pallas kernels  6.13 us (6%)
  waiting for transfers between devices  3.91 us (4%)
  local copies, waits for them, and re-layouts  2.17 us (2%)
    all_to_all x4, blocking collectives, exchange(): return lax.all_to_all(copies, axis, 0, 0, tiled=True)  68.6 us
    ppermute x4, starting transfers between devices, neighbour(): lax.ppermute(value, 'space', [(i, (i + by) % count) for i in range(count)])  16.3 us
    pallas_call x8, Pallas kernels, kernel_call(): pl.pallas_call(body, out_shape=outputs, in_specs=in_specs or [VMEM] * len...  6.13 us
    all_to_all x1, starting transfers between devices, exchange(): return lax.all_to_all(copies, axis, 0, 0, tiled=True)  5.96 us
    ppermute x4, waiting for transfers between devices, neighbour(): lax.ppermute(value, 'space', [(i, (i + by) % count) for i in range(count)])  3.47 us
    unnamed x20, local copies, waits for them, and re-layouts  2.17 us
  transfers between devices with their start and end apart: 5, of which 2 were waited for; matrix products, arithmetic and copies ran while one was open for 0% of the time, Pallas kernels for 1%

profile of v3, /device:TPU:1, one launch (start us, length us, event | category | flops | bytes accessed | tf_op | source)
XLA Modules:
  0.0 103.2 jit_solution(2456751306853396489)
XLA Ops:
  0.0 0.0 copy-start
  0.0 0.0 copy-start.2
  0.0 1.1 %copy-done.2 = bf16[27,32,256]{2,1,0:T(8,128)(2,1)S(1)} copy-done((bf16[27,32,256]{2,1,0:T(8,128)(2,1)S(1)}, bf16[27,32,256]{2,1,0:T(8,128)(2,1)}, u32[]{:S(2)}) %copy-start.2) | copy-done | bytes 442392
  1.1 0.0 copy-start.9
  1.1 1.0 %copy-done.9 = bf16[256,2,512]{2,1,0:T(2,128)(2,1)S(1)} copy-done((bf16[256,2,512]{2,1,0:T(2,128)(2,1)S(1)}, bf16[256,2,512]{2,1,0:T(2,128)(2,1)}, u32[]{:S(2)}) %copy-start.9) | copy-done | bytes 524312
  2.1 1.5 %send.1 = (bf16[2,256,512]{2,1,0:T(8,128)(2,1)S(1)}, f32[2,32,512]{2,1,0:T(8,128)S(1)}, f32[32,512]{1,0:T(8,128)S(1)}) custom-call(bf16[256,2,512]{2,1,0:T(2,128)(2,1)S(1)} %copy-done.9, bf16[864,256]{1,0:T(8,128)(2,1)S(1)} %bitcast.24), custom_call_target="tpu_custom_call" | custom-call | flops 301989888 | bytes 2097152 | tf_op jit(solution)/shard_map/send/pallas_call | solution.py:24
  3.7 0.0 copy-start.1
  3.7 0.0 copy-start.7
  3.7 0.0 copy-start.8
  3.7 5.5 %collective-permute-start = (f32[2,32,512]{2,1,0:T(8,128)S(1)}, f32[2,32,512]{2,1,0:T(8,128)S(1)}, u32[]{:S(2)}, u32[]{:S(2)}) collective-permute-start(f32[2,32,512]{2,1,0:T(8,128)S(1)} %get-tuple-element.17.up_ref), channel_id=1, source_target_pairs={{0,8},{8,16},{16,24},{24,32},{32,40},{40,48},{48,56},{56,64},{64,7... | collective-permute-start | bytes 393224 | tf_op jit(solution)/shard_map/ppermute | solution.py:253
  9.2 5.3 %collective-permute-start.1 = (f32[32,512]{1,0:T(8,128)S(1)}, f32[32,512]{1,0:T(8,128)S(1)}, u32[]{:S(2)}, u32[]{:S(2)}) collective-permute-start(f32[32,512]{1,0:T(8,128)S(1)} %get-tuple-element.18.down_ref), channel_id=1, source_target_pairs={{0,504},{8,0},{16,8},{24,16},{32,24},{40,32},{48,40},{56,48},{64,5... | collective-permute-start | bytes 196616 | tf_op jit(solution)/shard_map/ppermute | solution.py:253
  14.5 0.0 copy-done
  14.6 0.9 own.1
  15.5 0.0 collective-permute-done.1.back_ref
  15.5 0.0 collective-permute-done.got_ref
  15.5 0.2 total.1
  15.7 22.2 %all_to_all.43 = f32[64,1,128]{2,1,0:T(1,128)S(1)} all-to-all(f32[64,1,128]{2,1,0:T(1,128)S(1)} %bitcast.29), channel_id=1, replica_groups=mesh['space'=64,'chan'=8] {'space'}, dimensions={0} | all-to-all | bytes 65536 | tf_op jit(solution)/shard_map/all_to_all | solution.py:257
  38.0 0.0 copy-done.1
  38.0 0.0 copy-done.7
  38.0 0.0 copy-done.8
  38.0 0.0 copy-start.3
  38.0 0.0 copy-start.4
  38.0 1.1 %down.1 = bf16[8,40,128]{2,1,0:T(8,128)(2,1)S(1)} custom-call(f32[64,128]{1,0:T(8,128)S(1)} %bitcast.26, f32[3,32,512]{2,1,0:T(8,128)S(1)} %get-tuple-element.22.first_ref, f32[1,32]{1,0:T(1,128)S(1)} %bitcast.35, f32[1,32]{1,0:T(1,128)S(1)} %bitcast.36, bf16[1152,512]{1,0:T(8,128)(2,1)S(1)} %get-tuple-element.23.select_ref, bf16[864,320]{1,0:T(8,128)(2,1)S(1)} %bitcast.23), custom_call_target="tpu_custom_call" | custom-call | flops 75497472 | bytes 2097152 | tf_op jit(solution)/shard_map/down/pallas_call | solution.py:24
  39.1 14.1 %all_to_all.44.parts_ref = bf16[8,40,128]{2,1,0:T(8,128)(2,1)S(1)} all-to-all(bf16[8,40,128]{2,1,0:T(8,128)(2,1)S(1)} %down.1), channel_id=1, replica_groups=mesh['space'=64,'chan'=8] {'chan'}, dimensions={0} | all-to-all | bytes 163840 | tf_op jit(solution)/shard_map/all_to_all | solution.py:257
  53.2 0.0 copy-start.5
  53.2 0.0 copy-start.6
  53.2 0.8 reduced.1
  54.0 6.0 %all-to-all-start.2 = ((f32[64,1,128]{2,1,0:T(1,128)}), f32[64,1,128]{2,1,0:T(1,128)S(1)}, u32[]{:S(2)}, u32[]{:S(2)}) async-start(f32[64,1,128]{2,1,0:T(1,128)} %bitcast.9), calls=%async_computation.2 | async-start | bytes 65536 | tf_op jit(solution)/shard_map/all_to_all | solution.py:257
  60.0 3.5 %collective-permute-start.2 = (f32[40,128]{1,0:T(8,128)S(1)}, f32[40,128]{1,0:T(8,128)S(1)}, u32[]{:S(2)}, u32[]{:S(2)}) collective-permute-start(f32[40,128]{1,0:T(8,128)S(1)} %get-tuple-element.25.own_ref), channel_id=1, source_target_pairs={{0,8},{8,16},{16,24},{24,32},{32,40},{40,48},{48,56},{56,64},{64,7... | collective-permute-start | bytes 61448 | tf_op jit(solution)/shard_map/ppermute | solution.py:253
  63.5 1.9 %collective-permute-start.3 = (f32[40,128]{1,0:T(8,128)S(1)}, f32[40,128]{1,0:T(8,128)S(1)}, u32[]{:S(2)}, u32[]{:S(2)}) collective-permute-start(f32[40,128]{1,0:T(8,128)S(1)} %get-tuple-element.25.own_ref), channel_id=1, source_target_pairs={{0,504},{8,0},{16,8},{24,16},{32,24},{40,32},{48,40},{56,48},{64,5... | collective-permute-start | bytes 61448 | tf_op jit(solution)/shard_map/ppermute | solution.py:253
  65.4 0.0 collective-permute-done.2.before_ref
  65.5 3.5 %collective-permute-done.3.after_ref = f32[40,128]{1,0:T(8,128)S(1)} collective-permute-done((f32[40,128]{1,0:T(8,128)S(1)}, f32[40,128]{1,0:T(8,128)S(1)}, u32[]{:S(2)}, u32[]{:S(2)}) %collective-permute-start.3) | collective-permute-done | bytes 20512 | tf_op jit(solution)/shard_map/ppermute | solution.py:253
  68.9 0.4 all-to-all-done.2
  69.4 0.0 copy-done.3
  69.4 0.0 copy-done.4
  69.4 0.1 bottom.1
  69.5 12.0 %all_to_all.45.bottom_ref = bf16[8,3,40,128]{3,2,1,0:T(8,128)(2,1)S(1)} all-to-all(bf16[8,3,40,128]{3,2,1,0:T(8,128)(2,1)S(1)} %bottom.1), channel_id=1, replica_groups=mesh['space'=64,'chan'=8] {'chan'}, dimensions={0} | all-to-all | bytes 491520 | tf_op jit(solution)/shard_map/all_to_all | solution.py:257
  81.5 0.8 third.1
  82.2 20.2 %all_to_all.46 = f32[64,1,128]{2,1,0:T(1,128)S(1)} all-to-all(f32[64,1,128]{2,1,0:T(1,128)S(1)} %bitcast.30), channel_id=1, replica_groups=mesh['space'=64,'chan'=8] {'space'}, dimensions={0} | all-to-all | bytes 65536 | tf_op jit(solution)/shard_map/all_to_all | solution.py:257
  102.5 0.0 copy-done.5
  102.5 0.0 copy-done.6
  102.5 0.7 last.1
Async XLA Ops:
  0.0 14.5 %copy-start = (bf16[27,40,320]{2,1,0:T(8,128)(2,1)S(1)}, bf16[27,40,320]{2,1,0:T(8,128)(2,1)}, u32[]{:S(2)}) copy-start(bf16[27,40,320]{2,1,0:T(8,128)(2,1)} %third_ref.1) | copy-start | bytes 2073604
  0.0 1.1 %copy-start.2 = (bf16[27,32,256]{2,1,0:T(8,128)(2,1)S(1)}, bf16[27,32,256]{2,1,0:T(8,128)(2,1)}, u32[]{:S(2)}) copy-start(bf16[27,32,256]{2,1,0:T(8,128)(2,1)} %param.11) | copy-start | bytes 1327108
  1.1 1.0 %copy-start.9 = (bf16[256,2,512]{2,1,0:T(2,128)(2,1)S(1)}, bf16[256,2,512]{2,1,0:T(2,128)(2,1)}, u32[]{:S(2)}) copy-start(bf16[256,2,512]{2,1,0:T(2,128)(2,1)} %features_hbm.1) | copy-start | bytes 1572868
  3.7 34.3 %copy-start.1 = (bf16[27,320,32]{1,2,0:T(8,128)(2,1)S(1)}, bf16[27,320,32]{1,2,0:T(8,128)(2,1)}, u32[]{:S(2)}) copy-start(bf16[27,320,32]{1,2,0:T(8,128)(2,1)} %param.14) | copy-start | bytes 1658884
  3.7 34.3 %copy-start.7 = (f32[32]{0:T(128)S(1)}, f32[32]{0:T(128)}, u32[]{:S(2)}) copy-start(f32[32]{0:T(128)} %param.12) | copy-start | bytes 388
  3.7 34.3 %copy-start.8 = (f32[32]{0:T(128)S(1)}, f32[32]{0:T(128)}, u32[]{:S(2)}) copy-start(f32[32]{0:T(128)} %param.13) | copy-start | bytes 388
  3.7 11.8 %collective-permute-start = (f32[2,32,512]{2,1,0:T(8,128)S(1)}, f32[2,32,512]{2,1,0:T(8,128)S(1)}, u32[]{:S(2)}, u32[]{:S(2)}) collective-permute-start(f32[2,32,512]{2,1,0:T(8,128)S(1)} %get-tuple-element.17.up_ref), channel_id=1, source_target_pairs={{0,8},{8,16},{16,24},{24,32},{32,40},{40,48},{48,56},{56,64},{64,7... | collective-permute-start | bytes 393224 | tf_op jit(solution)/shard_map/ppermute | solution.py:253
  9.2 6.3 %collective-permute-start.1 = (f32[32,512]{1,0:T(8,128)S(1)}, f32[32,512]{1,0:T(8,128)S(1)}, u32[]{:S(2)}, u32[]{:S(2)}) collective-permute-start(f32[32,512]{1,0:T(8,128)S(1)} %get-tuple-element.18.down_ref), channel_id=1, source_target_pairs={{0,504},{8,0},{16,8},{24,16},{32,24},{40,32},{48,40},{56,48},{64,5... | collective-permute-start | bytes 196616 | tf_op jit(solution)/shard_map/ppermute | solution.py:253
  38.0 31.4 %copy-start.3 = (f32[40]{0:T(128)S(1)}, f32[40]{0:T(128)}, u32[]{:S(2)}) copy-start(f32[40]{0:T(128)} %param.15) | copy-start | bytes 484
  38.0 31.4 %copy-start.4 = (f32[40]{0:T(128)S(1)}, f32[40]{0:T(128)}, u32[]{:S(2)}) copy-start(f32[40]{0:T(128)} %param.16) | copy-start | bytes 484
  53.2 49.3 %copy-start.5 = (f32[40]{0:T(128)S(1)}, f32[40]{0:T(128)}, u32[]{:S(2)}) copy-start(f32[40]{0:T(128)} %param.18) | copy-start | bytes 484
  53.2 49.3 %copy-start.6 = (f32[40]{0:T(128)S(1)}, f32[40]{0:T(128)}, u32[]{:S(2)}) copy-start(f32[40]{0:T(128)} %param.19) | copy-start | bytes 484
  54.0 15.4 %all-to-all-start.2 = ((f32[64,1,128]{2,1,0:T(1,128)}), f32[64,1,128]{2,1,0:T(1,128)S(1)}, u32[]{:S(2)}, u32[]{:S(2)}) async-start(f32[64,1,128]{2,1,0:T(1,128)} %bitcast.9), calls=%async_computation.2 | async-start | bytes 65536 | tf_op jit(solution)/shard_map/all_to_all | solution.py:257
  60.0 5.5 %collective-permute-start.2 = (f32[40,128]{1,0:T(8,128)S(1)}, f32[40,128]{1,0:T(8,128)S(1)}, u32[]{:S(2)}, u32[]{:S(2)}) collective-permute-start(f32[40,128]{1,0:T(8,128)S(1)} %get-tuple-element.25.own_ref), channel_id=1, source_target_pairs={{0,8},{8,16},{16,24},{24,32},{32,40},{40,48},{48,56},{56,64},{64,7... | collective-permute-start | bytes 61448 | tf_op jit(solution)/shard_map/ppermute | solution.py:253
  63.5 5.4 %collective-permute-start.3 = (f32[40,128]{1,0:T(8,128)S(1)}, f32[40,128]{1,0:T(8,128)S(1)}, u32[]{:S(2)}, u32[]{:S(2)}) collective-permute-start(f32[40,128]{1,0:T(8,128)S(1)} %get-tuple-element.25.own_ref), channel_id=1, source_target_pairs={{0,504},{8,0},{16,8},{24,16},{32,24},{40,32},{48,40},{56,48},{64,5... | collective-permute-start | bytes 61448 | tf_op jit(solution)/shard_map/ppermute | solution.py:253

commit v4 on v3

--- a/solution.py
+++ b/solution.py
@@ -83,7 +83,7 @@
 
 
 def send_kernel(
-    features_hbm, weight_hbm, slices_ref, up_ref, down_ref, features_ref, weight_ref, sems
+    features_hbm, weight_hbm, slices_ref, cross_ref, pair_ref, features_ref, weight_ref, sems
 ):
     loads = [
         pltpu.make_async_copy(features_hbm, features_ref, sems.at[0]),
@@ -104,10 +104,14 @@
     lower, upper = slices_ref[0], slices_ref[1]
     loads[1].wait()
     tap0, tap1, tap2 = (weight_ref[k * block : (k + 1) * block] for k in range(3))
-    up_ref[0] = shift_add(dot(tap0, lower) + dot(tap1, upper), out_chans, ROWS, COLS)
-    up_ref[1] = shift_add(dot(tap0, upper), out_chans, ROWS, COLS)
-    at_start = lax.axis_index("space") == 0
-    down_ref[...] = jnp.where(at_start, 0.0, shift_add(dot(tap2, lower), out_chans, ROWS, COLS))
+    up0 = shift_add(dot(tap0, lower) + dot(tap1, upper), out_chans, ROWS, COLS)
+    up1 = shift_add(dot(tap0, upper), out_chans, ROWS, COLS)
+    down = jnp.where(slab() == 0, 0.0, shift_add(dot(tap2, lower), out_chans, ROWS, COLS))
+    even = lax.axis_index("core") == 0
+    cross_ref[0] = jnp.where(even, down, up0)
+    cross_ref[1] = up1
+    pair_ref[0] = jnp.where(even, up0, down)
+    pair_ref[1] = up1
 
 
 def own_kernel(slices_ref, weight_ref, third_ref, own_ref, select_ref, stacked_ref):
@@ -136,13 +140,19 @@
             ]
 
 
-def total_kernel(up_ref, down_ref, own_ref, got_ref, back_ref, first_ref, copies_ref):
-    at_start = lax.axis_index("space") == 0
-    first0 = got_ref[0] + down_ref[...]
-    first1 = own_ref[...] + jnp.where(at_start, 0.0, got_ref[1])
+def total_kernel(cross_ref, pair_ref, own_ref, got_cross_ref, got_pair_ref, first_ref, copies_ref):
+    even = lax.axis_index("core") == 0
+
+    def choose(if_even, if_odd):
+        return jnp.where(even, if_even, if_odd)
+
+    first0 = choose(cross_ref[0], pair_ref[0]) + choose(got_cross_ref[0], got_pair_ref[0])
+    first1 = own_ref[...] + jnp.where(
+        slab() == 0, 0.0, choose(got_cross_ref[1], got_pair_ref[1])
+    )
     first_ref[0] = first0
     first_ref[1] = first1
-    first_ref[2] = up_ref[0] + back_ref[...]
+    first_ref[2] = choose(pair_ref[0], cross_ref[0]) + choose(got_pair_ref[0], got_cross_ref[0])
     cells = 2 * CELLS
     mean = (
         jnp.sum(first0, axis=1, keepdims=True) + jnp.sum(first1, axis=1, keepdims=True)
@@ -171,9 +181,8 @@
     gain = to_column(gain_ref[...], 0, n)
     bias = to_column(bias_ref[...], 0, n)
     scale = gain * lax.rsqrt(spread + EPSILON)
-    at_start = lax.axis_index("space") == 0
     levels = [leaky(scale * (first_ref[k] - mean) + bias) for k in range(3)]
-    levels[0] = jnp.where(at_start, 0.0, levels[0])
+    levels[0] = jnp.where(slab() == 0, 0.0, levels[0])
     levels.append(jnp.zeros((LANES - 3 * n, CELLS), jnp.float32))
     layers = jnp.concatenate(levels, axis=0).astype(jnp.bfloat16)
     out_chans = weight_ref.shape[1]
@@ -189,8 +198,11 @@
     spare = -out_chans % LANES
     parts = jnp.concatenate([parts, jnp.zeros((HALF_CELLS, spare), jnp.float32)], axis=1).T
     share = parts_ref.shape[1]
-    for c in range(parts_ref.shape[0]):
-        parts_ref[c] = parts[c * share : (c + 1) * share].astype(jnp.bfloat16)
+    chans = out_chans // share
+    for c in range(chans):
+        part = parts[c * share : (c + 1) * share].astype(jnp.bfloat16)
+        for core in range(2):
+            parts_ref[core * chans + c] = part
 
 
 def own_statistics(value):
@@ -200,24 +212,37 @@
     return to_row(mean, 0) + to_row(spread, value.shape[0])
 
 
-def reduced_kernel(parts_ref, reduced_ref, copies_ref):
-    total = parts_ref[0].astype(jnp.float32)
-    for c in range(1, parts_ref.shape[0]):
-        total = total + parts_ref[c].astype(jnp.float32)
-    reduced_ref[...] = total
-    copies_ref[...] = jnp.broadcast_to(own_statistics(total), copies_ref.shape)
-
-
-def bottom_kernel(rows_ref, before_ref, own_ref, after_ref, gain_ref, bias_ref, copies_ref):
-    n = own_ref.shape[0]
+def reduced_kernel(parts_ref, reduced_ref, mine_ref, copies_ref):
+    chans = parts_ref.shape[0] // 2
+    totals = []
+    for core in range(2):
+        total = parts_ref[core * chans].astype(jnp.float32)
+        for c in range(1, chans):
+            total = total + parts_ref[core * chans + c].astype(jnp.float32)
+        reduced_ref[core] = total
+        totals.append(total)
+    mine_ref[...] = jnp.where(lax.axis_index("core") == 0, totals[0], totals[1])
+    row = own_statistics(jnp.concatenate(totals, axis=1))
+    copies_ref[...] = jnp.broadcast_to(row, copies_ref.shape)
+
+
+def bottom_kernel(rows_ref, reduced_ref, got_ref, gain_ref, bias_ref, copies_ref):
+    n = got_ref.shape[0]
     mean, spread = column_statistics(rows_ref[...], n)
     gain = to_column(gain_ref[...], 0, n)
     bias = to_column(bias_ref[...], 0, n)
     scale = gain * lax.rsqrt(spread + EPSILON)
-    space = lax.axis_index("space")
-    keeps = (space != 0, None, space != lax.axis_size("space") - 1)
-    for k, (ref, keep) in enumerate(zip((before_ref, own_ref, after_ref), keeps)):
-        bottom = leaky(scale * (ref[...] - mean) + bias)
+    even = lax.axis_index("core") == 0
+    space = slab()
+    last = 2 * lax.axis_size("chip") - 1
+    got, reduced0, reduced1 = got_ref[...], reduced_ref[0], reduced_ref[1]
+    slices = (
+        (jnp.where(even, got, reduced0), space != 0),
+        (jnp.where(even, reduced0, reduced1), None),
+        (jnp.where(even, reduced1, got), space != last),
+    )
+    for k, (value, keep) in enumerate(slices):
+        bottom = leaky(scale * (value - mean) + bias)
         if keep is not None:
             bottom = jnp.where(keep, bottom, 0.0)
         bottom = bottom.astype(jnp.bfloat16)
@@ -248,13 +273,22 @@
     out_ref[...] = leaky(scale * (third_ref[...] - mean) + bias).astype(jnp.bfloat16)
 
 
-def neighbour(value, by):
-    count = lax.axis_size("space")
-    return lax.ppermute(value, "space", [(i, (i + by) % count) for i in range(count)])
-
-
-def exchange(copies, axis):
-    return lax.all_to_all(copies, axis, 0, 0, tiled=True)
+def slab():
+    return 2 * lax.axis_index("chip") + lax.axis_index("core")
+
+
+def across(value):
+    count = 2 * lax.axis_size("chip")
+    pairs = [(i, (i + 2 * (i % 2) - 1) % count) for i in range(count)]
+    return lax.ppermute(value, ("chip", "core"), pairs)
+
+
+def beside(value):
+    return lax.ppermute(value, "core", [(0, 1), (1, 0)])
+
+
+def exchange(copies, axes):
+    return lax.all_to_all(copies, axes, 0, 0, tiled=True)
 
 
 def struct(shape, dtype=jnp.float32):
@@ -273,7 +307,7 @@
     third_gain,
     third_bias,
 ):
-    spaces, chans = lax.axis_size("space"), lax.axis_size("chan")
+    chips, chans = lax.axis_size("chip"), lax.axis_size("chan")
     in_chans = features.shape[0]
     n = first_weight.shape[1]
     m = third_weight.shape[1]
@@ -284,14 +318,17 @@
     biases = [v.reshape(1, -1) for v in (first_bias, down_bias, third_bias)]
     unit = 2 * 9 * n * in_chans * CELLS
 
-    slices, up, down = kernel_call(
+    slices, cross, pair = kernel_call(
         send_kernel,
         (
             struct((2, in_chans, CELLS), jnp.bfloat16),
             struct((2, n, CELLS)),
-            struct((n, CELLS)),
+            struct((2, n, CELLS)),
         ),
-        (features, first_weight),
+        (
+            pltpu.with_memory_space_constraint(features, pltpu.HBM),
+            pltpu.with_memory_space_constraint(first_weight, pltpu.HBM),
+        ),
         4 * unit,
         "send",
         in_specs=[HBM, HBM],
@@ -301,8 +338,7 @@
             pltpu.SemaphoreType.DMA((2,)),
         ],
     )
-    got = neighbour(up, 1)
-    back = neighbour(down, -1)
+    got_cross, got_pair = across(cross), beside(pair)
     own, select, stacked = kernel_call(
         own_kernel,
         (
@@ -316,45 +352,45 @@
     )
     first, copies = kernel_call(
         total_kernel,
-        (struct((3, n, CELLS)), struct((spaces, LANES))),
-        (up, down, own, got, back),
+        (struct((3, n, CELLS)), struct((2 * chips, LANES))),
+        (cross, pair, own, got_cross, got_pair),
         1 << 20,
         "total",
     )
-    rows = exchange(copies, "space")
+    rows = exchange(copies, ("chip", "core"))
     parts = kernel_call(
         down_kernel,
-        struct((chans, m, HALF_CELLS), jnp.bfloat16),
+        struct((2 * chans, m, HALF_CELLS), jnp.bfloat16),
         (rows, first, gains[0], biases[0], select, down_weight),
         unit,
         "down",
     )
-    parts = exchange(parts, "chan")
-    reduced, copies = kernel_call(
+    parts = exchange(parts, ("core", "chan"))
+    reduced, mine, copies = kernel_call(
         reduced_kernel,
-        (struct((m, HALF_CELLS)), struct((spaces, LANES))),
+        (struct((2, m, HALF_CELLS)), struct((m, HALF_CELLS)), struct((chips, LANES))),
         (parts,),
         1 << 20,
         "reduced",
     )
-    before, after = neighbour(reduced, 1), neighbour(reduced, -1)
-    rows = exchange(copies, "space")
+    got = across(mine)
+    rows = exchange(copies, "chip")
     copies = kernel_call(
         bottom_kernel,
         struct((chans, 3, m, HALF_CELLS), jnp.bfloat16),
-        (rows, before, reduced, after, gains[1], biases[1]),
+        (rows, reduced, got, gains[1], biases[1]),
         1 << 20,
         "bottom",
     )
     bottom = exchange(copies, "chan")
     third, copies = kernel_call(
         third_kernel,
-        (struct((m, HALF_CELLS)), struct((spaces, LANES))),
+        (struct((m, HALF_CELLS)), struct((2 * chips, LANES))),
         (bottom, stacked),
         unit,
         "third",
     )
-    rows = exchange(copies, "space")
+    rows = exchange(copies, ("chip", "core"))
     out = kernel_call(
         last_kernel,
         struct((m, HALF_CELLS), jnp.bfloat16),
@@ -366,11 +402,14 @@
 
 
 def solution(mesh):
+    chans = mesh.shape["chan"]
+    pairs = jax.sharding.Mesh(mesh.devices.reshape(-1, 2, chans), ("chip", "core", "chan"))
+    space = ("chip", "core")
     return jax.shard_map(
         local,
-        mesh=mesh,
+        mesh=pairs,
         in_specs=(
-            P(None, "space", None),
+            P(None, space, None),
             P(None, "chan", None),
             P("chan"),
             P("chan"),
@@ -381,6 +420,6 @@
             P("chan"),
             P("chan"),
         ),
-        out_specs=P("chan", "space", None),
+        out_specs=P("chan", space, None),
         check_vma=False,
     )

time: 104 us -> 98.6 us (0.948)
  blocking collectives: 68.6 us -> 61.6 us
  starting transfers between devices: 22.3 us -> 24 us
  local copies, waits for them, and re-layouts: 2.17 us -> 1.04 us
    all_to_all x4, blocking collectives: 68.6 us -> 61.6 us  [exchange(): return lax.all_to_all(copies, axes, 0, 0, tiled=True)]
    ppermute x4 -> x3, starting transfers between devices: 16.3 us -> 20.2 us  [the longest x1 10.6 us: beside(): return lax.ppermute(value, 'core', [(0, 1), (1, 0)])]
    all_to_all x1, waiting for transfers between devices: 0.45 us -> 2.63 us  [exchange(): return lax.all_to_all(copies, axes, 0, 0, tiled=True)]
    all_to_all x1, starting transfers between devices: 5.96 us -> 3.85 us  [exchange(): return lax.all_to_all(copies, axes, 0, 0, tiled=True)]
    ppermute x4 -> x3, waiting for transfers between devices: 3.47 us -> 1.79 us  [the longest x2 1.79 us: across(): return lax.ppermute(value, ('chip', 'core'), pairs)]
    unnamed x20 -> x18, local copies, waits for them, and re-layouts: 2.17 us -> 1.04 us
  transfers between devices with their start and end apart: 5 -> 4, of which waited for: 2 -> 2; matrix products, arithmetic and copies ran while one was open for 0% -> 0% of each run, Pallas kernels for 1% -> 1%
where the time goes in v4:
time: 98.6 us; the launch traced here: 98.2 us
  blocking collectives  61.6 us (62%)
  starting transfers between devices  24 us (24%)
  Pallas kernels  6.96 us (7%)
  waiting for transfers between devices  4.42 us (4%)
  local copies, waits for them, and re-layouts  1.04 us (1%)
    all_to_all x4, blocking collectives, exchange(): return lax.all_to_all(copies, axes, 0, 0, tiled=True)  61.6 us
    ppermute x1, starting transfers between devices, beside(): return lax.ppermute(value, 'core', [(0, 1), (1, 0)])  10.6 us
    ppermute x2, starting transfers between devices, across(): return lax.ppermute(value, ('chip', 'core'), pairs)  9.59 us
    pallas_call x8, Pallas kernels, kernel_call(): pl.pallas_call(body, out_shape=outputs, in_specs=in_specs or [VMEM] * len...  6.96 us
    all_to_all x1, starting transfers between devices, exchange(): return lax.all_to_all(copies, axes, 0, 0, tiled=True)  3.85 us
    all_to_all x1, waiting for transfers between devices, exchange(): return lax.all_to_all(copies, axes, 0, 0, tiled=True)  2.63 us
  transfers between devices with their start and end apart: 4, of which 2 were waited for; matrix products, arithmetic and copies ran while one was open for 0% of the time, Pallas kernels for 1%

profile of v4, /device:TPU:1, one launch (start us, length us, event | category | flops | bytes accessed | tf_op | source)
XLA Modules:
  0.0 98.2 jit_solution(7563995516998060104)
XLA Ops:
  0.0 0.0 copy-start
  0.0 2.3 %send.1 = (bf16[2,256,512]{2,1,0:T(8,128)(2,1)S(1)}, f32[2,32,512]{2,1,0:T(8,128)S(1)}, f32[2,32,512]{2,1,0:T(8,128)S(1)}) custom-call(bf16[256,2,512]{2,1,0:T(2,128)(2,1)} %features_hbm.1, bf16[864,256]{1,0:T(8,128)(2,1)} %bitcast.24), custom_call_target="tpu_custom_call" | custom-call | flops 301989888 | bytes 2097152 | tf_op jit(solution)/shard_map/send/pallas_call | solution.py:24
  2.4 5.4 %collective-permute-start = (f32[2,32,512]{2,1,0:T(8,128)S(1)}, f32[2,32,512]{2,1,0:T(8,128)S(1)}, u32[]{:S(2)}, u32[]{:S(2)}) collective-permute-start(f32[2,32,512]{2,1,0:T(8,128)S(1)} %get-tuple-element.18.cross_ref), channel_id=1, source_target_pairs={{0,504},{8,16},{16,8},{24,32},{32,24},{40,48},{48,40},{56,64},{64,... | collective-permute-start | bytes 393224 | tf_op jit(solution)/shard_map/ppermute | solution.py:283
  7.8 10.6 %collective-permute-start.1 = (f32[2,32,512]{2,1,0:T(8,128)S(1)}, f32[2,32,512]{2,1,0:T(8,128)S(1)}, u32[]{:S(2)}, u32[]{:S(2)}) collective-permute-start(f32[2,32,512]{2,1,0:T(8,128)S(1)} %get-tuple-element.19.pair_ref), channel_id=1, source_target_pairs={{0,8},{8,0},{1,9},{9,1},{2,10},{10,2},{3,11},{11,3},{4,12},{12,4},... | collective-permute-start | bytes 393224 | tf_op jit(solution)/shard_map/ppermute | solution.py:287
  18.4 0.0 copy-done
  18.4 0.0 copy-start.2
  18.4 1.0 %copy-done.2 = bf16[27,32,256]{2,1,0:T(8,128)(2,1)S(1)} copy-done((bf16[27,32,256]{2,1,0:T(8,128)(2,1)S(1)}, bf16[27,32,256]{2,1,0:T(8,128)(2,1)}, u32[]{:S(2)}) %copy-start.2) | copy-done | bytes 442392
  19.4 0.0 copy-start.1
  19.4 0.0 copy-start.7
  19.4 0.0 copy-start.8
  19.4 0.9 own.1
  20.3 0.0 collective-permute-done.got_cross_ref
  20.4 0.0 collective-permute-done.1.got_pair_ref
  20.4 0.2 total.1
  20.6 14.7 %all_to_all.43 = f32[64,1,128]{2,1,0:T(1,128)S(1)} all-to-all(f32[64,1,128]{2,1,0:T(1,128)S(1)} %bitcast.29), channel_id=1, replica_groups=mesh['chip'=32,'core'=2,'chan'=8] {'chip','core'}, dimensions={0} | all-to-all | bytes 65536 | tf_op jit(solution)/shard_map/all_to_all | solution.py:291
  35.3 0.0 copy-done.1
  35.3 0.0 copy-done.7
  35.3 0.0 copy-done.8
  35.3 0.0 copy-start.3
  35.3 0.0 copy-start.4
  35.3 1.1 %down.1 = bf16[16,40,128]{2,1,0:T(8,128)(2,1)S(1)} custom-call(f32[64,128]{1,0:T(8,128)S(1)} %bitcast.26, f32[3,32,512]{2,1,0:T(8,128)S(1)} %get-tuple-element.23.first_ref, f32[1,32]{1,0:T(1,128)S(1)} %bitcast.35, f32[1,32]{1,0:T(1,128)S(1)} %bitcast.36, bf16[1152,512]{1,0:T(8,128)(2,1)S(1)} %get-tuple-element.24.select_ref, bf16[864,320]{1,0:T(8,128)(2,1)S(1)} %bitcast.23), custom_call_target="tpu_custom_call" | custom-call | flops 75497472 | bytes 2097152 | tf_op jit(solution)/shard_map/down/pallas_call | solution.py:24
  36.4 15.4 %all_to_all.44.parts_ref = bf16[16,40,128]{2,1,0:T(8,128)(2,1)S(1)} all-to-all(bf16[16,40,128]{2,1,0:T(8,128)(2,1)S(1)} %down.1), channel_id=1, replica_groups=mesh['chip'=32,'core'=2,'chan'=8] {'core','chan'}, dimensions={0} | all-to-all | bytes 327680 | tf_op jit(solution)/shard_map/all_to_all | solution.py:291
  51.8 0.0 copy-start.5
  51.8 0.0 copy-start.6
  51.8 0.8 reduced.1
  52.6 3.8 %all-to-all-start.2 = ((f32[32,1,128]{2,1,0:T(1,128)}), f32[32,1,128]{2,1,0:T(1,128)S(1)}, u32[]{:S(2)}, u32[]{:S(2)}) async-start(f32[32,1,128]{2,1,0:T(1,128)} %bitcast.9), calls=%async_computation.2 | async-start | bytes 32768 | tf_op jit(solution)/shard_map/all_to_all | solution.py:291
  56.5 4.2 %collective-permute-start.2 = (f32[40,128]{1,0:T(8,128)S(1)}, f32[40,128]{1,0:T(8,128)S(1)}, u32[]{:S(2)}, u32[]{:S(2)}) collective-permute-start(f32[40,128]{1,0:T(8,128)S(1)} %get-tuple-element.27), channel_id=1, source_target_pairs={{0,504},{8,16},{16,8},{24,32},{32,24},{40,48},{48,40},{56,64},{64,... | collective-permute-start | bytes 61448 | tf_op jit(solution)/shard_map/ppermute | solution.py:283
  60.7 1.8 %collective-permute-done.2.got_ref = f32[40,128]{1,0:T(8,128)S(1)} collective-permute-done((f32[40,128]{1,0:T(8,128)S(1)}, f32[40,128]{1,0:T(8,128)S(1)}, u32[]{:S(2)}, u32[]{:S(2)}) %collective-permute-start.2) | collective-permute-done | bytes 20512 | tf_op jit(solution)/shard_map/ppermute | solution.py:283
  62.4 2.6 %all-to-all-done.2 = f32[32,1,128]{2,1,0:T(1,128)S(1)} async-done(((f32[32,1,128]{2,1,0:T(1,128)}), f32[32,1,128]{2,1,0:T(1,128)S(1)}, u32[]{:S(2)}, u32[]{:S(2)}) %all-to-all-start.2) | async-done | bytes 16416 | tf_op jit(solution)/shard_map/all_to_all | solution.py:291
  65.1 0.0 copy-done.3
  65.1 0.0 copy-done.4
  65.1 0.1 bottom.1
  65.2 12.7 %all_to_all.45.bottom_ref = bf16[8,3,40,128]{3,2,1,0:T(8,128)(2,1)S(1)} all-to-all(bf16[8,3,40,128]{3,2,1,0:T(8,128)(2,1)S(1)} %bottom.1), channel_id=1, replica_groups=mesh['chip'=32,'core'=2,'chan'=8] {'chan'}, dimensions={0} | all-to-all | bytes 491520 | tf_op jit(solution)/shard_map/all_to_all | solution.py:291
  78.0 0.7 third.1
  78.7 18.8 %all_to_all.46 = f32[64,1,128]{2,1,0:T(1,128)S(1)} all-to-all(f32[64,1,128]{2,1,0:T(1,128)S(1)} %bitcast.30), channel_id=1, replica_groups=mesh['chip'=32,'core'=2,'chan'=8] {'chip','core'}, dimensions={0} | all-to-all | bytes 65536 | tf_op jit(solution)/shard_map/all_to_all | solution.py:291
  97.5 0.0 copy-done.5
  97.5 0.0 copy-done.6
  97.5 0.7 last.1
Async XLA Ops:
  0.0 18.4 %copy-start = (bf16[27,40,320]{2,1,0:T(8,128)(2,1)S(1)}, bf16[27,40,320]{2,1,0:T(8,128)(2,1)}, u32[]{:S(2)}) copy-start(bf16[27,40,320]{2,1,0:T(8,128)(2,1)} %third_ref.1) | copy-start | bytes 2073604
  2.4 18.0 %collective-permute-start = (f32[2,32,512]{2,1,0:T(8,128)S(1)}, f32[2,32,512]{2,1,0:T(8,128)S(1)}, u32[]{:S(2)}, u32[]{:S(2)}) collective-permute-start(f32[2,32,512]{2,1,0:T(8,128)S(1)} %get-tuple-element.18.cross_ref), channel_id=1, source_target_pairs={{0,504},{8,16},{16,8},{24,32},{32,24},{40,48},{48,40},{56,64},{64,... | collective-permute-start | bytes 393224 | tf_op jit(solution)/shard_map/ppermute | solution.py:283
  7.8 12.6 %collective-permute-start.1 = (f32[2,32,512]{2,1,0:T(8,128)S(1)}, f32[2,32,512]{2,1,0:T(8,128)S(1)}, u32[]{:S(2)}, u32[]{:S(2)}) collective-permute-start(f32[2,32,512]{2,1,0:T(8,128)S(1)} %get-tuple-element.19.pair_ref), channel_id=1, source_target_pairs={{0,8},{8,0},{1,9},{9,1},{2,10},{10,2},{3,11},{11,3},{4,12},{12,4},... | collective-permute-start | bytes 393224 | tf_op jit(solution)/shard_map/ppermute | solution.py:287
  18.4 1.0 %copy-start.2 = (bf16[27,32,256]{2,1,0:T(8,128)(2,1)S(1)}, bf16[27,32,256]{2,1,0:T(8,128)(2,1)}, u32[]{:S(2)}) copy-start(bf16[27,32,256]{2,1,0:T(8,128)(2,1)} %param.11) | copy-start | bytes 1327108
  19.4 15.9 %copy-start.1 = (bf16[27,320,32]{1,2,0:T(8,128)(2,1)S(1)}, bf16[27,320,32]{1,2,0:T(8,128)(2,1)}, u32[]{:S(2)}) copy-start(bf16[27,320,32]{1,2,0:T(8,128)(2,1)} %param.14) | copy-start | bytes 1658884
  19.4 15.9 %copy-start.7 = (f32[32]{0:T(128)S(1)}, f32[32]{0:T(128)}, u32[]{:S(2)}) copy-start(f32[32]{0:T(128)} %param.12) | copy-start | bytes 388
  19.4 15.9 %copy-start.8 = (f32[32]{0:T(128)S(1)}, f32[32]{0:T(128)}, u32[]{:S(2)}) copy-start(f32[32]{0:T(128)} %param.13) | copy-start | bytes 388
  35.3 29.8 %copy-start.3 = (f32[40]{0:T(128)S(1)}, f32[40]{0:T(128)}, u32[]{:S(2)}) copy-start(f32[40]{0:T(128)} %param.15) | copy-start | bytes 484
  35.3 29.8 %copy-start.4 = (f32[40]{0:T(128)S(1)}, f32[40]{0:T(128)}, u32[]{:S(2)}) copy-start(f32[40]{0:T(128)} %param.16) | copy-start | bytes 484
  51.8 45.7 %copy-start.5 = (f32[40]{0:T(128)S(1)}, f32[40]{0:T(128)}, u32[]{:S(2)}) copy-start(f32[40]{0:T(128)} %param.18) | copy-start | bytes 484
  51.8 45.7 %copy-start.6 = (f32[40]{0:T(128)S(1)}, f32[40]{0:T(128)}, u32[]{:S(2)}) copy-start(f32[40]{0:T(128)} %param.19) | copy-start | bytes 484
  52.6 12.5 %all-to-all-start.2 = ((f32[32,1,128]{2,1,0:T(1,128)}), f32[32,1,128]{2,1,0:T(1,128)S(1)}, u32[]{:S(2)}, u32[]{:S(2)}) async-start(f32[32,1,128]{2,1,0:T(1,128)} %bitcast.9), calls=%async_computation.2 | async-start | bytes 32768 | tf_op jit(solution)/shard_map/all_to_all | solution.py:291
  56.5 6.0 %collective-permute-start.2 = (f32[40,128]{1,0:T(8,128)S(1)}, f32[40,128]{1,0:T(8,128)S(1)}, u32[]{:S(2)}, u32[]{:S(2)}) collective-permute-start(f32[40,128]{1,0:T(8,128)S(1)} %get-tuple-element.27), channel_id=1, source_target_pairs={{0,504},{8,16},{16,8},{24,32},{32,24},{40,48},{48,40},{56,64},{64,... | collective-permute-start | bytes 61448 | tf_op jit(solution)/shard_map/ppermute | solution.py:283

commit v5 on v4

--- a/solution.py
+++ b/solution.py
@@ -13,6 +13,10 @@
 HALF_CELLS = HALF_ROWS * HALF_COLS
 LANES = 128
 PAIR = 48
+FIRST_CHIP = 31
+SECOND_CHIP = 0
+THIRD_CHIP = 20
+FIRST_CHAN = 4
 EPSILON = 1e-05
 SLOPE = 0.01
 
@@ -83,7 +87,9 @@
 
 
 def send_kernel(
-    features_hbm, weight_hbm, slices_ref, cross_ref, pair_ref, features_ref, weight_ref, sems
+    features_hbm, weight_hbm,
+    slices_ref, weight_ref, kept_ref, cross_ref, pair_ref,
+    features_ref, sems,
 ):
     loads = [
         pltpu.make_async_copy(features_hbm, features_ref, sems.at[0]),
@@ -107,10 +113,13 @@
     up0 = shift_add(dot(tap0, lower) + dot(tap1, upper), out_chans, ROWS, COLS)
     up1 = shift_add(dot(tap0, upper), out_chans, ROWS, COLS)
     down = jnp.where(slab() == 0, 0.0, shift_add(dot(tap2, lower), out_chans, ROWS, COLS))
+    kept_ref[0] = up0
+    kept_ref[1] = down
     even = lax.axis_index("core") == 0
-    cross_ref[0] = jnp.where(even, down, up0)
+    up1 = up1.astype(jnp.bfloat16)
+    cross_ref[0] = jnp.where(even, down, up0).astype(jnp.bfloat16)
     cross_ref[1] = up1
-    pair_ref[0] = jnp.where(even, up0, down)
+    pair_ref[0] = jnp.where(even, up0, down).astype(jnp.bfloat16)
     pair_ref[1] = up1
 
 
@@ -140,19 +149,16 @@
             ]
 
 
-def total_kernel(cross_ref, pair_ref, own_ref, got_cross_ref, got_pair_ref, first_ref, copies_ref):
+def total_kernel(kept_ref, own_ref, got_cross_ref, got_pair_ref, first_ref, copies_ref):
     even = lax.axis_index("core") == 0
 
-    def choose(if_even, if_odd):
-        return jnp.where(even, if_even, if_odd)
-
-    first0 = choose(cross_ref[0], pair_ref[0]) + choose(got_cross_ref[0], got_pair_ref[0])
-    first1 = own_ref[...] + jnp.where(
-        slab() == 0, 0.0, choose(got_cross_ref[1], got_pair_ref[1])
-    )
+    cross = got_cross_ref[...].astype(jnp.float32)
+    pair = got_pair_ref[...].astype(jnp.float32)
+    first0 = kept_ref[1] + jnp.where(even, cross[0], pair[0])
+    first1 = own_ref[...] + jnp.where(slab() == 0, 0.0, jnp.where(even, cross[1], pair[1]))
     first_ref[0] = first0
     first_ref[1] = first1
-    first_ref[2] = choose(pair_ref[0], cross_ref[0]) + choose(got_pair_ref[0], got_cross_ref[0])
+    first_ref[2] = kept_ref[0] + jnp.where(even, pair[0], cross[0])
     cells = 2 * CELLS
     mean = (
         jnp.sum(first0, axis=1, keepdims=True) + jnp.sum(first1, axis=1, keepdims=True)
@@ -197,12 +203,13 @@
     parts = dot(jnp.concatenate(windows, axis=1), jnp.concatenate(weights, axis=0))
     spare = -out_chans % LANES
     parts = jnp.concatenate([parts, jnp.zeros((HALF_CELLS, spare), jnp.float32)], axis=1).T
-    share = parts_ref.shape[1]
-    chans = out_chans // share
-    for c in range(chans):
-        part = parts[c * share : (c + 1) * share].astype(jnp.bfloat16)
-        for core in range(2):
-            parts_ref[core * chans + c] = part
+    chans = lax.axis_size("chan")
+    share = out_chans // chans
+    parts = jnp.concatenate(
+        [parts[c * share : (c + 1) * share] for c in turned(chans, FIRST_CHAN)], axis=0
+    ).astype(jnp.bfloat16)
+    for core in range(2):
+        parts_ref[core * out_chans : (core + 1) * out_chans] = parts
 
 
 def own_statistics(value):
@@ -213,14 +220,17 @@
 
 
 def reduced_kernel(parts_ref, reduced_ref, mine_ref, copies_ref):
-    chans = parts_ref.shape[0] // 2
+    share = reduced_ref.shape[1]
+    parts = parts_ref[...].astype(jnp.float32)
+    chans = parts.shape[0] // (2 * share)
     totals = []
     for core in range(2):
-        total = parts_ref[core * chans].astype(jnp.float32)
-        for c in range(1, chans):
-            total = total + parts_ref[core * chans + c].astype(jnp.float32)
-        reduced_ref[core] = total
-        totals.append(total)
+        shares = [
+            parts[(core * chans + c) * share : (core * chans + c + 1) * share]
+            for c in range(chans)
+        ]
+        totals.append(sum(shares[1:], shares[0]))
+        reduced_ref[core] = totals[core]
     mine_ref[...] = jnp.where(lax.axis_index("core") == 0, totals[0], totals[1])
     row = own_statistics(jnp.concatenate(totals, axis=1))
     copies_ref[...] = jnp.broadcast_to(row, copies_ref.shape)
@@ -241,25 +251,31 @@
         (jnp.where(even, reduced0, reduced1), None),
         (jnp.where(even, reduced1, got), space != last),
     )
-    for k, (value, keep) in enumerate(slices):
+    bottoms = []
+    for value, keep in slices:
         bottom = leaky(scale * (value - mean) + bias)
-        if keep is not None:
-            bottom = jnp.where(keep, bottom, 0.0)
-        bottom = bottom.astype(jnp.bfloat16)
-        for c in range(copies_ref.shape[0]):
-            copies_ref[c, k] = bottom
+        bottoms.append(bottom if keep is None else jnp.where(keep, bottom, 0.0))
+    copies = jnp.concatenate(bottoms * 2, axis=0).astype(jnp.bfloat16)
+    size = copies.shape[0]
+    for c in range(copies_ref.shape[0] // size):
+        copies_ref[c * size : (c + 1) * size] = copies
 
 
 def third_kernel(bottom_ref, stacked_ref, third_ref, copies_ref):
-    chans, depths, share, cells = bottom_ref.shape
+    share, cells = third_ref.shape
+    depths = 3
+    chans = bottom_ref.shape[0] // (depths * share)
     wide = stacked_ref.shape[2] // depths
+    gathered = bottom_ref[...].astype(jnp.float32)
     blocks = []
     for k in range(depths):
-        blocks += [bottom_ref[c, k].astype(jnp.float32) for c in range(chans)]
+        for c in turned(chans, chans - FIRST_CHAN):
+            at = (c * depths + k) * share
+            blocks.append(gathered[at : at + share])
         blocks.append(jnp.zeros((wide - chans * share, cells), jnp.float32))
     bottom = jnp.concatenate(blocks, axis=0).astype(jnp.bfloat16)
     taps = dot(stacked_ref[...].reshape(9 * PAIR, bottom.shape[0]), bottom)
-    third = shift_add(taps, PAIR, HALF_ROWS, HALF_COLS)[: third_ref.shape[0]]
+    third = shift_add(taps, PAIR, HALF_ROWS, HALF_COLS)[:share]
     third_ref[...] = third
     copies_ref[...] = jnp.broadcast_to(own_statistics(third), copies_ref.shape)
 
@@ -287,8 +303,12 @@
     return lax.ppermute(value, "core", [(0, 1), (1, 0)])
 
 
-def exchange(copies, axes):
-    return lax.all_to_all(copies, axes, 0, 0, tiled=True)
+def turned(count, first):
+    return [(first + i) % count for i in range(count)]
+
+
+def exchange(copies, axes, order):
+    return lax.all_to_all(copies, axes, 0, 0, axis_index_groups=[order], tiled=True)
 
 
 def struct(shape, dtype=jnp.float32):
@@ -318,12 +338,14 @@
     biases = [v.reshape(1, -1) for v in (first_bias, down_bias, third_bias)]
     unit = 2 * 9 * n * in_chans * CELLS
 
-    slices, cross, pair = kernel_call(
+    slices, weights, kept, cross, pair = kernel_call(
         send_kernel,
         (
             struct((2, in_chans, CELLS), jnp.bfloat16),
+            struct(first_weight.shape, jnp.bfloat16),
             struct((2, n, CELLS)),
-            struct((2, n, CELLS)),
+            struct((2, n, CELLS), jnp.bfloat16),
+            struct((2, n, CELLS), jnp.bfloat16),
         ),
         (
             pltpu.with_memory_space_constraint(features, pltpu.HBM),
@@ -334,7 +356,6 @@
         in_specs=[HBM, HBM],
         scratch=[
             pltpu.VMEM(features.shape, jnp.bfloat16),
-            pltpu.VMEM(first_weight.shape, jnp.bfloat16),
             pltpu.SemaphoreType.DMA((2,)),
         ],
     )
@@ -346,26 +367,30 @@
             struct((9 * HALF_CELLS, CELLS), jnp.bfloat16),
             struct((9, PAIR, 3 * 3 * LANES), jnp.bfloat16),
         ),
-        (slices, first_weight, third_weight),
+        (slices, weights, third_weight),
         2 * unit,
         "own",
     )
     first, copies = kernel_call(
         total_kernel,
         (struct((3, n, CELLS)), struct((2 * chips, LANES))),
-        (cross, pair, own, got_cross, got_pair),
+        (kept, own, got_cross, got_pair),
         1 << 20,
         "total",
     )
-    rows = exchange(copies, ("chip", "core"))
+    rows = exchange(copies, ("chip", "core"), turned(2 * chips, 2 * FIRST_CHIP))
     parts = kernel_call(
         down_kernel,
-        struct((2 * chans, m, HALF_CELLS), jnp.bfloat16),
+        struct((2 * chans * m, HALF_CELLS), jnp.bfloat16),
         (rows, first, gains[0], biases[0], select, down_weight),
         unit,
         "down",
     )
-    parts = exchange(parts, ("core", "chan"))
+    parts = exchange(
+        parts,
+        ("core", "chan"),
+        [core * chans + c for core in range(2) for c in turned(chans, FIRST_CHAN)],
+    )
     reduced, mine, copies = kernel_call(
         reduced_kernel,
         (struct((2, m, HALF_CELLS)), struct((m, HALF_CELLS)), struct((chips, LANES))),
@@ -374,15 +399,15 @@
         "reduced",
     )
     got = across(mine)
-    rows = exchange(copies, "chip")
+    rows = exchange(copies, "chip", turned(chips, SECOND_CHIP))
     copies = kernel_call(
         bottom_kernel,
-        struct((chans, 3, m, HALF_CELLS), jnp.bfloat16),
+        struct((chans * 3 * m, HALF_CELLS), jnp.bfloat16),
         (rows, reduced, got, gains[1], biases[1]),
         1 << 20,
         "bottom",
     )
-    bottom = exchange(copies, "chan")
+    bottom = exchange(copies, "chan", turned(chans, FIRST_CHAN))
     third, copies = kernel_call(
         third_kernel,
         (struct((m, HALF_CELLS)), struct((2 * chips, LANES))),
@@ -390,7 +415,7 @@
         unit,
         "third",
     )
-    rows = exchange(copies, ("chip", "core"))
+    rows = exchange(copies, ("chip", "core"), turned(2 * chips, 2 * THIRD_CHIP))
     out = kernel_call(
         last_kernel,
         struct((m, HALF_CELLS), jnp.bfloat16),

time: 98.6 us -> 89.6 us (0.909)
  blocking collectives: 61.6 us -> 51.8 us
  starting transfers between devices: 24 us -> 25.9 us
  local copies, waits for them, and re-layouts: 1.04 us -> 0.04 us
    all_to_all x4, blocking collectives: 61.6 us -> 51.8 us  [exchange(): lax.all_to_all(copies, axes, 0, 0, axis_index_groups=[order], tiled=True)]
    all_to_all x1, starting transfers between devices: 3.85 us -> 5.5 us  [exchange(): lax.all_to_all(copies, axes, 0, 0, axis_index_groups=[order], tiled=True)]
    unnamed x18 -> x16, local copies, waits for them, and re-layouts: 1.04 us -> 0.04 us
where the time goes in v5:
time: 89.6 us; the launch traced here: 89.2 us
  blocking collectives  51.8 us (58%)
  starting transfers between devices  25.9 us (29%)
  Pallas kernels  6.98 us (8%)
  waiting for transfers between devices  4.36 us (5%)
    all_to_all x4, blocking collectives, exchange(): lax.all_to_all(copies, axes, 0, 0, axis_index_groups=[order], tiled=True)  51.8 us
    ppermute x1, starting transfers between devices, beside(): return lax.ppermute(value, 'core', [(0, 1), (1, 0)])  10.6 us
    ppermute x2, starting transfers between devices, across(): return lax.ppermute(value, ('chip', 'core'), pairs)  9.79 us
    pallas_call x8, Pallas kernels, kernel_call(): pl.pallas_call(body, out_shape=outputs, in_specs=in_specs or [VMEM] * len...  6.98 us
    all_to_all x1, starting transfers between devices, exchange(): lax.all_to_all(copies, axes, 0, 0, axis_index_groups=[order], tiled=True)  5.5 us
    all_to_all x1, waiting for transfers between devices, exchange(): lax.all_to_all(copies, axes, 0, 0, axis_index_groups=[order], tiled=True)  2.57 us
  transfers between devices with their start and end apart: 4, of which 2 were waited for; matrix products, arithmetic and copies ran while one was open for 0% of the time, Pallas kernels for 1%

profile of v5, /device:TPU:1, one launch (start us, length us, event | category | flops | bytes accessed | tf_op | source)
XLA Modules:
  0.0 89.2 jit_solution(10109221084387856197)
XLA Ops:
  0.0 0.0 copy-start
  0.0 2.4 %send.1 = (bf16[2,256,512]{2,1,0:T(8,128)(2,1)S(1)}, bf16[864,256]{1,0:T(8,128)(2,1)S(1)}, f32[2,32,512]{2,1,0:T(8,128)S(1)}, bf16[2,32,512]{2,1,0:T(8,128)(2,1)S(1)}, bf16[2,32,512]{2,1,0:T(8,128)(2,1)S(1)}) custom-call(bf16[256,2,512]{2,1,0:T(2,128)(2,1)} %features_hbm.1, bf16[864,256]{1,0:T(8,128)(2,1)} %bitcast.43), custom_call_target="tpu_custom_call" | custom-call | flops 301989888 | bytes 2097152 | tf_op jit(solution)/shard_map/send/pallas_call | solution.py:28
  2.4 0.0 copy-start.1
  2.4 0.0 copy-start.6
  2.4 0.0 copy-start.7
  2.4 5.5 %collective-permute-start = (bf16[2,32,512]{2,1,0:T(8,128)(2,1)S(1)}, bf16[2,32,512]{2,1,0:T(8,128)(2,1)S(1)}, u32[]{:S(2)}, u32[]{:S(2)}) collective-permute-start(bf16[2,32,512]{2,1,0:T(8,128)(2,1)S(1)} %get-tuple-element.24), channel_id=1, source_target_pairs={{0,504},{8,16},{16,8},{24,32},{32,24},{40,48},{48,40},{56,64},{64,... | collective-permute-start | bytes 196616 | tf_op jit(solution)/shard_map/ppermute | solution.py:299
  7.9 10.6 %collective-permute-start.1 = (bf16[2,32,512]{2,1,0:T(8,128)(2,1)S(1)}, bf16[2,32,512]{2,1,0:T(8,128)(2,1)S(1)}, u32[]{:S(2)}, u32[]{:S(2)}) collective-permute-start(bf16[2,32,512]{2,1,0:T(8,128)(2,1)S(1)} %get-tuple-element.25), channel_id=1, source_target_pairs={{0,8},{8,0},{1,9},{9,1},{2,10},{10,2},{3,11},{11,3},{4,12},{12,4},... | collective-permute-start | bytes 196616 | tf_op jit(solution)/shard_map/ppermute | solution.py:303
  18.5 0.0 copy-done
  18.6 0.9 %own.1 = (f32[32,512]{1,0:T(8,128)S(1)}, bf16[1152,512]{1,0:T(8,128)(2,1)S(1)}, bf16[9,48,1152]{2,1,0:T(8,128)(2,1)S(1)}) custom-call(bf16[2,256,512]{2,1,0:T(8,128)(2,1)S(1)} %get-tuple-element.21.slices_ref, bf16[864,256]{1,0:T(8,128)(2,1)S(1)} %get-tuple-element.22.weight_ref, bf16[27,40,320]{2,1,0:T(8,128)(2,1)S(1)} %copy-done), custom_call_target="tpu_custom_call" | custom-call | flops 150994944 | bytes 2097152 | tf_op jit(solution)/shard_map/own/pallas_call | solution.py:28
  19.5 0.0 collective-permute-done.got_cross_ref
  19.5 0.0 collective-permute-done.1.got_pair_ref
  19.5 0.2 total.1
  19.7 12.4 %all_to_all.55 = f32[64,1,128]{2,1,0:T(1,128)S(1)} all-to-all(f32[64,1,128]{2,1,0:T(1,128)S(1)} %bitcast.35), channel_id=1, replica_groups={{496,504,0,8,16,24,32,40,48,56,64,72,80,88,96,104,112,120,128,136,144,1..., dimensions={0} | all-to-all | bytes 65536 | tf_op jit(solution)/shard_map/all_to_all | solution.py:311
  32.1 0.0 copy-done.1
  32.1 0.0 copy-done.6
  32.1 0.0 copy-done.7
  32.1 0.0 copy-start.2
  32.2 0.0 copy-start.3
  32.2 1.1 %down.1 = bf16[640,128]{1,0:T(8,128)(2,1)S(1)} custom-call(f32[64,128]{1,0:T(8,128)S(1)} %bitcast.32, f32[3,32,512]{2,1,0:T(8,128)S(1)} %get-tuple-element.27.first_ref, f32[1,32]{1,0:T(1,128)S(1)} %bitcast.41, f32[1,32]{1,0:T(1,128)S(1)} %bitcast.42, bf16[1152,512]{1,0:T(8,128)(2,1)S(1)} %get-tuple-element.28.select_ref, bf16[864,320]{1,0:T(8,128)(2,1)S(1)} %bitcast.29), custom_call_target="tpu_custom_call" | custom-call | flops 75497472 | bytes 2097152 | tf_op jit(solution)/shard_map/down/pallas_call | solution.py:28
  33.2 13.5 %all_to_all.56 = bf16[16,40,128]{2,1,0:T(8,128)(2,1)S(1)} all-to-all(bf16[16,40,128]{2,1,0:T(8,128)(2,1)S(1)} %bitcast.31), channel_id=1, replica_groups={{4,5,6,7,0,1,2,3,12,13,14,15,8,9,10,11},{20,21,22,23,16,17,18,19,28,29,..., dimensions={0} | all-to-all | bytes 327680 | tf_op jit(solution)/shard_map/all_to_all | solution.py:311
  46.8 0.0 copy-start.4
  46.8 0.0 copy-start.5
  46.8 0.8 reduced.1
  47.6 5.5 %all-to-all-start.2 = ((f32[32,1,128]{2,1,0:T(1,128)}), f32[32,1,128]{2,1,0:T(1,128)S(1)}, u32[]{:S(2)}, u32[]{:S(2)}) async-start(f32[32,1,128]{2,1,0:T(1,128)} %bitcast.11), calls=%async_computation.2 | async-start | bytes 32768 | tf_op jit(solution)/shard_map/all_to_all | solution.py:311
  53.1 4.3 %collective-permute-start.2 = (f32[40,128]{1,0:T(8,128)S(1)}, f32[40,128]{1,0:T(8,128)S(1)}, u32[]{:S(2)}, u32[]{:S(2)}) collective-permute-start(f32[40,128]{1,0:T(8,128)S(1)} %get-tuple-element.31), channel_id=1, source_target_pairs={{0,504},{8,16},{16,8},{24,32},{32,24},{40,48},{48,40},{56,64},{64,... | collective-permute-start | bytes 61448 | tf_op jit(solution)/shard_map/ppermute | solution.py:299
  57.4 1.8 %collective-permute-done.2.got_ref = f32[40,128]{1,0:T(8,128)S(1)} collective-permute-done((f32[40,128]{1,0:T(8,128)S(1)}, f32[40,128]{1,0:T(8,128)S(1)}, u32[]{:S(2)}, u32[]{:S(2)}) %collective-permute-start.2) | collective-permute-done | bytes 20512 | tf_op jit(solution)/shard_map/ppermute | solution.py:299
  59.1 2.6 %all-to-all-done.2 = f32[32,1,128]{2,1,0:T(1,128)S(1)} async-done(((f32[32,1,128]{2,1,0:T(1,128)}), f32[32,1,128]{2,1,0:T(1,128)S(1)}, u32[]{:S(2)}, u32[]{:S(2)}) %all-to-all-start.2) | async-done | bytes 16416 | tf_op jit(solution)/shard_map/all_to_all | solution.py:311
  61.7 0.0 copy-done.2
  61.7 0.0 copy-done.3
  61.7 0.1 bottom.1
  61.9 10.8 %all_to_all.57 = bf16[8,120,128]{2,1,0:T(8,128)(2,1)S(1)} all-to-all(bf16[8,120,128]{2,1,0:T(8,128)(2,1)S(1)} %bitcast.28), channel_id=1, replica_groups={{4,5,6,7,0,1,2,3},{12,13,14,15,8,9,10,11},{20,21,22,23,16,17,18,19},{28..., dimensions={0} | all-to-all | bytes 491520 | tf_op jit(solution)/shard_map/all_to_all | solution.py:311
  72.7 0.8 third.1
  73.4 15.0 %all_to_all.58 = f32[64,1,128]{2,1,0:T(1,128)S(1)} all-to-all(f32[64,1,128]{2,1,0:T(1,128)S(1)} %bitcast.36), channel_id=1, replica_groups={{320,328,336,344,352,360,368,376,384,392,400,408,416,424,432,440,448,45..., dimensions={0} | all-to-all | bytes 65536 | tf_op jit(solution)/shard_map/all_to_all | solution.py:311
  88.5 0.0 copy-done.4
  88.5 0.0 copy-done.5
  88.5 0.7 last.1
Async XLA Ops:
  0.0 18.5 %copy-start = (bf16[27,40,320]{2,1,0:T(8,128)(2,1)S(1)}, bf16[27,40,320]{2,1,0:T(8,128)(2,1)}, u32[]{:S(2)}) copy-start(bf16[27,40,320]{2,1,0:T(8,128)(2,1)} %third_ref.1) | copy-start | bytes 2073604
  2.4 29.8 %copy-start.1 = (bf16[27,320,32]{1,2,0:T(8,128)(2,1)S(1)}, bf16[27,320,32]{1,2,0:T(8,128)(2,1)}, u32[]{:S(2)}) copy-start(bf16[27,320,32]{1,2,0:T(8,128)(2,1)} %param.14) | copy-start | bytes 1658884
  2.4 29.8 %copy-start.6 = (f32[32]{0:T(128)S(1)}, f32[32]{0:T(128)}, u32[]{:S(2)}) copy-start(f32[32]{0:T(128)} %param.12) | copy-start | bytes 388
  2.4 29.8 %copy-start.7 = (f32[32]{0:T(128)S(1)}, f32[32]{0:T(128)}, u32[]{:S(2)}) copy-start(f32[32]{0:T(128)} %param.13) | copy-start | bytes 388
  2.4 17.1 %collective-permute-start = (bf16[2,32,512]{2,1,0:T(8,128)(2,1)S(1)}, bf16[2,32,512]{2,1,0:T(8,128)(2,1)S(1)}, u32[]{:S(2)}, u32[]{:S(2)}) collective-permute-start(bf16[2,32,512]{2,1,0:T(8,128)(2,1)S(1)} %get-tuple-element.24), channel_id=1, source_target_pairs={{0,504},{8,16},{16,8},{24,32},{32,24},{40,48},{48,40},{56,64},{64,... | collective-permute-start | bytes 196616 | tf_op jit(solution)/shard_map/ppermute | solution.py:299
  7.9 11.6 %collective-permute-start.1 = (bf16[2,32,512]{2,1,0:T(8,128)(2,1)S(1)}, bf16[2,32,512]{2,1,0:T(8,128)(2,1)S(1)}, u32[]{:S(2)}, u32[]{:S(2)}) collective-permute-start(bf16[2,32,512]{2,1,0:T(8,128)(2,1)S(1)} %get-tuple-element.25), channel_id=1, source_target_pairs={{0,8},{8,0},{1,9},{9,1},{2,10},{10,2},{3,11},{11,3},{4,12},{12,4},... | collective-permute-start | bytes 196616 | tf_op jit(solution)/shard_map/ppermute | solution.py:303
  32.1 29.6 %copy-start.2 = (f32[40]{0:T(128)S(1)}, f32[40]{0:T(128)}, u32[]{:S(2)}) copy-start(f32[40]{0:T(128)} %param.15) | copy-start | bytes 484
  32.2 29.6 %copy-start.3 = (f32[40]{0:T(128)S(1)}, f32[40]{0:T(128)}, u32[]{:S(2)}) copy-start(f32[40]{0:T(128)} %param.16) | copy-start | bytes 484
  46.8 41.7 %copy-start.4 = (f32[40]{0:T(128)S(1)}, f32[40]{0:T(128)}, u32[]{:S(2)}) copy-start(f32[40]{0:T(128)} %param.18) | copy-start | bytes 484
  46.8 41.7 %copy-start.5 = (f32[40]{0:T(128)S(1)}, f32[40]{0:T(128)}, u32[]{:S(2)}) copy-start(f32[40]{0:T(128)} %param.19) | copy-start | bytes 484
  47.6 14.1 %all-to-all-start.2 = ((f32[32,1,128]{2,1,0:T(1,128)}), f32[32,1,128]{2,1,0:T(1,128)S(1)}, u32[]{:S(2)}, u32[]{:S(2)}) async-start(f32[32,1,128]{2,1,0:T(1,128)} %bitcast.11), calls=%async_computation.2 | async-start | bytes 32768 | tf_op jit(solution)/shard_map/all_to_all | solution.py:311
  53.1 6.1 %collective-permute-start.2 = (f32[40,128]{1,0:T(8,128)S(1)}, f32[40,128]{1,0:T(8,128)S(1)}, u32[]{:S(2)}, u32[]{:S(2)}) collective-permute-start(f32[40,128]{1,0:T(8,128)S(1)} %get-tuple-element.31), channel_id=1, source_target_pairs={{0,504},{8,16},{16,8},{24,32},{32,24},{40,48},{48,40},{56,64},{64,... | collective-permute-start | bytes 61448 | tf_op jit(solution)/shard_map/ppermute | solution.py:299

commit v6 on v5

--- a/solution.py
+++ b/solution.py
@@ -88,7 +88,7 @@
 
 def send_kernel(
     features_hbm, weight_hbm,
-    slices_ref, weight_ref, kept_ref, cross_ref, pair_ref,
+    slices_ref, weight_ref, kept_ref, up_ref,
     features_ref, sems,
 ):
     loads = [
@@ -109,25 +109,24 @@
     out_chans = block // 9
     lower, upper = slices_ref[0], slices_ref[1]
     loads[1].wait()
-    tap0, tap1, tap2 = (weight_ref[k * block : (k + 1) * block] for k in range(3))
+    tap0, tap1 = (weight_ref[k * block : (k + 1) * block] for k in range(2))
     up0 = shift_add(dot(tap0, lower) + dot(tap1, upper), out_chans, ROWS, COLS)
-    up1 = shift_add(dot(tap0, upper), out_chans, ROWS, COLS)
-    down = jnp.where(slab() == 0, 0.0, shift_add(dot(tap2, lower), out_chans, ROWS, COLS))
-    kept_ref[0] = up0
-    kept_ref[1] = down
-    even = lax.axis_index("core") == 0
-    up1 = up1.astype(jnp.bfloat16)
-    cross_ref[0] = jnp.where(even, down, up0).astype(jnp.bfloat16)
-    cross_ref[1] = up1
-    pair_ref[0] = jnp.where(even, up0, down).astype(jnp.bfloat16)
-    pair_ref[1] = up1
-
-
-def own_kernel(slices_ref, weight_ref, third_ref, own_ref, select_ref, stacked_ref):
+    kept_ref[...] = up0
+    up_ref[0] = up0.astype(jnp.bfloat16)
+    up_ref[1] = shift_add(dot(tap0, upper), out_chans, ROWS, COLS).astype(jnp.bfloat16)
+
+
+def own_kernel(
+    slices_ref, weight_ref, third_ref, own_ref, down_ref, below_ref, select_ref, stacked_ref
+):
     block = weight_ref.shape[0] // 3
     out_chans = block // 9
     lower, upper = slices_ref[0], slices_ref[1]
     tap1, tap2 = weight_ref[block : 2 * block], weight_ref[2 * block :]
+    down = shift_add(dot(tap2, lower), out_chans, ROWS, COLS)
+    down = jnp.where(slab() == 0, 0.0, down)
+    down_ref[...] = down
+    below_ref[...] = down.astype(below_ref.dtype)
     own_ref[...] = shift_add(dot(tap1, lower) + dot(tap2, upper), out_chans, ROWS, COLS)
 
     place = iota((HALF_CELLS, CELLS), 0)
@@ -149,16 +148,12 @@
             ]
 
 
-def total_kernel(kept_ref, own_ref, got_cross_ref, got_pair_ref, first_ref, copies_ref):
-    even = lax.axis_index("core") == 0
-
-    cross = got_cross_ref[...].astype(jnp.float32)
-    pair = got_pair_ref[...].astype(jnp.float32)
-    first0 = kept_ref[1] + jnp.where(even, cross[0], pair[0])
-    first1 = own_ref[...] + jnp.where(slab() == 0, 0.0, jnp.where(even, cross[1], pair[1]))
+def total_kernel(down_ref, own_ref, got_ref, first_ref, copies_ref):
+    got = got_ref[...].astype(jnp.float32)
+    first0 = down_ref[...] + got[0]
+    first1 = own_ref[...] + jnp.where(slab() == 0, 0.0, got[1])
     first_ref[0] = first0
     first_ref[1] = first1
-    first_ref[2] = kept_ref[0] + jnp.where(even, pair[0], cross[0])
     cells = 2 * CELLS
     mean = (
         jnp.sum(first0, axis=1, keepdims=True) + jnp.sum(first1, axis=1, keepdims=True)
@@ -180,14 +175,16 @@
 
 
 def down_kernel(
-    rows_ref, first_ref, gain_ref, bias_ref, select_ref, weight_ref, parts_ref
+    rows_ref, first_ref, kept_ref, back_ref, gain_ref, bias_ref, select_ref, weight_ref,
+    parts_ref,
 ):
     n = first_ref.shape[1]
     mean, spread = column_statistics(rows_ref[...], n)
     gain = to_column(gain_ref[...], 0, n)
     bias = to_column(bias_ref[...], 0, n)
     scale = gain * lax.rsqrt(spread + EPSILON)
-    levels = [leaky(scale * (first_ref[k] - mean) + bias) for k in range(3)]
+    firsts = (first_ref[0], first_ref[1], kept_ref[...] + back_ref[...].astype(jnp.float32))
+    levels = [leaky(scale * (first - mean) + bias) for first in firsts]
     levels[0] = jnp.where(slab() == 0, 0.0, levels[0])
     levels.append(jnp.zeros((LANES - 3 * n, CELLS), jnp.float32))
     layers = jnp.concatenate(levels, axis=0).astype(jnp.bfloat16)
@@ -299,8 +296,10 @@
     return lax.ppermute(value, ("chip", "core"), pairs)
 
 
-def beside(value):
-    return lax.ppermute(value, "core", [(0, 1), (1, 0)])
+def shift(value, by):
+    count = 2 * lax.axis_size("chip")
+    pairs = [(i, (i + by) % count) for i in range(count)]
+    return lax.ppermute(value, ("chip", "core"), pairs)
 
 
 def turned(count, first):
@@ -338,13 +337,12 @@
     biases = [v.reshape(1, -1) for v in (first_bias, down_bias, third_bias)]
     unit = 2 * 9 * n * in_chans * CELLS
 
-    slices, weights, kept, cross, pair = kernel_call(
+    slices, weights, kept, up = kernel_call(
         send_kernel,
         (
             struct((2, in_chans, CELLS), jnp.bfloat16),
             struct(first_weight.shape, jnp.bfloat16),
-            struct((2, n, CELLS)),
-            struct((2, n, CELLS), jnp.bfloat16),
+            struct((n, CELLS)),
             struct((2, n, CELLS), jnp.bfloat16),
         ),
         (
@@ -359,11 +357,13 @@
             pltpu.SemaphoreType.DMA((2,)),
         ],
     )
-    got_cross, got_pair = across(cross), beside(pair)
-    own, select, stacked = kernel_call(
+    got = shift(up, 1)
+    own, down, below, select, stacked = kernel_call(
         own_kernel,
         (
             struct((n, CELLS)),
+            struct((n, CELLS)),
+            struct((n, CELLS), jnp.float32),
             struct((9 * HALF_CELLS, CELLS), jnp.bfloat16),
             struct((9, PAIR, 3 * 3 * LANES), jnp.bfloat16),
         ),
@@ -371,18 +371,24 @@
         2 * unit,
         "own",
     )
+    back = shift(below, -1)
     first, copies = kernel_call(
         total_kernel,
-        (struct((3, n, CELLS)), struct((2 * chips, LANES))),
-        (kept, own, got_cross, got_pair),
+        (struct((2, n, CELLS)), struct((2 * chips, LANES))),
+        (down, own, got),
         1 << 20,
         "total",
     )
-    rows = exchange(copies, ("chip", "core"), turned(2 * chips, 2 * FIRST_CHIP))
+    rows = lax.cond(
+        slab() < 2 * chips,
+        lambda sent: exchange(sent, ("chip", "core"), turned(2 * chips, 2 * FIRST_CHIP)),
+        lambda sent: sent,
+        copies,
+    )
     parts = kernel_call(
         down_kernel,
         struct((2 * chans * m, HALF_CELLS), jnp.bfloat16),
-        (rows, first, gains[0], biases[0], select, down_weight),
+        (rows, first, kept, back, gains[0], biases[0], select, down_weight),
         unit,
         "down",
     )

time: 89.6 us -> 89.2 us (level)
  starting transfers between devices: 25.9 us -> 20.6 us
  blocking collectives: 51.8 us -> 56.9 us
    ppermute x2 -> x1, starting transfers between devices: 9.79 us -> 4.27 us  [across(): return lax.ppermute(value, ('chip', 'core'), pairs)]
    all_to_all x4, blocking collectives: 51.8 us -> 56.9 us  [exchange(): lax.all_to_all(copies, axes, 0, 0, axis_index_groups=[order], tiled=True)]
    ppermute x1 -> x2, starting transfers between devices: 10.6 us -> 10.8 us  [shift(): return lax.ppermute(value, ('chip', 'core'), pairs)]
where the time goes in v6:
time: 89.2 us; the launch traced here: 88.8 us
  blocking collectives  56.9 us (64%)
  starting transfers between devices  20.6 us (23%)
  Pallas kernels  6.83 us (8%)
  waiting for transfers between devices  4.35 us (5%)
    all_to_all x4, blocking collectives, exchange(): lax.all_to_all(copies, axes, 0, 0, axis_index_groups=[order], tiled=True)  56.9 us
    ppermute x2, starting transfers between devices, shift(): return lax.ppermute(value, ('chip', 'core'), pairs)  10.8 us
    pallas_call x8, Pallas kernels, kernel_call(): pl.pallas_call(body, out_shape=outputs, in_specs=in_specs or [VMEM] * len...  6.83 us
    all_to_all x1, starting transfers between devices, exchange(): lax.all_to_all(copies, axes, 0, 0, axis_index_groups=[order], tiled=True)  5.5 us
    ppermute x1, starting transfers between devices, across(): return lax.ppermute(value, ('chip', 'core'), pairs)  4.27 us
    all_to_all x1, waiting for transfers between devices, exchange(): lax.all_to_all(copies, axes, 0, 0, axis_index_groups=[order], tiled=True)  2.56 us
    ppermute x1, waiting for transfers between devices, across(): return lax.ppermute(value, ('chip', 'core'), pairs)  1.78 us
  transfers between devices with their start and end apart: 4, of which 2 were waited for; matrix products, arithmetic and copies ran while one was open for 0% of the time, Pallas kernels for 1%

profile of v6, /device:TPU:1, one launch (start us, length us, event | category | flops | bytes accessed | tf_op | source)
XLA Modules:
  0.0 88.8 jit_solution(7324480001364235986)
XLA Ops:
  0.0 0.0 copy-start
  0.0 2.2 %send.1 = (bf16[2,256,512]{2,1,0:T(8,128)(2,1)S(1)}, bf16[864,256]{1,0:T(8,128)(2,1)S(1)}, f32[32,512]{1,0:T(8,128)S(1)}, bf16[2,32,512]{2,1,0:T(8,128)(2,1)S(1)}) custom-call(bf16[256,2,512]{2,1,0:T(2,128)(2,1)} %features_hbm.1, bf16[864,256]{1,0:T(8,128)(2,1)} %bitcast.41), custom_call_target="tpu_custom_call" | custom-call | flops 301989888 | bytes 2097152 | tf_op jit(solution)/shard_map/send/pallas_call | solution.py:28
  2.2 0.0 copy-start.1
  2.2 0.0 copy-start.6
  2.2 0.0 copy-start.7
  2.3 5.5 %collective-permute-start = (bf16[2,32,512]{2,1,0:T(8,128)(2,1)S(1)}, bf16[2,32,512]{2,1,0:T(8,128)(2,1)S(1)}, u32[]{:S(2)}, u32[]{:S(2)}) collective-permute-start(bf16[2,32,512]{2,1,0:T(8,128)(2,1)S(1)} %get-tuple-element.30), channel_id=1, source_target_pairs={{0,8},{8,16},{16,24},{24,32},{32,40},{40,48},{48,56},{56,64},{64,7... | collective-permute-start | bytes 196616 | tf_op jit(solution)/shard_map/ppermute | solution.py:302
  7.8 0.0 copy-done
  7.8 1.0 %own.1 = (f32[32,512]{1,0:T(8,128)S(1)}, f32[32,512]{1,0:T(8,128)S(1)}, f32[32,512]{1,0:T(8,128)S(1)}, bf16[1152,512]{1,0:T(8,128)(2,1)S(1)}, bf16[9,48,1152]{2,1,0:T(8,128)(2,1)S(1)}) custom-call(bf16[2,256,512]{2,1,0:T(8,128)(2,1)S(1)} %get-tuple-element.26.slices_ref, bf16[864,256]{1,0:T(8,128)(2,1)S(1)} %get-tuple-element.27.weight_ref, ...), custom_call_target="tpu_custom_call" | custom-call | flops 150994944 | bytes 2097152 | tf_op jit(solution)/shard_map/own/pallas_call | solution.py:28
  8.8 5.3 %collective-permute-start.1 = (f32[32,512]{1,0:T(8,128)S(1)}, f32[32,512]{1,0:T(8,128)S(1)}, u32[]{:S(2)}, u32[]{:S(2)}) collective-permute-start(f32[32,512]{1,0:T(8,128)S(1)} %get-tuple-element.34), channel_id=1, source_target_pairs={{0,504},{8,0},{16,8},{24,16},{32,24},{40,32},{48,40},{56,48},{64,5... | collective-permute-start | bytes 196616 | tf_op jit(solution)/shard_map/ppermute | solution.py:302
  14.1 0.0 collective-permute-done.got_ref
  14.1 0.2 total.1
  14.3 17.5 %conditional.1 = (f32[64,128]{1,0:T(8,128)S(1)}) conditional(s32[]{:T(128)} %convert_element_type.3, f32[64,128]{1,0:T(8,128)S(1)} %get-tuple-element.31, f32[64,128]{1,0:T(8,128)S(1)} %get-tuple-element.31), branch_computations={%region_0.0_spmd, %region_1.0_spmd} | conditional | bytes 131080 | solution.py:382
  14.3 17.5 %all_to_all.53 = f32[64,1,128]{2,1,0:T(1,128)S(1)} all-to-all(f32[64,1,128]{2,1,0:T(1,128)S(1)} %copy.15), channel_id=1, replica_groups={{496,504,0,8,16,24,32,40,48,56,64,72,80,88,96,104,112,120,128,136,144,1..., dimensions={0} | all-to-all | bytes 65536 | tf_op jit(solution)/shard_map/cond/branch_1_fun/all_to_all | solution.py:310
  31.8 0.0 collective-permute-done.1.back_ref
  31.8 0.0 copy-done.1
  31.8 0.0 copy-done.6
  31.8 0.0 copy-done.7
  31.8 0.0 copy-start.2
  31.8 0.0 copy-start.3
  31.8 1.1 %down.1 = bf16[640,128]{1,0:T(8,128)(2,1)S(1)} custom-call(f32[64,128]{1,0:T(8,128)S(1)} %get-tuple-element.42.rows_ref, f32[2,32,512]{2,1,0:T(8,128)S(1)} %get-tuple-element.32.first_ref, f32[32,512]{1,0:T(8,128)S(1)} %get-tuple-element.33.kept_ref, f32[32,512]{1,0:T(8,128)S(1)} %collective-permute-done.1.back_ref, f32[1,32]{1,0:T(1,128)S(1)} %bitcast.37, ...), custom_call_target="tpu_custom_call" | custom-call | flops 75497472 | bytes 2097152 | tf_op jit(solution)/shard_map/down/pallas_call | solution.py:28
  32.9 13.5 %all_to_all.54 = bf16[16,40,128]{2,1,0:T(8,128)(2,1)S(1)} all-to-all(bf16[16,40,128]{2,1,0:T(8,128)(2,1)S(1)} %bitcast.28), channel_id=1, replica_groups={{4,5,6,7,0,1,2,3,12,13,14,15,8,9,10,11},{20,21,22,23,16,17,18,19,28,29,..., dimensions={0} | all-to-all | bytes 327680 | tf_op jit(solution)/shard_map/all_to_all | solution.py:310
  46.4 0.0 copy-start.4
  46.4 0.0 copy-start.5
  46.4 0.8 reduced.1
  47.2 5.5 %all-to-all-start.2 = ((f32[32,1,128]{2,1,0:T(1,128)}), f32[32,1,128]{2,1,0:T(1,128)S(1)}, u32[]{:S(2)}, u32[]{:S(2)}) async-start(f32[32,1,128]{2,1,0:T(1,128)} %bitcast.10), calls=%async_computation.2 | async-start | bytes 32768 | tf_op jit(solution)/shard_map/all_to_all | solution.py:310
  52.7 4.3 %collective-permute-start.2 = (f32[40,128]{1,0:T(8,128)S(1)}, f32[40,128]{1,0:T(8,128)S(1)}, u32[]{:S(2)}, u32[]{:S(2)}) collective-permute-start(f32[40,128]{1,0:T(8,128)S(1)} %get-tuple-element.38), channel_id=1, source_target_pairs={{0,504},{8,16},{16,8},{24,32},{32,24},{40,48},{48,40},{56,64},{64,... | collective-permute-start | bytes 61448 | tf_op jit(solution)/shard_map/ppermute | solution.py:296
  57.0 1.8 %collective-permute-done.2.got_ref = f32[40,128]{1,0:T(8,128)S(1)} collective-permute-done((f32[40,128]{1,0:T(8,128)S(1)}, f32[40,128]{1,0:T(8,128)S(1)}, u32[]{:S(2)}, u32[]{:S(2)}) %collective-permute-start.2) | collective-permute-done | bytes 20512 | tf_op jit(solution)/shard_map/ppermute | solution.py:296
  58.8 2.6 %all-to-all-done.2 = f32[32,1,128]{2,1,0:T(1,128)S(1)} async-done(((f32[32,1,128]{2,1,0:T(1,128)}), f32[32,1,128]{2,1,0:T(1,128)S(1)}, u32[]{:S(2)}, u32[]{:S(2)}) %all-to-all-start.2) | async-done | bytes 16416 | tf_op jit(solution)/shard_map/all_to_all | solution.py:310
  61.3 0.0 copy-done.2
  61.4 0.0 copy-done.3
  61.4 0.1 bottom.1
  61.5 10.8 %all_to_all.55 = bf16[8,120,128]{2,1,0:T(8,128)(2,1)S(1)} all-to-all(bf16[8,120,128]{2,1,0:T(8,128)(2,1)S(1)} %bitcast.26), channel_id=1, replica_groups={{4,5,6,7,0,1,2,3},{12,13,14,15,8,9,10,11},{20,21,22,23,16,17,18,19},{28..., dimensions={0} | all-to-all | bytes 491520 | tf_op jit(solution)/shard_map/all_to_all | solution.py:310
  72.3 0.7 third.1
  73.1 15.1 %all_to_all.56 = f32[64,1,128]{2,1,0:T(1,128)S(1)} all-to-all(f32[64,1,128]{2,1,0:T(1,128)S(1)} %bitcast.32), channel_id=1, replica_groups={{320,328,336,344,352,360,368,376,384,392,400,408,416,424,432,440,448,45..., dimensions={0} | all-to-all | bytes 65536 | tf_op jit(solution)/shard_map/all_to_all | solution.py:310
  88.1 0.0 copy-done.4
  88.1 0.0 copy-done.5
  88.1 0.7 last.1
  (1 shorter events, 0.0 us)
Async XLA Ops:
  0.0 7.8 %copy-start = (bf16[27,40,320]{2,1,0:T(8,128)(2,1)S(1)}, bf16[27,40,320]{2,1,0:T(8,128)(2,1)}, u32[]{:S(2)}) copy-start(bf16[27,40,320]{2,1,0:T(8,128)(2,1)} %third_ref.1) | copy-start | bytes 2073604
  2.2 29.6 %copy-start.1 = (bf16[27,320,32]{1,2,0:T(8,128)(2,1)S(1)}, bf16[27,320,32]{1,2,0:T(8,128)(2,1)}, u32[]{:S(2)}) copy-start(bf16[27,320,32]{1,2,0:T(8,128)(2,1)} %param.16) | copy-start | bytes 1658884
  2.2 29.5 %copy-start.6 = (f32[32]{0:T(128)S(1)}, f32[32]{0:T(128)}, u32[]{:S(2)}) copy-start(f32[32]{0:T(128)} %param.14) | copy-start | bytes 388
  2.2 29.5 %copy-start.7 = (f32[32]{0:T(128)S(1)}, f32[32]{0:T(128)}, u32[]{:S(2)}) copy-start(f32[32]{0:T(128)} %param.15) | copy-start | bytes 388
  2.3 11.8 %collective-permute-start = (bf16[2,32,512]{2,1,0:T(8,128)(2,1)S(1)}, bf16[2,32,512]{2,1,0:T(8,128)(2,1)S(1)}, u32[]{:S(2)}, u32[]{:S(2)}) collective-permute-start(bf16[2,32,512]{2,1,0:T(8,128)(2,1)S(1)} %get-tuple-element.30), channel_id=1, source_target_pairs={{0,8},{8,16},{16,24},{24,32},{32,40},{40,48},{48,56},{56,64},{64,7... | collective-permute-start | bytes 196616 | tf_op jit(solution)/shard_map/ppermute | solution.py:302
  8.8 23.0 %collective-permute-start.1 = (f32[32,512]{1,0:T(8,128)S(1)}, f32[32,512]{1,0:T(8,128)S(1)}, u32[]{:S(2)}, u32[]{:S(2)}) collective-permute-start(f32[32,512]{1,0:T(8,128)S(1)} %get-tuple-element.34), channel_id=1, source_target_pairs={{0,504},{8,0},{16,8},{24,16},{32,24},{40,32},{48,40},{56,48},{64,5... | collective-permute-start | bytes 196616 | tf_op jit(solution)/shard_map/ppermute | solution.py:302
  31.8 29.6 %copy-start.2 = (f32[40]{0:T(128)S(1)}, f32[40]{0:T(128)}, u32[]{:S(2)}) copy-start(f32[40]{0:T(128)} %param.17) | copy-start | bytes 484
  31.8 29.6 %copy-start.3 = (f32[40]{0:T(128)S(1)}, f32[40]{0:T(128)}, u32[]{:S(2)}) copy-start(f32[40]{0:T(128)} %param.18) | copy-start | bytes 484
  46.4 41.7 %copy-start.4 = (f32[40]{0:T(128)S(1)}, f32[40]{0:T(128)}, u32[]{:S(2)}) copy-start(f32[40]{0:T(128)} %param.20) | copy-start | bytes 484
  46.4 41.7 %copy-start.5 = (f32[40]{0:T(128)S(1)}, f32[40]{0:T(128)}, u32[]{:S(2)}) copy-start(f32[40]{0:T(128)} %param.21) | copy-start | bytes 484
  47.2 14.1 %all-to-all-start.2 = ((f32[32,1,128]{2,1,0:T(1,128)}), f32[32,1,128]{2,1,0:T(1,128)S(1)}, u32[]{:S(2)}, u32[]{:S(2)}) async-start(f32[32,1,128]{2,1,0:T(1,128)} %bitcast.10), calls=%async_computation.2 | async-start | bytes 32768 | tf_op jit(solution)/shard_map/all_to_all | solution.py:310
  52.7 6.1 %collective-permute-start.2 = (f32[40,128]{1,0:T(8,128)S(1)}, f32[40,128]{1,0:T(8,128)S(1)}, u32[]{:S(2)}, u32[]{:S(2)}) collective-permute-start(f32[40,128]{1,0:T(8,128)S(1)} %get-tuple-element.38), channel_id=1, source_target_pairs={{0,504},{8,16},{16,8},{24,32},{32,24},{40,48},{48,40},{56,64},{64,... | collective-permute-start | bytes 61448 | tf_op jit(solution)/shard_map/ppermute | solution.py:296

commit v7 on v6

--- a/solution.py
+++ b/solution.py
@@ -14,9 +14,10 @@
 LANES = 128
 PAIR = 48
 FIRST_CHIP = 31
-SECOND_CHIP = 0
+SECOND_CHIP = 7
 THIRD_CHIP = 20
-FIRST_CHAN = 4
+FIRST_CHAN = 5
+SECOND_CHAN = 5
 EPSILON = 1e-05
 SLOPE = 0.01
 
@@ -98,13 +99,12 @@
     for load in loads:
         load.start()
     chans = features_ref.shape[0]
+    gap = iota((chans, 2 * chans), 1) - 2 * iota((chans, 2 * chans), 0)
+    picks = [(gap == j).astype(jnp.bfloat16) for j in range(2)]
     loads[0].wait()
     pairs = features_ref[...].reshape(2 * chans, CELLS)
     for j in range(2):
-        pick = (iota((chans, 2 * chans), 1) == 2 * iota((chans, 2 * chans), 0) + j).astype(
-            jnp.bfloat16
-        )
-        slices_ref[j] = dot(pick, pairs).astype(jnp.bfloat16)
+        slices_ref[j] = dot(picks[j], pairs).astype(jnp.bfloat16)
     block = weight_ref.shape[0] // 3
     out_chans = block // 9
     lower, upper = slices_ref[0], slices_ref[1]
@@ -129,14 +129,14 @@
     below_ref[...] = down.astype(below_ref.dtype)
     own_ref[...] = shift_add(dot(tap1, lower) + dot(tap2, upper), out_chans, ROWS, COLS)
 
-    place = iota((HALF_CELLS, CELLS), 0)
-    cell = iota((HALF_CELLS, CELLS), 1)
-    row, column = cell // COLS, cell % COLS
-    row_gap = row - 2 * (place // HALF_COLS)
-    column_gap = column - 2 * (place % HALF_COLS)
+    cell = iota((CELLS, HALF_CELLS), 0)
+    place = iota((CELLS, HALF_CELLS), 1)
+    row_gap = cell // COLS - 2 * (place // HALF_COLS)
+    column_gap = cell % COLS - 2 * (place % HALF_COLS)
+    gap = row_gap * (2 * COLS) + column_gap
     for tap in range(9):
-        hit = (row_gap == tap // 3 - 1) & (column_gap == tap % 3 - 1)
-        select_ref[tap * HALF_CELLS : (tap + 1) * HALF_CELLS] = hit.astype(jnp.bfloat16)
+        hit = gap == (tap // 3 - 1) * (2 * COLS) + tap % 3 - 1
+        select_ref[:, tap * HALF_CELLS : (tap + 1) * HALF_CELLS] = hit.astype(jnp.bfloat16)
 
     third_out, third_in = third_ref.shape[1:]
     stacked_ref[...] = jnp.zeros_like(stacked_ref)
@@ -186,18 +186,20 @@
     firsts = (first_ref[0], first_ref[1], kept_ref[...] + back_ref[...].astype(jnp.float32))
     levels = [leaky(scale * (first - mean) + bias) for first in firsts]
     levels[0] = jnp.where(slab() == 0, 0.0, levels[0])
-    levels.append(jnp.zeros((LANES - 3 * n, CELLS), jnp.float32))
     layers = jnp.concatenate(levels, axis=0).astype(jnp.bfloat16)
     out_chans = weight_ref.shape[1]
-    picked = dot_nt(select_ref[...], layers).astype(jnp.bfloat16)
-    windows, weights = [], []
-    for tap in range(9):
-        windows.append(picked[tap * HALF_CELLS : (tap + 1) * HALF_CELLS])
-        for depth in range(3):
-            at = (depth * 9 + tap) * n
-            weights.append(weight_ref[at : at + n])
-        weights.append(jnp.zeros((LANES - 3 * n, out_chans), jnp.bfloat16))
-    parts = dot(jnp.concatenate(windows, axis=1), jnp.concatenate(weights, axis=0))
+    picked = dot(layers, select_ref[...]).astype(jnp.bfloat16)
+    windows = jnp.concatenate(
+        [
+            picked[depth * n : (depth + 1) * n, tap * HALF_CELLS : (tap + 1) * HALF_CELLS]
+            for depth in range(3)
+            for tap in range(9)
+        ],
+        axis=0,
+    )
+    parts = lax.dot_general(
+        windows, weight_ref[...], (((0,), (0,)), ((), ())), preferred_element_type=jnp.float32
+    )
     spare = -out_chans % LANES
     parts = jnp.concatenate([parts, jnp.zeros((HALF_CELLS, spare), jnp.float32)], axis=1).T
     chans = lax.axis_size("chan")
@@ -266,7 +268,7 @@
     gathered = bottom_ref[...].astype(jnp.float32)
     blocks = []
     for k in range(depths):
-        for c in turned(chans, chans - FIRST_CHAN):
+        for c in turned(chans, chans - SECOND_CHAN):
             at = (c * depths + k) * share
             blocks.append(gathered[at : at + share])
         blocks.append(jnp.zeros((wide - chans * share, cells), jnp.float32))
@@ -364,7 +366,7 @@
             struct((n, CELLS)),
             struct((n, CELLS)),
             struct((n, CELLS), jnp.float32),
-            struct((9 * HALF_CELLS, CELLS), jnp.bfloat16),
+            struct((CELLS, 9 * HALF_CELLS), jnp.bfloat16),
             struct((9, PAIR, 3 * 3 * LANES), jnp.bfloat16),
         ),
         (slices, weights, third_weight),
@@ -413,7 +415,7 @@
         1 << 20,
         "bottom",
     )
-    bottom = exchange(copies, "chan", turned(chans, FIRST_CHAN))
+    bottom = exchange(copies, "chan", turned(chans, SECOND_CHAN))
     third, copies = kernel_call(
         third_kernel,
         (struct((m, HALF_CELLS)), struct((2 * chips, LANES))),

time: 89.2 us -> 88 us (0.987)
  waiting for transfers between devices: 4.35 us -> 2.4 us
    all_to_all x1, waiting for transfers between devices: 2.56 us -> 0.61 us  [exchange(): lax.all_to_all(copies, axes, 0, 0, axis_index_groups=[order], tiled=True)]
where the time goes in v7:
time: 88 us; the launch traced here: 87.6 us
  blocking collectives  57.5 us (65%)
  starting transfers between devices  20.9 us (24%)
  Pallas kernels  6.59 us (7%)
  waiting for transfers between devices  2.4 us (3%)
    all_to_all x4, blocking collectives, exchange(): lax.all_to_all(copies, axes, 0, 0, axis_index_groups=[order], tiled=True)  57.5 us
    ppermute x2, starting transfers between devices, shift(): return lax.ppermute(value, ('chip', 'core'), pairs)  10.8 us
    pallas_call x8, Pallas kernels, kernel_call(): pl.pallas_call(body, out_shape=outputs, in_specs=in_specs or [VMEM] * len...  6.59 us
    all_to_all x1, starting transfers between devices, exchange(): lax.all_to_all(copies, axes, 0, 0, axis_index_groups=[order], tiled=True)  6.1 us
    ppermute x1, starting transfers between devices, across(): return lax.ppermute(value, ('chip', 'core'), pairs)  4 us
    ppermute x1, waiting for transfers between devices, across(): return lax.ppermute(value, ('chip', 'core'), pairs)  1.79 us
  transfers between devices with their start and end apart: 4, of which 2 were waited for; matrix products, arithmetic and copies ran while one was open for 0% of the time, Pallas kernels for 1%

profile of v7, /device:TPU:1, one launch (start us, length us, event | category | flops | bytes accessed | tf_op | source)
XLA Modules:
  0.0 87.6 jit_solution(17443174752092871363)
XLA Ops:
  0.0 0.0 copy-start
  0.0 2.2 %send.1 = (bf16[2,256,512]{2,1,0:T(8,128)(2,1)S(1)}, bf16[864,256]{1,0:T(8,128)(2,1)S(1)}, f32[32,512]{1,0:T(8,128)S(1)}, bf16[2,32,512]{2,1,0:T(8,128)(2,1)S(1)}) custom-call(bf16[256,2,512]{2,1,0:T(2,128)(2,1)} %features_hbm.1, bf16[864,256]{1,0:T(8,128)(2,1)} %bitcast.41), custom_call_target="tpu_custom_call" | custom-call | flops 301989888 | bytes 2097152 | tf_op jit(solution)/shard_map/send/pallas_call | solution.py:29
  2.2 0.0 copy-start.1
  2.2 0.0 copy-start.6
  2.2 0.0 copy-start.7
  2.3 5.5 %collective-permute-start = (bf16[2,32,512]{2,1,0:T(8,128)(2,1)S(1)}, bf16[2,32,512]{2,1,0:T(8,128)(2,1)S(1)}, u32[]{:S(2)}, u32[]{:S(2)}) collective-permute-start(bf16[2,32,512]{2,1,0:T(8,128)(2,1)S(1)} %get-tuple-element.30), channel_id=1, source_target_pairs={{0,8},{8,16},{16,24},{24,32},{32,40},{40,48},{48,56},{56,64},{64,7... | collective-permute-start | bytes 196616 | tf_op jit(solution)/shard_map/ppermute | solution.py:304
  7.8 0.0 copy-done
  7.8 1.0 %own.1 = (f32[32,512]{1,0:T(8,128)S(1)}, f32[32,512]{1,0:T(8,128)S(1)}, f32[32,512]{1,0:T(8,128)S(1)}, bf16[512,1152]{1,0:T(8,128)(2,1)S(1)}, bf16[9,48,1152]{2,1,0:T(8,128)(2,1)S(1)}) custom-call(bf16[2,256,512]{2,1,0:T(8,128)(2,1)S(1)} %get-tuple-element.26.slices_ref, bf16[864,256]{1,0:T(8,128)(2,1)S(1)} %get-tuple-element.27.weight_ref, ...), custom_call_target="tpu_custom_call" | custom-call | flops 150994944 | bytes 2097152 | tf_op jit(solution)/shard_map/own/pallas_call | solution.py:29
  8.8 5.3 %collective-permute-start.1 = (f32[32,512]{1,0:T(8,128)S(1)}, f32[32,512]{1,0:T(8,128)S(1)}, u32[]{:S(2)}, u32[]{:S(2)}) collective-permute-start(f32[32,512]{1,0:T(8,128)S(1)} %get-tuple-element.34), channel_id=1, source_target_pairs={{0,504},{8,0},{16,8},{24,16},{32,24},{40,32},{48,40},{56,48},{64,5... | collective-permute-start | bytes 196616 | tf_op jit(solution)/shard_map/ppermute | solution.py:304
  14.1 0.0 collective-permute-done.got_ref
  14.1 0.2 total.1
  14.3 17.5 %conditional.1 = (f32[64,128]{1,0:T(8,128)S(1)}) conditional(s32[]{:T(128)} %convert_element_type.3, f32[64,128]{1,0:T(8,128)S(1)} %get-tuple-element.31, f32[64,128]{1,0:T(8,128)S(1)} %get-tuple-element.31), branch_computations={%region_0.0_spmd, %region_1.0_spmd} | conditional | bytes 131080 | solution.py:384
  14.4 17.5 %all_to_all.53 = f32[64,1,128]{2,1,0:T(1,128)S(1)} all-to-all(f32[64,1,128]{2,1,0:T(1,128)S(1)} %copy.15), channel_id=1, replica_groups={{496,504,0,8,16,24,32,40,48,56,64,72,80,88,96,104,112,120,128,136,144,1..., dimensions={0} | all-to-all | bytes 65536 | tf_op jit(solution)/shard_map/cond/branch_1_fun/all_to_all | solution.py:312
  31.8 0.0 collective-permute-done.1.back_ref
  31.8 0.0 copy-done.1
  31.8 0.0 copy-done.6
  31.8 0.0 copy-done.7
  31.8 0.0 copy-start.2
  31.9 0.0 copy-start.3
  31.9 0.8 down.1
  32.7 13.6 %all_to_all.54 = bf16[16,40,128]{2,1,0:T(8,128)(2,1)S(1)} all-to-all(bf16[16,40,128]{2,1,0:T(8,128)(2,1)S(1)} %bitcast.28), channel_id=1, replica_groups={{5,6,7,0,1,2,3,4,13,14,15,8,9,10,11,12},{21,22,23,16,17,18,19,20,29,30,..., dimensions={0} | all-to-all | bytes 327680 | tf_op jit(solution)/shard_map/all_to_all | solution.py:312
  46.2 0.0 copy-start.4
  46.2 0.0 copy-start.5
  46.2 0.8 reduced.1
  47.0 6.1 %all-to-all-start.2 = ((f32[32,1,128]{2,1,0:T(1,128)}), f32[32,1,128]{2,1,0:T(1,128)S(1)}, u32[]{:S(2)}, u32[]{:S(2)}) async-start(f32[32,1,128]{2,1,0:T(1,128)} %bitcast.10), calls=%async_computation.2 | async-start | bytes 32768 | tf_op jit(solution)/shard_map/all_to_all | solution.py:312
  53.1 4.0 %collective-permute-start.2 = (f32[40,128]{1,0:T(8,128)S(1)}, f32[40,128]{1,0:T(8,128)S(1)}, u32[]{:S(2)}, u32[]{:S(2)}) collective-permute-start(f32[40,128]{1,0:T(8,128)S(1)} %get-tuple-element.38), channel_id=1, source_target_pairs={{0,504},{8,16},{16,8},{24,32},{32,24},{40,48},{48,40},{56,64},{64,... | collective-permute-start | bytes 61448 | tf_op jit(solution)/shard_map/ppermute | solution.py:298
  57.1 1.8 %collective-permute-done.2.got_ref = f32[40,128]{1,0:T(8,128)S(1)} collective-permute-done((f32[40,128]{1,0:T(8,128)S(1)}, f32[40,128]{1,0:T(8,128)S(1)}, u32[]{:S(2)}, u32[]{:S(2)}) %collective-permute-start.2) | collective-permute-done | bytes 20512 | tf_op jit(solution)/shard_map/ppermute | solution.py:298
  58.9 0.6 all-to-all-done.2
  59.5 0.0 copy-done.2
  59.5 0.0 copy-done.3
  59.5 0.1 bottom.1
  59.7 9.8 %all_to_all.55 = bf16[8,120,128]{2,1,0:T(8,128)(2,1)S(1)} all-to-all(bf16[8,120,128]{2,1,0:T(8,128)(2,1)S(1)} %bitcast.26), channel_id=1, replica_groups={{5,6,7,0,1,2,3,4},{13,14,15,8,9,10,11,12},{21,22,23,16,17,18,19,20},{29..., dimensions={0} | all-to-all | bytes 491520 | tf_op jit(solution)/shard_map/all_to_all | solution.py:312
  69.5 0.7 third.1
  70.2 16.7 %all_to_all.56 = f32[64,1,128]{2,1,0:T(1,128)S(1)} all-to-all(f32[64,1,128]{2,1,0:T(1,128)S(1)} %bitcast.32), channel_id=1, replica_groups={{320,328,336,344,352,360,368,376,384,392,400,408,416,424,432,440,448,45..., dimensions={0} | all-to-all | bytes 65536 | tf_op jit(solution)/shard_map/all_to_all | solution.py:312
  86.9 0.0 copy-done.4
  86.9 0.0 copy-done.5
  86.9 0.7 last.1
  (1 shorter events, 0.0 us)
Async XLA Ops:
  0.0 7.8 %copy-start = (bf16[27,40,320]{2,1,0:T(8,128)(2,1)S(1)}, bf16[27,40,320]{2,1,0:T(8,128)(2,1)}, u32[]{:S(2)}) copy-start(bf16[27,40,320]{2,1,0:T(8,128)(2,1)} %third_ref.1) | copy-start | bytes 2073604
  2.2 29.6 %copy-start.1 = (bf16[27,320,32]{1,2,0:T(8,128)(2,1)S(1)}, bf16[27,320,32]{1,2,0:T(8,128)(2,1)}, u32[]{:S(2)}) copy-start(bf16[27,320,32]{1,2,0:T(8,128)(2,1)} %param.16) | copy-start | bytes 1658884
  2.2 29.6 %copy-start.6 = (f32[32]{0:T(128)S(1)}, f32[32]{0:T(128)}, u32[]{:S(2)}) copy-start(f32[32]{0:T(128)} %param.14) | copy-start | bytes 388
  2.2 29.6 %copy-start.7 = (f32[32]{0:T(128)S(1)}, f32[32]{0:T(128)}, u32[]{:S(2)}) copy-start(f32[32]{0:T(128)} %param.15) | copy-start | bytes 388
  2.3 11.9 %collective-permute-start = (bf16[2,32,512]{2,1,0:T(8,128)(2,1)S(1)}, bf16[2,32,512]{2,1,0:T(8,128)(2,1)S(1)}, u32[]{:S(2)}, u32[]{:S(2)}) collective-permute-start(bf16[2,32,512]{2,1,0:T(8,128)(2,1)S(1)} %get-tuple-element.30), channel_id=1, source_target_pairs={{0,8},{8,16},{16,24},{24,32},{32,40},{40,48},{48,56},{56,64},{64,7... | collective-permute-start | bytes 196616 | tf_op jit(solution)/shard_map/ppermute | solution.py:304
  8.8 23.0 %collective-permute-start.1 = (f32[32,512]{1,0:T(8,128)S(1)}, f32[32,512]{1,0:T(8,128)S(1)}, u32[]{:S(2)}, u32[]{:S(2)}) collective-permute-start(f32[32,512]{1,0:T(8,128)S(1)} %get-tuple-element.34), channel_id=1, source_target_pairs={{0,504},{8,0},{16,8},{24,16},{32,24},{40,32},{48,40},{56,48},{64,5... | collective-permute-start | bytes 196616 | tf_op jit(solution)/shard_map/ppermute | solution.py:304
  31.8 27.7 %copy-start.2 = (f32[40]{0:T(128)S(1)}, f32[40]{0:T(128)}, u32[]{:S(2)}) copy-start(f32[40]{0:T(128)} %param.17) | copy-start | bytes 484
  31.9 27.7 %copy-start.3 = (f32[40]{0:T(128)S(1)}, f32[40]{0:T(128)}, u32[]{:S(2)}) copy-start(f32[40]{0:T(128)} %param.18) | copy-start | bytes 484
  46.2 40.7 %copy-start.4 = (f32[40]{0:T(128)S(1)}, f32[40]{0:T(128)}, u32[]{:S(2)}) copy-start(f32[40]{0:T(128)} %param.20) | copy-start | bytes 484
  46.2 40.7 %copy-start.5 = (f32[40]{0:T(128)S(1)}, f32[40]{0:T(128)}, u32[]{:S(2)}) copy-start(f32[40]{0:T(128)} %param.21) | copy-start | bytes 484
  47.0 12.5 %all-to-all-start.2 = ((f32[32,1,128]{2,1,0:T(1,128)}), f32[32,1,128]{2,1,0:T(1,128)S(1)}, u32[]{:S(2)}, u32[]{:S(2)}) async-start(f32[32,1,128]{2,1,0:T(1,128)} %bitcast.10), calls=%async_computation.2 | async-start | bytes 32768 | tf_op jit(solution)/shard_map/all_to_all | solution.py:312
  53.1 5.8 %collective-permute-start.2 = (f32[40,128]{1,0:T(8,128)S(1)}, f32[40,128]{1,0:T(8,128)S(1)}, u32[]{:S(2)}, u32[]{:S(2)}) collective-permute-start(f32[40,128]{1,0:T(8,128)S(1)} %get-tuple-element.38), channel_id=1, source_target_pairs={{0,504},{8,16},{16,8},{24,32},{32,24},{40,48},{48,40},{56,64},{64,... | collective-permute-start | bytes 61448 | tf_op jit(solution)/shard_map/ppermute | solution.py:298

commit v8 on v7

--- a/solution.py
+++ b/solution.py
@@ -1,5 +1,7 @@
 import jax
 import jax.numpy as jnp
+import ml_dtypes
+import numpy as np
 from jax import lax
 from jax.experimental import pallas as pl
 from jax.experimental.pallas import tpu as pltpu
@@ -117,7 +119,7 @@
 
 
 def own_kernel(
-    slices_ref, weight_ref, third_ref, own_ref, down_ref, below_ref, select_ref, stacked_ref
+    slices_ref, weight_ref, third_ref, own_ref, down_ref, below_ref, stacked_ref
 ):
     block = weight_ref.shape[0] // 3
     out_chans = block // 9
@@ -128,15 +130,6 @@
     down_ref[...] = down
     below_ref[...] = down.astype(below_ref.dtype)
     own_ref[...] = shift_add(dot(tap1, lower) + dot(tap2, upper), out_chans, ROWS, COLS)
-
-    cell = iota((CELLS, HALF_CELLS), 0)
-    place = iota((CELLS, HALF_CELLS), 1)
-    row_gap = cell // COLS - 2 * (place // HALF_COLS)
-    column_gap = cell % COLS - 2 * (place % HALF_COLS)
-    gap = row_gap * (2 * COLS) + column_gap
-    for tap in range(9):
-        hit = gap == (tap // 3 - 1) * (2 * COLS) + tap % 3 - 1
-        select_ref[:, tap * HALF_CELLS : (tap + 1) * HALF_CELLS] = hit.astype(jnp.bfloat16)
 
     third_out, third_in = third_ref.shape[1:]
     stacked_ref[...] = jnp.zeros_like(stacked_ref)
@@ -312,6 +305,16 @@
     return lax.all_to_all(copies, axes, 0, 0, axis_index_groups=[order], tiled=True)
 
 
+def sampling():
+    cell = np.arange(CELLS)[:, None, None]
+    tap = np.arange(9)[None, :, None]
+    place = np.arange(HALF_CELLS)[None, None, :]
+    row = 2 * (place // HALF_COLS) + tap // 3 - 1
+    column = 2 * (place % HALF_COLS) + tap % 3 - 1
+    hit = (cell // COLS == row) & (cell % COLS == column)
+    return hit.reshape(CELLS, 9 * HALF_CELLS).astype(ml_dtypes.bfloat16)
+
+
 def struct(shape, dtype=jnp.float32):
     return jax.ShapeDtypeStruct(shape, dtype)
 
@@ -360,13 +363,12 @@
         ],
     )
     got = shift(up, 1)
-    own, down, below, select, stacked = kernel_call(
+    own, down, below, stacked = kernel_call(
         own_kernel,
         (
             struct((n, CELLS)),
             struct((n, CELLS)),
             struct((n, CELLS), jnp.float32),
-            struct((CELLS, 9 * HALF_CELLS), jnp.bfloat16),
             struct((9, PAIR, 3 * 3 * LANES), jnp.bfloat16),
         ),
         (slices, weights, third_weight),
@@ -390,7 +392,7 @@
     parts = kernel_call(
         down_kernel,
         struct((2 * chans * m, HALF_CELLS), jnp.bfloat16),
-        (rows, first, kept, back, gains[0], biases[0], select, down_weight),
+        (rows, first, kept, back, gains[0], biases[0], jnp.asarray(sampling()), down_weight),
         unit,
         "down",
     )

time: 88 us -> 87.7 us (level)
  no operation moved by 1% of the time
where the time goes in v8:
time: 87.7 us; the launch traced here: 87.3 us
  blocking collectives  57.5 us (66%)
  starting transfers between devices  20.9 us (24%)
  Pallas kernels  6.22 us (7%)
  waiting for transfers between devices  2.4 us (3%)
    all_to_all x4, blocking collectives, exchange(): lax.all_to_all(copies, axes, 0, 0, axis_index_groups=[order], tiled=True)  57.5 us
    ppermute x2, starting transfers between devices, shift(): return lax.ppermute(value, ('chip', 'core'), pairs)  10.8 us
    pallas_call x8, Pallas kernels, kernel_call(): pl.pallas_call(body, out_shape=outputs, in_specs=in_specs or [VMEM] * len...  6.22 us
    all_to_all x1, starting transfers between devices, exchange(): lax.all_to_all(copies, axes, 0, 0, axis_index_groups=[order], tiled=True)  6.1 us
    ppermute x1, starting transfers between devices, across(): return lax.ppermute(value, ('chip', 'core'), pairs)  4 us
    ppermute x1, waiting for transfers between devices, across(): return lax.ppermute(value, ('chip', 'core'), pairs)  1.79 us
  transfers between devices with their start and end apart: 4, of which 2 were waited for; matrix products, arithmetic and copies ran while one was open for 0% of the time, Pallas kernels for 1%

profile of v8, /device:TPU:1, one launch (start us, length us, event | category | flops | bytes accessed | tf_op | source)
XLA Modules:
  0.0 87.3 jit_solution(2362587358083296017)
XLA Ops:
  0.0 0.0 copy-start.1
  0.0 2.2 %send.1 = (bf16[2,256,512]{2,1,0:T(8,128)(2,1)S(1)}, bf16[864,256]{1,0:T(8,128)(2,1)S(1)}, f32[32,512]{1,0:T(8,128)S(1)}, bf16[2,32,512]{2,1,0:T(8,128)(2,1)S(1)}) custom-call(bf16[256,2,512]{2,1,0:T(2,128)(2,1)} %features_hbm.1, bf16[864,256]{1,0:T(8,128)(2,1)} %bitcast.41), custom_call_target="tpu_custom_call" | custom-call | flops 301989888 | bytes 2097152 | tf_op jit(solution)/shard_map/send/pallas_call | solution.py:31
  2.2 0.0 copy-start
  2.2 0.0 copy-start.2
  2.2 0.0 copy-start.7
  2.3 0.0 copy-start.8
  2.3 5.5 %collective-permute-start = (bf16[2,32,512]{2,1,0:T(8,128)(2,1)S(1)}, bf16[2,32,512]{2,1,0:T(8,128)(2,1)S(1)}, u32[]{:S(2)}, u32[]{:S(2)}) collective-permute-start(bf16[2,32,512]{2,1,0:T(8,128)(2,1)S(1)} %get-tuple-element.29), channel_id=1, source_target_pairs={{0,8},{8,16},{16,24},{24,32},{32,40},{40,48},{48,56},{56,64},{64,7... | collective-permute-start | bytes 196616 | tf_op jit(solution)/shard_map/ppermute | solution.py:297
  7.8 0.0 copy-done.1
  7.8 0.6 own.1
  8.5 5.3 %collective-permute-start.1 = (f32[32,512]{1,0:T(8,128)S(1)}, f32[32,512]{1,0:T(8,128)S(1)}, u32[]{:S(2)}, u32[]{:S(2)}) collective-permute-start(f32[32,512]{1,0:T(8,128)S(1)} %get-tuple-element.33), channel_id=1, source_target_pairs={{0,504},{8,0},{16,8},{24,16},{32,24},{40,32},{48,40},{56,48},{64,5... | collective-permute-start | bytes 196616 | tf_op jit(solution)/shard_map/ppermute | solution.py:297
  13.8 0.0 collective-permute-done.got_ref
  13.8 0.2 total.1
  14.0 17.5 %conditional.1 = (f32[64,128]{1,0:T(8,128)S(1)}) conditional(s32[]{:T(128)} %convert_element_type.3, f32[64,128]{1,0:T(8,128)S(1)} %get-tuple-element.30, f32[64,128]{1,0:T(8,128)S(1)} %get-tuple-element.30), branch_computations={%region_0.0_spmd, %region_1.0_spmd} | conditional | bytes 131080 | solution.py:386
  14.0 17.5 %all_to_all.53 = f32[64,1,128]{2,1,0:T(1,128)S(1)} all-to-all(f32[64,1,128]{2,1,0:T(1,128)S(1)} %copy.16), channel_id=1, replica_groups={{496,504,0,8,16,24,32,40,48,56,64,72,80,88,96,104,112,120,128,136,144,1..., dimensions={0} | all-to-all | bytes 65536 | tf_op jit(solution)/shard_map/cond/branch_1_fun/all_to_all | solution.py:305
  31.5 0.0 collective-permute-done.1.back_ref
  31.5 0.0 copy-done
  31.5 0.0 copy-done.2
  31.5 0.0 copy-done.7
  31.5 0.0 copy-done.8
  31.5 0.0 copy-start.3
  31.5 0.0 copy-start.4
  31.5 0.8 down.1
  32.3 13.6 %all_to_all.54 = bf16[16,40,128]{2,1,0:T(8,128)(2,1)S(1)} all-to-all(bf16[16,40,128]{2,1,0:T(8,128)(2,1)S(1)} %bitcast.28), channel_id=1, replica_groups={{5,6,7,0,1,2,3,4,13,14,15,8,9,10,11,12},{21,22,23,16,17,18,19,20,29,30,..., dimensions={0} | all-to-all | bytes 327680 | tf_op jit(solution)/shard_map/all_to_all | solution.py:305
  45.9 0.0 copy-start.5
  45.9 0.0 copy-start.6
  45.9 0.8 reduced.1
  46.7 6.1 %all-to-all-start.2 = ((f32[32,1,128]{2,1,0:T(1,128)}), f32[32,1,128]{2,1,0:T(1,128)S(1)}, u32[]{:S(2)}, u32[]{:S(2)}) async-start(f32[32,1,128]{2,1,0:T(1,128)} %bitcast.10), calls=%async_computation.2 | async-start | bytes 32768 | tf_op jit(solution)/shard_map/all_to_all | solution.py:305
  52.8 4.0 %collective-permute-start.2 = (f32[40,128]{1,0:T(8,128)S(1)}, f32[40,128]{1,0:T(8,128)S(1)}, u32[]{:S(2)}, u32[]{:S(2)}) collective-permute-start(f32[40,128]{1,0:T(8,128)S(1)} %get-tuple-element.36), channel_id=1, source_target_pairs={{0,504},{8,16},{16,8},{24,32},{32,24},{40,48},{48,40},{56,64},{64,... | collective-permute-start | bytes 61448 | tf_op jit(solution)/shard_map/ppermute | solution.py:291
  56.8 1.8 %collective-permute-done.2.got_ref = f32[40,128]{1,0:T(8,128)S(1)} collective-permute-done((f32[40,128]{1,0:T(8,128)S(1)}, f32[40,128]{1,0:T(8,128)S(1)}, u32[]{:S(2)}, u32[]{:S(2)}) %collective-permute-start.2) | collective-permute-done | bytes 20512 | tf_op jit(solution)/shard_map/ppermute | solution.py:291
  58.6 0.6 all-to-all-done.2
  59.2 0.0 copy-done.3
  59.2 0.0 copy-done.4
  59.2 0.1 bottom.1
  59.3 9.8 %all_to_all.55 = bf16[8,120,128]{2,1,0:T(8,128)(2,1)S(1)} all-to-all(bf16[8,120,128]{2,1,0:T(8,128)(2,1)S(1)} %bitcast.26), channel_id=1, replica_groups={{5,6,7,0,1,2,3,4},{13,14,15,8,9,10,11,12},{21,22,23,16,17,18,19,20},{29..., dimensions={0} | all-to-all | bytes 491520 | tf_op jit(solution)/shard_map/all_to_all | solution.py:305
  69.1 0.8 third.1
  69.9 16.7 %all_to_all.56 = f32[64,1,128]{2,1,0:T(1,128)S(1)} all-to-all(f32[64,1,128]{2,1,0:T(1,128)S(1)} %bitcast.32), channel_id=1, replica_groups={{320,328,336,344,352,360,368,376,384,392,400,408,416,424,432,440,448,45..., dimensions={0} | all-to-all | bytes 65536 | tf_op jit(solution)/shard_map/all_to_all | solution.py:305
  86.5 0.0 copy-done.5
  86.5 0.0 copy-done.6
  86.6 0.7 last.1
  (1 shorter events, 0.0 us)
Async XLA Ops:
  0.0 7.8 %copy-start.1 = (bf16[27,40,320]{2,1,0:T(8,128)(2,1)S(1)}, bf16[27,40,320]{2,1,0:T(8,128)(2,1)}, u32[]{:S(2)}) copy-start(bf16[27,40,320]{2,1,0:T(8,128)(2,1)} %third_ref.1) | copy-start | bytes 2073604
  2.2 29.3 %copy-start = (bf16[512,1152]{1,0:T(8,128)(2,1)S(1)}, bf16[512,1152]{1,0:T(8,128)(2,1)}, u32[]{:S(2)}) copy-start(bf16[512,1152]{1,0:T(8,128)(2,1)} %constant.18.clone.select_ref) | copy-start | bytes 3538948
  2.2 29.2 %copy-start.2 = (bf16[27,320,32]{1,2,0:T(8,128)(2,1)S(1)}, bf16[27,320,32]{1,2,0:T(8,128)(2,1)}, u32[]{:S(2)}) copy-start(bf16[27,320,32]{1,2,0:T(8,128)(2,1)} %param.17) | copy-start | bytes 1658884
  2.2 29.2 %copy-start.7 = (f32[32]{0:T(128)S(1)}, f32[32]{0:T(128)}, u32[]{:S(2)}) copy-start(f32[32]{0:T(128)} %param.15) | copy-start | bytes 388
  2.3 29.2 %copy-start.8 = (f32[32]{0:T(128)S(1)}, f32[32]{0:T(128)}, u32[]{:S(2)}) copy-start(f32[32]{0:T(128)} %param.16) | copy-start | bytes 388
  2.3 11.5 %collective-permute-start = (bf16[2,32,512]{2,1,0:T(8,128)(2,1)S(1)}, bf16[2,32,512]{2,1,0:T(8,128)(2,1)S(1)}, u32[]{:S(2)}, u32[]{:S(2)}) collective-permute-start(bf16[2,32,512]{2,1,0:T(8,128)(2,1)S(1)} %get-tuple-element.29), channel_id=1, source_target_pairs={{0,8},{8,16},{16,24},{24,32},{32,40},{40,48},{48,56},{56,64},{64,7... | collective-permute-start | bytes 196616 | tf_op jit(solution)/shard_map/ppermute | solution.py:297
  8.5 23.0 %collective-permute-start.1 = (f32[32,512]{1,0:T(8,128)S(1)}, f32[32,512]{1,0:T(8,128)S(1)}, u32[]{:S(2)}, u32[]{:S(2)}) collective-permute-start(f32[32,512]{1,0:T(8,128)S(1)} %get-tuple-element.33), channel_id=1, source_target_pairs={{0,504},{8,0},{16,8},{24,16},{32,24},{40,32},{48,40},{56,48},{64,5... | collective-permute-start | bytes 196616 | tf_op jit(solution)/shard_map/ppermute | solution.py:297
  31.5 27.7 %copy-start.3 = (f32[40]{0:T(128)S(1)}, f32[40]{0:T(128)}, u32[]{:S(2)}) copy-start(f32[40]{0:T(128)} %param.18) | copy-start | bytes 484
  31.5 27.7 %copy-start.4 = (f32[40]{0:T(128)S(1)}, f32[40]{0:T(128)}, u32[]{:S(2)}) copy-start(f32[40]{0:T(128)} %param.19) | copy-start | bytes 484
  45.9 40.7 %copy-start.5 = (f32[40]{0:T(128)S(1)}, f32[40]{0:T(128)}, u32[]{:S(2)}) copy-start(f32[40]{0:T(128)} %param.21) | copy-start | bytes 484
  45.9 40.7 %copy-start.6 = (f32[40]{0:T(128)S(1)}, f32[40]{0:T(128)}, u32[]{:S(2)}) copy-start(f32[40]{0:T(128)} %param.22) | copy-start | bytes 484
  46.7 12.5 %all-to-all-start.2 = ((f32[32,1,128]{2,1,0:T(1,128)}), f32[32,1,128]{2,1,0:T(1,128)S(1)}, u32[]{:S(2)}, u32[]{:S(2)}) async-start(f32[32,1,128]{2,1,0:T(1,128)} %bitcast.10), calls=%async_computation.2 | async-start | bytes 32768 | tf_op jit(solution)/shard_map/all_to_all | solution.py:305
  52.8 5.8 %collective-permute-start.2 = (f32[40,128]{1,0:T(8,128)S(1)}, f32[40,128]{1,0:T(8,128)S(1)}, u32[]{:S(2)}, u32[]{:S(2)}) collective-permute-start(f32[40,128]{1,0:T(8,128)S(1)} %get-tuple-element.36), channel_id=1, source_target_pairs={{0,504},{8,16},{16,8},{24,32},{32,24},{40,48},{48,40},{56,64},{64,... | collective-permute-start | bytes 61448 | tf_op jit(solution)/shard_map/ppermute | solution.py:291

commit v9 on v8

--- a/solution.py
+++ b/solution.py
@@ -46,10 +46,6 @@
 
 def dot(a, b):
     return jnp.dot(a, b, preferred_element_type=jnp.float32)
-
-
-def dot_nt(a, b):
-    return lax.dot_general(a, b, (((1,), (1,)), ((), ())), preferred_element_type=jnp.float32)
 
 
 def to_row(column, offset):
@@ -385,7 +381,7 @@
     )
     rows = lax.cond(
         slab() < 2 * chips,
-        lambda sent: exchange(sent, ("chip", "core"), turned(2 * chips, 2 * FIRST_CHIP)),
+        lambda sent: exchange(sent, ("chip", "core"), turned(2 * chips, 2 * FIRST_CHIP + 1)),
         lambda sent: sent,
         copies,
     )

time: 87.7 us -> 87.4 us (level)
  no operation moved by 1% of the time
where the time goes in v9:
time: 87.4 us; the launch traced here: 87 us
  blocking collectives  57.2 us (65%)
  starting transfers between devices  20.9 us (24%)
  Pallas kernels  6.22 us (7%)
  waiting for transfers between devices  2.4 us (3%)
    all_to_all x4, blocking collectives, exchange(): lax.all_to_all(copies, axes, 0, 0, axis_index_groups=[order], tiled=True)  57.2 us
    ppermute x2, starting transfers between devices, shift(): return lax.ppermute(value, ('chip', 'core'), pairs)  10.8 us
    pallas_call x8, Pallas kernels, kernel_call(): pl.pallas_call(body, out_shape=outputs, in_specs=in_specs or [VMEM] * len...  6.22 us
    all_to_all x1, starting transfers between devices, exchange(): lax.all_to_all(copies, axes, 0, 0, axis_index_groups=[order], tiled=True)  6.1 us
    ppermute x1, starting transfers between devices, across(): return lax.ppermute(value, ('chip', 'core'), pairs)  4 us
    ppermute x1, waiting for transfers between devices, across(): return lax.ppermute(value, ('chip', 'core'), pairs)  1.79 us
  transfers between devices with their start and end apart: 4, of which 2 were waited for; matrix products, arithmetic and copies ran while one was open for 0% of the time, Pallas kernels for 1%

profile of v9, /device:TPU:1, one launch (start us, length us, event | category | flops | bytes accessed | tf_op | source)
XLA Modules:
  0.0 87.0 jit_solution(3300691680913622303)
XLA Ops:
  0.0 0.0 copy-start.1
  0.0 2.2 %send.1 = (bf16[2,256,512]{2,1,0:T(8,128)(2,1)S(1)}, bf16[864,256]{1,0:T(8,128)(2,1)S(1)}, f32[32,512]{1,0:T(8,128)S(1)}, bf16[2,32,512]{2,1,0:T(8,128)(2,1)S(1)}) custom-call(bf16[256,2,512]{2,1,0:T(2,128)(2,1)} %features_hbm.1, bf16[864,256]{1,0:T(8,128)(2,1)} %bitcast.41), custom_call_target="tpu_custom_call" | custom-call | flops 301989888 | bytes 2097152 | tf_op jit(solution)/shard_map/send/pallas_call | solution.py:31
  2.2 0.0 copy-start
  2.2 0.0 copy-start.2
  2.2 0.0 copy-start.7
  2.3 0.0 copy-start.8
  2.3 5.5 %collective-permute-start = (bf16[2,32,512]{2,1,0:T(8,128)(2,1)S(1)}, bf16[2,32,512]{2,1,0:T(8,128)(2,1)S(1)}, u32[]{:S(2)}, u32[]{:S(2)}) collective-permute-start(bf16[2,32,512]{2,1,0:T(8,128)(2,1)S(1)} %get-tuple-element.29), channel_id=1, source_target_pairs={{0,8},{8,16},{16,24},{24,32},{32,40},{40,48},{48,56},{56,64},{64,7... | collective-permute-start | bytes 196616 | tf_op jit(solution)/shard_map/ppermute | solution.py:293
  7.8 0.0 copy-done.1
  7.8 0.6 own.1
  8.5 5.3 %collective-permute-start.1 = (f32[32,512]{1,0:T(8,128)S(1)}, f32[32,512]{1,0:T(8,128)S(1)}, u32[]{:S(2)}, u32[]{:S(2)}) collective-permute-start(f32[32,512]{1,0:T(8,128)S(1)} %get-tuple-element.33), channel_id=1, source_target_pairs={{0,504},{8,0},{16,8},{24,16},{32,24},{40,32},{48,40},{56,48},{64,5... | collective-permute-start | bytes 196616 | tf_op jit(solution)/shard_map/ppermute | solution.py:293
  13.8 0.0 collective-permute-done.got_ref
  13.8 0.2 total.1
  14.0 17.2 %conditional.1 = (f32[64,128]{1,0:T(8,128)S(1)}) conditional(s32[]{:T(128)} %convert_element_type.3, f32[64,128]{1,0:T(8,128)S(1)} %get-tuple-element.30, f32[64,128]{1,0:T(8,128)S(1)} %get-tuple-element.30), branch_computations={%region_0.0_spmd, %region_1.0_spmd} | conditional | bytes 131080 | solution.py:382
  14.0 17.2 %all_to_all.53 = f32[64,1,128]{2,1,0:T(1,128)S(1)} all-to-all(f32[64,1,128]{2,1,0:T(1,128)S(1)} %copy.16), channel_id=1, replica_groups={{504,0,8,16,24,32,40,48,56,64,72,80,88,96,104,112,120,128,136,144,152,1..., dimensions={0} | all-to-all | bytes 65536 | tf_op jit(solution)/shard_map/cond/branch_1_fun/all_to_all | solution.py:301
  31.2 0.0 collective-permute-done.1.back_ref
  31.2 0.0 copy-done
  31.2 0.0 copy-done.2
  31.2 0.0 copy-done.7
  31.2 0.0 copy-done.8
  31.2 0.0 copy-start.3
  31.2 0.0 copy-start.4
  31.2 0.8 down.1
  32.0 13.6 %all_to_all.54 = bf16[16,40,128]{2,1,0:T(8,128)(2,1)S(1)} all-to-all(bf16[16,40,128]{2,1,0:T(8,128)(2,1)S(1)} %bitcast.28), channel_id=1, replica_groups={{5,6,7,0,1,2,3,4,13,14,15,8,9,10,11,12},{21,22,23,16,17,18,19,20,29,30,..., dimensions={0} | all-to-all | bytes 327680 | tf_op jit(solution)/shard_map/all_to_all | solution.py:301
  45.6 0.0 copy-start.5
  45.6 0.0 copy-start.6
  45.6 0.8 reduced.1
  46.4 6.1 %all-to-all-start.2 = ((f32[32,1,128]{2,1,0:T(1,128)}), f32[32,1,128]{2,1,0:T(1,128)S(1)}, u32[]{:S(2)}, u32[]{:S(2)}) async-start(f32[32,1,128]{2,1,0:T(1,128)} %bitcast.10), calls=%async_computation.2 | async-start | bytes 32768 | tf_op jit(solution)/shard_map/all_to_all | solution.py:301
  52.5 4.0 %collective-permute-start.2 = (f32[40,128]{1,0:T(8,128)S(1)}, f32[40,128]{1,0:T(8,128)S(1)}, u32[]{:S(2)}, u32[]{:S(2)}) collective-permute-start(f32[40,128]{1,0:T(8,128)S(1)} %get-tuple-element.36), channel_id=1, source_target_pairs={{0,504},{8,16},{16,8},{24,32},{32,24},{40,48},{48,40},{56,64},{64,... | collective-permute-start | bytes 61448 | tf_op jit(solution)/shard_map/ppermute | solution.py:287
  56.5 1.8 %collective-permute-done.2.got_ref = f32[40,128]{1,0:T(8,128)S(1)} collective-permute-done((f32[40,128]{1,0:T(8,128)S(1)}, f32[40,128]{1,0:T(8,128)S(1)}, u32[]{:S(2)}, u32[]{:S(2)}) %collective-permute-start.2) | collective-permute-done | bytes 20512 | tf_op jit(solution)/shard_map/ppermute | solution.py:287
  58.3 0.6 all-to-all-done.2
  58.9 0.0 copy-done.3
  58.9 0.0 copy-done.4
  58.9 0.1 bottom.1
  59.1 9.8 %all_to_all.55 = bf16[8,120,128]{2,1,0:T(8,128)(2,1)S(1)} all-to-all(bf16[8,120,128]{2,1,0:T(8,128)(2,1)S(1)} %bitcast.26), channel_id=1, replica_groups={{5,6,7,0,1,2,3,4},{13,14,15,8,9,10,11,12},{21,22,23,16,17,18,19,20},{29..., dimensions={0} | all-to-all | bytes 491520 | tf_op jit(solution)/shard_map/all_to_all | solution.py:301
  68.9 0.8 third.1
  69.6 16.7 %all_to_all.56 = f32[64,1,128]{2,1,0:T(1,128)S(1)} all-to-all(f32[64,1,128]{2,1,0:T(1,128)S(1)} %bitcast.32), channel_id=1, replica_groups={{320,328,336,344,352,360,368,376,384,392,400,408,416,424,432,440,448,45..., dimensions={0} | all-to-all | bytes 65536 | tf_op jit(solution)/shard_map/all_to_all | solution.py:301
  86.3 0.0 copy-done.5
  86.3 0.0 copy-done.6
  86.3 0.7 last.1
  (1 shorter events, 0.0 us)
Async XLA Ops:
  0.0 7.8 %copy-start.1 = (bf16[27,40,320]{2,1,0:T(8,128)(2,1)S(1)}, bf16[27,40,320]{2,1,0:T(8,128)(2,1)}, u32[]{:S(2)}) copy-start(bf16[27,40,320]{2,1,0:T(8,128)(2,1)} %third_ref.1) | copy-start | bytes 2073604
  2.2 29.0 %copy-start = (bf16[512,1152]{1,0:T(8,128)(2,1)S(1)}, bf16[512,1152]{1,0:T(8,128)(2,1)}, u32[]{:S(2)}) copy-start(bf16[512,1152]{1,0:T(8,128)(2,1)} %constant.18.clone.select_ref) | copy-start | bytes 3538948
  2.2 29.0 %copy-start.2 = (bf16[27,320,32]{1,2,0:T(8,128)(2,1)S(1)}, bf16[27,320,32]{1,2,0:T(8,128)(2,1)}, u32[]{:S(2)}) copy-start(bf16[27,320,32]{1,2,0:T(8,128)(2,1)} %param.17) | copy-start | bytes 1658884
  2.2 28.9 %copy-start.7 = (f32[32]{0:T(128)S(1)}, f32[32]{0:T(128)}, u32[]{:S(2)}) copy-start(f32[32]{0:T(128)} %param.15) | copy-start | bytes 388
  2.3 28.9 %copy-start.8 = (f32[32]{0:T(128)S(1)}, f32[32]{0:T(128)}, u32[]{:S(2)}) copy-start(f32[32]{0:T(128)} %param.16) | copy-start | bytes 388
  2.3 11.5 %collective-permute-start = (bf16[2,32,512]{2,1,0:T(8,128)(2,1)S(1)}, bf16[2,32,512]{2,1,0:T(8,128)(2,1)S(1)}, u32[]{:S(2)}, u32[]{:S(2)}) collective-permute-start(bf16[2,32,512]{2,1,0:T(8,128)(2,1)S(1)} %get-tuple-element.29), channel_id=1, source_target_pairs={{0,8},{8,16},{16,24},{24,32},{32,40},{40,48},{48,56},{56,64},{64,7... | collective-permute-start | bytes 196616 | tf_op jit(solution)/shard_map/ppermute | solution.py:293
  8.5 22.7 %collective-permute-start.1 = (f32[32,512]{1,0:T(8,128)S(1)}, f32[32,512]{1,0:T(8,128)S(1)}, u32[]{:S(2)}, u32[]{:S(2)}) collective-permute-start(f32[32,512]{1,0:T(8,128)S(1)} %get-tuple-element.33), channel_id=1, source_target_pairs={{0,504},{8,0},{16,8},{24,16},{32,24},{40,32},{48,40},{56,48},{64,5... | collective-permute-start | bytes 196616 | tf_op jit(solution)/shard_map/ppermute | solution.py:293
  31.2 27.7 %copy-start.3 = (f32[40]{0:T(128)S(1)}, f32[40]{0:T(128)}, u32[]{:S(2)}) copy-start(f32[40]{0:T(128)} %param.18) | copy-start | bytes 484
  31.2 27.7 %copy-start.4 = (f32[40]{0:T(128)S(1)}, f32[40]{0:T(128)}, u32[]{:S(2)}) copy-start(f32[40]{0:T(128)} %param.19) | copy-start | bytes 484
  45.6 40.7 %copy-start.5 = (f32[40]{0:T(128)S(1)}, f32[40]{0:T(128)}, u32[]{:S(2)}) copy-start(f32[40]{0:T(128)} %param.21) | copy-start | bytes 484
  45.6 40.7 %copy-start.6 = (f32[40]{0:T(128)S(1)}, f32[40]{0:T(128)}, u32[]{:S(2)}) copy-start(f32[40]{0:T(128)} %param.22) | copy-start | bytes 484
  46.4 12.5 %all-to-all-start.2 = ((f32[32,1,128]{2,1,0:T(1,128)}), f32[32,1,128]{2,1,0:T(1,128)S(1)}, u32[]{:S(2)}, u32[]{:S(2)}) async-start(f32[32,1,128]{2,1,0:T(1,128)} %bitcast.10), calls=%async_computation.2 | async-start | bytes 32768 | tf_op jit(solution)/shard_map/all_to_all | solution.py:301
  52.5 5.8 %collective-permute-start.2 = (f32[40,128]{1,0:T(8,128)S(1)}, f32[40,128]{1,0:T(8,128)S(1)}, u32[]{:S(2)}, u32[]{:S(2)}) collective-permute-start(f32[40,128]{1,0:T(8,128)S(1)} %get-tuple-element.36), channel_id=1, source_target_pairs={{0,504},{8,16},{16,8},{24,32},{32,24},{40,48},{48,40},{56,64},{64,... | collective-permute-start | bytes 61448 | tf_op jit(solution)/shard_map/ppermute | solution.py:287

commit v10 on v9

--- a/solution.py
+++ b/solution.py
@@ -253,14 +253,12 @@
     share, cells = third_ref.shape
     depths = 3
     chans = bottom_ref.shape[0] // (depths * share)
-    wide = stacked_ref.shape[2] // depths
     gathered = bottom_ref[...].astype(jnp.float32)
     blocks = []
     for k in range(depths):
         for c in turned(chans, chans - SECOND_CHAN):
             at = (c * depths + k) * share
             blocks.append(gathered[at : at + share])
-        blocks.append(jnp.zeros((wide - chans * share, cells), jnp.float32))
     bottom = jnp.concatenate(blocks, axis=0).astype(jnp.bfloat16)
     taps = dot(stacked_ref[...].reshape(9 * PAIR, bottom.shape[0]), bottom)
     third = shift_add(taps, PAIR, HALF_ROWS, HALF_COLS)[:share]
@@ -365,7 +363,7 @@
             struct((n, CELLS)),
             struct((n, CELLS)),
             struct((n, CELLS), jnp.float32),
-            struct((9, PAIR, 3 * 3 * LANES), jnp.bfloat16),
+            struct((9, PAIR, 3 * wide), jnp.bfloat16),
         ),
         (slices, weights, third_weight),
         2 * unit,

time: 87.4 us -> 87.3 us (level)
  no operation moved by 1% of the time
where the time goes in v10:
time: 87.3 us; the launch traced here: 86.9 us
  blocking collectives  57.2 us (66%)
  starting transfers between devices  20.9 us (24%)
  Pallas kernels  6.15 us (7%)
  waiting for transfers between devices  2.4 us (3%)
    all_to_all x4, blocking collectives, exchange(): lax.all_to_all(copies, axes, 0, 0, axis_index_groups=[order], tiled=True)  57.2 us
    ppermute x2, starting transfers between devices, shift(): return lax.ppermute(value, ('chip', 'core'), pairs)  10.8 us
    pallas_call x8, Pallas kernels, kernel_call(): pl.pallas_call(body, out_shape=outputs, in_specs=in_specs or [VMEM] * len...  6.15 us
    all_to_all x1, starting transfers between devices, exchange(): lax.all_to_all(copies, axes, 0, 0, axis_index_groups=[order], tiled=True)  6.1 us
    ppermute x1, starting transfers between devices, across(): return lax.ppermute(value, ('chip', 'core'), pairs)  4 us
    ppermute x1, waiting for transfers between devices, across(): return lax.ppermute(value, ('chip', 'core'), pairs)  1.79 us
  transfers between devices with their start and end apart: 4, of which 2 were waited for; matrix products, arithmetic and copies ran while one was open for 0% of the time, Pallas kernels for 1%

profile of v10, /device:TPU:1, one launch (start us, length us, event | category | flops | bytes accessed | tf_op | source)
XLA Modules:
  0.0 86.9 jit_solution(12800445956293933548)
XLA Ops:
  0.0 0.0 copy-start.1
  0.0 2.2 %send.1 = (bf16[2,256,512]{2,1,0:T(8,128)(2,1)S(1)}, bf16[864,256]{1,0:T(8,128)(2,1)S(1)}, f32[32,512]{1,0:T(8,128)S(1)}, bf16[2,32,512]{2,1,0:T(8,128)(2,1)S(1)}) custom-call(bf16[256,2,512]{2,1,0:T(2,128)(2,1)} %features_hbm.1, bf16[864,256]{1,0:T(8,128)(2,1)} %bitcast.41), custom_call_target="tpu_custom_call" | custom-call | flops 301989888 | bytes 2097152 | tf_op jit(solution)/shard_map/send/pallas_call | solution.py:31
  2.2 0.0 copy-start
  2.2 0.0 copy-start.2
  2.2 0.0 copy-start.7
  2.3 0.0 copy-start.8
  2.3 5.5 %collective-permute-start = (bf16[2,32,512]{2,1,0:T(8,128)(2,1)S(1)}, bf16[2,32,512]{2,1,0:T(8,128)(2,1)S(1)}, u32[]{:S(2)}, u32[]{:S(2)}) collective-permute-start(bf16[2,32,512]{2,1,0:T(8,128)(2,1)S(1)} %get-tuple-element.29), channel_id=1, source_target_pairs={{0,8},{8,16},{16,24},{24,32},{32,40},{40,48},{48,56},{56,64},{64,7... | collective-permute-start | bytes 196616 | tf_op jit(solution)/shard_map/ppermute | solution.py:291
  7.8 0.0 copy-done.1
  7.8 0.6 own.1
  8.4 5.3 %collective-permute-start.1 = (f32[32,512]{1,0:T(8,128)S(1)}, f32[32,512]{1,0:T(8,128)S(1)}, u32[]{:S(2)}, u32[]{:S(2)}) collective-permute-start(f32[32,512]{1,0:T(8,128)S(1)} %get-tuple-element.33), channel_id=1, source_target_pairs={{0,504},{8,0},{16,8},{24,16},{32,24},{40,32},{48,40},{56,48},{64,5... | collective-permute-start | bytes 196616 | tf_op jit(solution)/shard_map/ppermute | solution.py:291
  13.8 0.0 collective-permute-done.got_ref
  13.8 0.2 total.1
  14.0 17.2 %conditional.1 = (f32[64,128]{1,0:T(8,128)S(1)}) conditional(s32[]{:T(128)} %convert_element_type.3, f32[64,128]{1,0:T(8,128)S(1)} %get-tuple-element.30, f32[64,128]{1,0:T(8,128)S(1)} %get-tuple-element.30), branch_computations={%region_0.0_spmd, %region_1.0_spmd} | conditional | bytes 131080 | solution.py:380
  14.0 17.2 %all_to_all.53 = f32[64,1,128]{2,1,0:T(1,128)S(1)} all-to-all(f32[64,1,128]{2,1,0:T(1,128)S(1)} %copy.16), channel_id=1, replica_groups={{504,0,8,16,24,32,40,48,56,64,72,80,88,96,104,112,120,128,136,144,152,1..., dimensions={0} | all-to-all | bytes 65536 | tf_op jit(solution)/shard_map/cond/branch_1_fun/all_to_all | solution.py:299
  31.2 0.0 collective-permute-done.1.back_ref
  31.2 0.0 copy-done
  31.2 0.0 copy-done.2
  31.2 0.0 copy-done.7
  31.2 0.0 copy-done.8
  31.2 0.0 copy-start.3
  31.2 0.0 copy-start.4
  31.2 0.8 down.1
  32.0 13.6 %all_to_all.54 = bf16[16,40,128]{2,1,0:T(8,128)(2,1)S(1)} all-to-all(bf16[16,40,128]{2,1,0:T(8,128)(2,1)S(1)} %bitcast.28), channel_id=1, replica_groups={{5,6,7,0,1,2,3,4,13,14,15,8,9,10,11,12},{21,22,23,16,17,18,19,20,29,30,..., dimensions={0} | all-to-all | bytes 327680 | tf_op jit(solution)/shard_map/all_to_all | solution.py:299
  45.6 0.0 copy-start.5
  45.6 0.0 copy-start.6
  45.6 0.8 reduced.1
  46.4 6.1 %all-to-all-start.2 = ((f32[32,1,128]{2,1,0:T(1,128)}), f32[32,1,128]{2,1,0:T(1,128)S(1)}, u32[]{:S(2)}, u32[]{:S(2)}) async-start(f32[32,1,128]{2,1,0:T(1,128)} %bitcast.10), calls=%async_computation.2 | async-start | bytes 32768 | tf_op jit(solution)/shard_map/all_to_all | solution.py:299
  52.5 4.0 %collective-permute-start.2 = (f32[40,128]{1,0:T(8,128)S(1)}, f32[40,128]{1,0:T(8,128)S(1)}, u32[]{:S(2)}, u32[]{:S(2)}) collective-permute-start(f32[40,128]{1,0:T(8,128)S(1)} %get-tuple-element.36), channel_id=1, source_target_pairs={{0,504},{8,16},{16,8},{24,32},{32,24},{40,48},{48,40},{56,64},{64,... | collective-permute-start | bytes 61448 | tf_op jit(solution)/shard_map/ppermute | solution.py:285
  56.5 1.8 %collective-permute-done.2.got_ref = f32[40,128]{1,0:T(8,128)S(1)} collective-permute-done((f32[40,128]{1,0:T(8,128)S(1)}, f32[40,128]{1,0:T(8,128)S(1)}, u32[]{:S(2)}, u32[]{:S(2)}) %collective-permute-start.2) | collective-permute-done | bytes 20512 | tf_op jit(solution)/shard_map/ppermute | solution.py:285
  58.3 0.6 all-to-all-done.2
  58.9 0.0 copy-done.3
  58.9 0.0 copy-done.4
  58.9 0.1 bottom.1
  59.0 9.8 %all_to_all.55 = bf16[8,120,128]{2,1,0:T(8,128)(2,1)S(1)} all-to-all(bf16[8,120,128]{2,1,0:T(8,128)(2,1)S(1)} %bitcast.26), channel_id=1, replica_groups={{5,6,7,0,1,2,3,4},{13,14,15,8,9,10,11,12},{21,22,23,16,17,18,19,20},{29..., dimensions={0} | all-to-all | bytes 491520 | tf_op jit(solution)/shard_map/all_to_all | solution.py:299
  68.8 0.7 third.1
  69.5 16.7 %all_to_all.56 = f32[64,1,128]{2,1,0:T(1,128)S(1)} all-to-all(f32[64,1,128]{2,1,0:T(1,128)S(1)} %bitcast.32), channel_id=1, replica_groups={{320,328,336,344,352,360,368,376,384,392,400,408,416,424,432,440,448,45..., dimensions={0} | all-to-all | bytes 65536 | tf_op jit(solution)/shard_map/all_to_all | solution.py:299
  86.2 0.0 copy-done.5
  86.2 0.0 copy-done.6
  86.2 0.7 last.1
  (1 shorter events, 0.0 us)
Async XLA Ops:
  0.0 7.8 %copy-start.1 = (bf16[27,40,320]{2,1,0:T(8,128)(2,1)S(1)}, bf16[27,40,320]{2,1,0:T(8,128)(2,1)}, u32[]{:S(2)}) copy-start(bf16[27,40,320]{2,1,0:T(8,128)(2,1)} %third_ref.1) | copy-start | bytes 2073604
  2.2 28.9 %copy-start = (bf16[512,1152]{1,0:T(8,128)(2,1)S(1)}, bf16[512,1152]{1,0:T(8,128)(2,1)}, u32[]{:S(2)}) copy-start(bf16[512,1152]{1,0:T(8,128)(2,1)} %constant.18.clone.select_ref) | copy-start | bytes 3538948
  2.2 28.9 %copy-start.2 = (bf16[27,320,32]{1,2,0:T(8,128)(2,1)S(1)}, bf16[27,320,32]{1,2,0:T(8,128)(2,1)}, u32[]{:S(2)}) copy-start(bf16[27,320,32]{1,2,0:T(8,128)(2,1)} %param.17) | copy-start | bytes 1658884
  2.2 28.9 %copy-start.7 = (f32[32]{0:T(128)S(1)}, f32[32]{0:T(128)}, u32[]{:S(2)}) copy-start(f32[32]{0:T(128)} %param.15) | copy-start | bytes 388
  2.3 28.9 %copy-start.8 = (f32[32]{0:T(128)S(1)}, f32[32]{0:T(128)}, u32[]{:S(2)}) copy-start(f32[32]{0:T(128)} %param.16) | copy-start | bytes 388
  2.3 11.5 %collective-permute-start = (bf16[2,32,512]{2,1,0:T(8,128)(2,1)S(1)}, bf16[2,32,512]{2,1,0:T(8,128)(2,1)S(1)}, u32[]{:S(2)}, u32[]{:S(2)}) collective-permute-start(bf16[2,32,512]{2,1,0:T(8,128)(2,1)S(1)} %get-tuple-element.29), channel_id=1, source_target_pairs={{0,8},{8,16},{16,24},{24,32},{32,40},{40,48},{48,56},{56,64},{64,7... | collective-permute-start | bytes 196616 | tf_op jit(solution)/shard_map/ppermute | solution.py:291
  8.4 22.7 %collective-permute-start.1 = (f32[32,512]{1,0:T(8,128)S(1)}, f32[32,512]{1,0:T(8,128)S(1)}, u32[]{:S(2)}, u32[]{:S(2)}) collective-permute-start(f32[32,512]{1,0:T(8,128)S(1)} %get-tuple-element.33), channel_id=1, source_target_pairs={{0,504},{8,0},{16,8},{24,16},{32,24},{40,32},{48,40},{56,48},{64,5... | collective-permute-start | bytes 196616 | tf_op jit(solution)/shard_map/ppermute | solution.py:291
  31.2 27.7 %copy-start.3 = (f32[40]{0:T(128)S(1)}, f32[40]{0:T(128)}, u32[]{:S(2)}) copy-start(f32[40]{0:T(128)} %param.18) | copy-start | bytes 484
  31.2 27.7 %copy-start.4 = (f32[40]{0:T(128)S(1)}, f32[40]{0:T(128)}, u32[]{:S(2)}) copy-start(f32[40]{0:T(128)} %param.19) | copy-start | bytes 484
  45.6 40.6 %copy-start.5 = (f32[40]{0:T(128)S(1)}, f32[40]{0:T(128)}, u32[]{:S(2)}) copy-start(f32[40]{0:T(128)} %param.21) | copy-start | bytes 484
  45.6 40.6 %copy-start.6 = (f32[40]{0:T(128)S(1)}, f32[40]{0:T(128)}, u32[]{:S(2)}) copy-start(f32[40]{0:T(128)} %param.22) | copy-start | bytes 484
  46.4 12.5 %all-to-all-start.2 = ((f32[32,1,128]{2,1,0:T(1,128)}), f32[32,1,128]{2,1,0:T(1,128)S(1)}, u32[]{:S(2)}, u32[]{:S(2)}) async-start(f32[32,1,128]{2,1,0:T(1,128)} %bitcast.10), calls=%async_computation.2 | async-start | bytes 32768 | tf_op jit(solution)/shard_map/all_to_all | solution.py:299
  52.5 5.8 %collective-permute-start.2 = (f32[40,128]{1,0:T(8,128)S(1)}, f32[40,128]{1,0:T(8,128)S(1)}, u32[]{:S(2)}, u32[]{:S(2)}) collective-permute-start(f32[40,128]{1,0:T(8,128)S(1)} %get-tuple-element.36), channel_id=1, source_target_pairs={{0,504},{8,16},{16,8},{24,32},{32,24},{40,48},{48,40},{56,64},{64,... | collective-permute-start | bytes 61448 | tf_op jit(solution)/shard_map/ppermute | solution.py:285

commit v11 on v10

--- a/solution.py
+++ b/solution.py
@@ -90,23 +90,27 @@
     slices_ref, weight_ref, kept_ref, up_ref,
     features_ref, sems,
 ):
+    chans = features_ref.shape[0]
+    half = chans // 2
+    parts = [slice(0, half), slice(half, chans)]
     loads = [
-        pltpu.make_async_copy(features_hbm, features_ref, sems.at[0]),
-        pltpu.make_async_copy(weight_hbm, weight_ref, sems.at[1]),
+        pltpu.make_async_copy(features_hbm.at[part], features_ref.at[part], sems.at[k])
+        for k, part in enumerate(parts)
     ]
+    loads.append(pltpu.make_async_copy(weight_hbm, weight_ref, sems.at[2]))
     for load in loads:
         load.start()
-    chans = features_ref.shape[0]
-    gap = iota((chans, 2 * chans), 1) - 2 * iota((chans, 2 * chans), 0)
+    gap = iota((half, chans), 1) - 2 * iota((half, chans), 0)
     picks = [(gap == j).astype(jnp.bfloat16) for j in range(2)]
-    loads[0].wait()
-    pairs = features_ref[...].reshape(2 * chans, CELLS)
-    for j in range(2):
-        slices_ref[j] = dot(picks[j], pairs).astype(jnp.bfloat16)
+    for load, part in zip(loads, parts):
+        load.wait()
+        pairs = features_ref[part].reshape(chans, CELLS)
+        for j in range(2):
+            slices_ref[j, part] = dot(picks[j], pairs).astype(jnp.bfloat16)
     block = weight_ref.shape[0] // 3
     out_chans = block // 9
     lower, upper = slices_ref[0], slices_ref[1]
-    loads[1].wait()
+    loads[2].wait()
     tap0, tap1 = (weight_ref[k * block : (k + 1) * block] for k in range(2))
     up0 = shift_add(dot(tap0, lower) + dot(tap1, upper), out_chans, ROWS, COLS)
     kept_ref[...] = up0
@@ -353,7 +357,7 @@
         in_specs=[HBM, HBM],
         scratch=[
             pltpu.VMEM(features.shape, jnp.bfloat16),
-            pltpu.SemaphoreType.DMA((2,)),
+            pltpu.SemaphoreType.DMA((3,)),
         ],
     )
     got = shift(up, 1)

time: 87.3 us -> 87.3 us (level)
  no operation moved by 1% of the time
where the time goes in v11:
time: 87.3 us; the launch traced here: 86.9 us
  blocking collectives  57.2 us (66%)
  starting transfers between devices  20.9 us (24%)
  Pallas kernels  6.12 us (7%)
  waiting for transfers between devices  2.4 us (3%)
    all_to_all x4, blocking collectives, exchange(): lax.all_to_all(copies, axes, 0, 0, axis_index_groups=[order], tiled=True)  57.2 us
    ppermute x2, starting transfers between devices, shift(): return lax.ppermute(value, ('chip', 'core'), pairs)  10.8 us
    pallas_call x8, Pallas kernels, kernel_call(): pl.pallas_call(body, out_shape=outputs, in_specs=in_specs or [VMEM] * len...  6.12 us
    all_to_all x1, starting transfers between devices, exchange(): lax.all_to_all(copies, axes, 0, 0, axis_index_groups=[order], tiled=True)  6.1 us
    ppermute x1, starting transfers between devices, across(): return lax.ppermute(value, ('chip', 'core'), pairs)  4 us
    ppermute x1, waiting for transfers between devices, across(): return lax.ppermute(value, ('chip', 'core'), pairs)  1.79 us
  transfers between devices with their start and end apart: 4, of which 2 were waited for; matrix products, arithmetic and copies ran while one was open for 0% of the time, Pallas kernels for 1%

profile of v11, /device:TPU:1, one launch (start us, length us, event | category | flops | bytes accessed | tf_op | source)
XLA Modules:
  0.0 86.9 jit_solution(5200265624959912632)
XLA Ops:
  0.0 0.0 copy-start.1
  0.0 2.2 %send.1 = (bf16[2,256,512]{2,1,0:T(8,128)(2,1)S(1)}, bf16[864,256]{1,0:T(8,128)(2,1)S(1)}, f32[32,512]{1,0:T(8,128)S(1)}, bf16[2,32,512]{2,1,0:T(8,128)(2,1)S(1)}) custom-call(bf16[256,2,512]{2,1,0:T(2,128)(2,1)} %features_hbm.1, bf16[864,256]{1,0:T(8,128)(2,1)} %bitcast.41), custom_call_target="tpu_custom_call" | custom-call | flops 301989888 | bytes 2097152 | tf_op jit(solution)/shard_map/send/pallas_call | solution.py:31
  2.2 0.0 copy-start
  2.2 0.0 copy-start.2
  2.2 0.0 copy-start.7
  2.2 0.0 copy-start.8
  2.2 5.5 %collective-permute-start = (bf16[2,32,512]{2,1,0:T(8,128)(2,1)S(1)}, bf16[2,32,512]{2,1,0:T(8,128)(2,1)S(1)}, u32[]{:S(2)}, u32[]{:S(2)}) collective-permute-start(bf16[2,32,512]{2,1,0:T(8,128)(2,1)S(1)} %get-tuple-element.29), channel_id=1, source_target_pairs={{0,8},{8,16},{16,24},{24,32},{32,40},{40,48},{48,56},{56,64},{64,7... | collective-permute-start | bytes 196616 | tf_op jit(solution)/shard_map/ppermute | solution.py:295
  7.8 0.0 copy-done.1
  7.8 0.6 own.1
  8.4 5.3 %collective-permute-start.1 = (f32[32,512]{1,0:T(8,128)S(1)}, f32[32,512]{1,0:T(8,128)S(1)}, u32[]{:S(2)}, u32[]{:S(2)}) collective-permute-start(f32[32,512]{1,0:T(8,128)S(1)} %get-tuple-element.33), channel_id=1, source_target_pairs={{0,504},{8,0},{16,8},{24,16},{32,24},{40,32},{48,40},{56,48},{64,5... | collective-permute-start | bytes 196616 | tf_op jit(solution)/shard_map/ppermute | solution.py:295
  13.7 0.0 collective-permute-done.got_ref
  13.7 0.2 total.1
  13.9 17.2 %conditional.1 = (f32[64,128]{1,0:T(8,128)S(1)}) conditional(s32[]{:T(128)} %convert_element_type.3, f32[64,128]{1,0:T(8,128)S(1)} %get-tuple-element.30, f32[64,128]{1,0:T(8,128)S(1)} %get-tuple-element.30), branch_computations={%region_0.0_spmd, %region_1.0_spmd} | conditional | bytes 131080 | solution.py:384
  14.0 17.2 %all_to_all.53 = f32[64,1,128]{2,1,0:T(1,128)S(1)} all-to-all(f32[64,1,128]{2,1,0:T(1,128)S(1)} %copy.16), channel_id=1, replica_groups={{504,0,8,16,24,32,40,48,56,64,72,80,88,96,104,112,120,128,136,144,152,1..., dimensions={0} | all-to-all | bytes 65536 | tf_op jit(solution)/shard_map/cond/branch_1_fun/all_to_all | solution.py:303
  31.1 0.0 collective-permute-done.1.back_ref
  31.1 0.0 copy-done
  31.1 0.0 copy-done.2
  31.1 0.0 copy-done.7
  31.2 0.0 copy-done.8
  31.2 0.0 copy-start.3
  31.2 0.0 copy-start.4
  31.2 0.8 down.1
  32.0 13.6 %all_to_all.54 = bf16[16,40,128]{2,1,0:T(8,128)(2,1)S(1)} all-to-all(bf16[16,40,128]{2,1,0:T(8,128)(2,1)S(1)} %bitcast.28), channel_id=1, replica_groups={{5,6,7,0,1,2,3,4,13,14,15,8,9,10,11,12},{21,22,23,16,17,18,19,20,29,30,..., dimensions={0} | all-to-all | bytes 327680 | tf_op jit(solution)/shard_map/all_to_all | solution.py:303
  45.6 0.0 copy-start.5
  45.6 0.0 copy-start.6
  45.6 0.8 reduced.1
  46.4 6.1 %all-to-all-start.2 = ((f32[32,1,128]{2,1,0:T(1,128)}), f32[32,1,128]{2,1,0:T(1,128)S(1)}, u32[]{:S(2)}, u32[]{:S(2)}) async-start(f32[32,1,128]{2,1,0:T(1,128)} %bitcast.10), calls=%async_computation.2 | async-start | bytes 32768 | tf_op jit(solution)/shard_map/all_to_all | solution.py:303
  52.5 4.0 %collective-permute-start.2 = (f32[40,128]{1,0:T(8,128)S(1)}, f32[40,128]{1,0:T(8,128)S(1)}, u32[]{:S(2)}, u32[]{:S(2)}) collective-permute-start(f32[40,128]{1,0:T(8,128)S(1)} %get-tuple-element.36), channel_id=1, source_target_pairs={{0,504},{8,16},{16,8},{24,32},{32,24},{40,48},{48,40},{56,64},{64,... | collective-permute-start | bytes 61448 | tf_op jit(solution)/shard_map/ppermute | solution.py:289
  56.5 1.8 %collective-permute-done.2.got_ref = f32[40,128]{1,0:T(8,128)S(1)} collective-permute-done((f32[40,128]{1,0:T(8,128)S(1)}, f32[40,128]{1,0:T(8,128)S(1)}, u32[]{:S(2)}, u32[]{:S(2)}) %collective-permute-start.2) | collective-permute-done | bytes 20512 | tf_op jit(solution)/shard_map/ppermute | solution.py:289
  58.3 0.6 all-to-all-done.2
  58.9 0.0 copy-done.3
  58.9 0.0 copy-done.4
  58.9 0.1 bottom.1
  59.0 9.8 %all_to_all.55 = bf16[8,120,128]{2,1,0:T(8,128)(2,1)S(1)} all-to-all(bf16[8,120,128]{2,1,0:T(8,128)(2,1)S(1)} %bitcast.26), channel_id=1, replica_groups={{5,6,7,0,1,2,3,4},{13,14,15,8,9,10,11,12},{21,22,23,16,17,18,19,20},{29..., dimensions={0} | all-to-all | bytes 491520 | tf_op jit(solution)/shard_map/all_to_all | solution.py:303
  68.8 0.7 third.1
  69.5 16.7 %all_to_all.56 = f32[64,1,128]{2,1,0:T(1,128)S(1)} all-to-all(f32[64,1,128]{2,1,0:T(1,128)S(1)} %bitcast.32), channel_id=1, replica_groups={{320,328,336,344,352,360,368,376,384,392,400,408,416,424,432,440,448,45..., dimensions={0} | all-to-all | bytes 65536 | tf_op jit(solution)/shard_map/all_to_all | solution.py:303
  86.2 0.0 copy-done.5
  86.2 0.0 copy-done.6
  86.2 0.7 last.1
  (1 shorter events, 0.0 us)
Async XLA Ops:
  0.0 7.8 %copy-start.1 = (bf16[27,40,320]{2,1,0:T(8,128)(2,1)S(1)}, bf16[27,40,320]{2,1,0:T(8,128)(2,1)}, u32[]{:S(2)}) copy-start(bf16[27,40,320]{2,1,0:T(8,128)(2,1)} %third_ref.1) | copy-start | bytes 2073604
  2.2 28.9 %copy-start = (bf16[512,1152]{1,0:T(8,128)(2,1)S(1)}, bf16[512,1152]{1,0:T(8,128)(2,1)}, u32[]{:S(2)}) copy-start(bf16[512,1152]{1,0:T(8,128)(2,1)} %constant.18.clone.select_ref) | copy-start | bytes 3538948
  2.2 28.9 %copy-start.2 = (bf16[27,320,32]{1,2,0:T(8,128)(2,1)S(1)}, bf16[27,320,32]{1,2,0:T(8,128)(2,1)}, u32[]{:S(2)}) copy-start(bf16[27,320,32]{1,2,0:T(8,128)(2,1)} %param.17) | copy-start | bytes 1658884
  2.2 28.9 %copy-start.7 = (f32[32]{0:T(128)S(1)}, f32[32]{0:T(128)}, u32[]{:S(2)}) copy-start(f32[32]{0:T(128)} %param.15) | copy-start | bytes 388
  2.2 28.9 %copy-start.8 = (f32[32]{0:T(128)S(1)}, f32[32]{0:T(128)}, u32[]{:S(2)}) copy-start(f32[32]{0:T(128)} %param.16) | copy-start | bytes 388
  2.2 11.5 %collective-permute-start = (bf16[2,32,512]{2,1,0:T(8,128)(2,1)S(1)}, bf16[2,32,512]{2,1,0:T(8,128)(2,1)S(1)}, u32[]{:S(2)}, u32[]{:S(2)}) collective-permute-start(bf16[2,32,512]{2,1,0:T(8,128)(2,1)S(1)} %get-tuple-element.29), channel_id=1, source_target_pairs={{0,8},{8,16},{16,24},{24,32},{32,40},{40,48},{48,56},{56,64},{64,7... | collective-permute-start | bytes 196616 | tf_op jit(solution)/shard_map/ppermute | solution.py:295
  8.4 22.7 %collective-permute-start.1 = (f32[32,512]{1,0:T(8,128)S(1)}, f32[32,512]{1,0:T(8,128)S(1)}, u32[]{:S(2)}, u32[]{:S(2)}) collective-permute-start(f32[32,512]{1,0:T(8,128)S(1)} %get-tuple-element.33), channel_id=1, source_target_pairs={{0,504},{8,0},{16,8},{24,16},{32,24},{40,32},{48,40},{56,48},{64,5... | collective-permute-start | bytes 196616 | tf_op jit(solution)/shard_map/ppermute | solution.py:295
  31.2 27.7 %copy-start.3 = (f32[40]{0:T(128)S(1)}, f32[40]{0:T(128)}, u32[]{:S(2)}) copy-start(f32[40]{0:T(128)} %param.18) | copy-start | bytes 484
  31.2 27.7 %copy-start.4 = (f32[40]{0:T(128)S(1)}, f32[40]{0:T(128)}, u32[]{:S(2)}) copy-start(f32[40]{0:T(128)} %param.19) | copy-start | bytes 484
  45.6 40.6 %copy-start.5 = (f32[40]{0:T(128)S(1)}, f32[40]{0:T(128)}, u32[]{:S(2)}) copy-start(f32[40]{0:T(128)} %param.21) | copy-start | bytes 484
  45.6 40.6 %copy-start.6 = (f32[40]{0:T(128)S(1)}, f32[40]{0:T(128)}, u32[]{:S(2)}) copy-start(f32[40]{0:T(128)} %param.22) | copy-start | bytes 484
  46.4 12.5 %all-to-all-start.2 = ((f32[32,1,128]{2,1,0:T(1,128)}), f32[32,1,128]{2,1,0:T(1,128)S(1)}, u32[]{:S(2)}, u32[]{:S(2)}) async-start(f32[32,1,128]{2,1,0:T(1,128)} %bitcast.10), calls=%async_computation.2 | async-start | bytes 32768 | tf_op jit(solution)/shard_map/all_to_all | solution.py:303
  52.5 5.8 %collective-permute-start.2 = (f32[40,128]{1,0:T(8,128)S(1)}, f32[40,128]{1,0:T(8,128)S(1)}, u32[]{:S(2)}, u32[]{:S(2)}) collective-permute-start(f32[40,128]{1,0:T(8,128)S(1)} %get-tuple-element.36), channel_id=1, source_target_pairs={{0,504},{8,16},{16,8},{24,32},{32,24},{40,48},{48,40},{56,64},{64,... | collective-permute-start | bytes 61448 | tf_op jit(solution)/shard_map/ppermute | solution.py:289
